TPU v7x, 32 devices: a whole 2x2x4 slice. The times are simulated.
32 devices in a mesh: span: 4 (over z), blk: 8 (over y, x, core).
Axes of the slice: x: 2, y: 2, z: 4, core: 2. Of those that a mesh axis runs over, the one named last changes fastest.
Arguments:
- populations: float32 [19, 64, 32, 128], P(None, 'blk', 'span'), may hold values from 0 to 0.5
- thermal: float32 [7, 64, 32, 128], P(None, 'blk', 'span'), may hold values from 0.1 to 0.2
- solid_mask: int32 [64, 32, 128], P('blk', 'span'), may hold values 0 or 1
- metal_temp: float32 [4, 2048], P('span', 'blk'), may hold values from 0.5 to 1.5
- conduction: float32 [1024, 2048], P('span', 'blk'), may hold values from 0 to 1
- wall_count: int32 [4, 8], P('span', 'blk'), may hold values from 256 to 512, as said below
- wall_node: int32 [4, 4096], P('span', 'blk'), may hold values from 0 to 8191
- wall_owner: int32 [4, 4096, 1], P('span', 'blk'), may hold values from 0 to 7; in each aligned block of 512 rows (0 to 511, 512 to 1023, ..., all dimensions but the last counted through in order) at most 96 rows name the same one
- wall_cell: int32 [4, 4096], P('span', 'blk'), may hold values from 0 to 255
Outputs:
- flow_out: float32 [19, 64, 32, 128], P(None, 'blk', 'span')
- heat_out: float32 [7, 64, 32, 128], P(None, 'blk', 'span')
- metal_out: float32 [4, 2048], P('span', 'blk')
Inputs may be any that keep to these rules, and one draw needn't show every extreme that they name: `wall_owner`: among the 512 wall entries of one device at most 96 name one owner; in some devices' entries one owner is named exactly 96 times. `wall_count`: some device has all 512 entries live in every draw.
All inputs are finite; a program needn't handle non-finite values. No bound on the sum of `solid_mask` on one device may be relied on, other than what follows from the above.
Results may differ from a plain program's by a relative error of at most 0.0001.
Values sent between devices are 32-bit elements; how exact they have to be, the bound alone decides.
No kernel may reach another device: no remote copies, remote signals or barrier semaphores. Data moves between devices by JAX's collectives and lax.ppermute only.
A program may use at most 64 MiB of HBM per device.

v0:
```python
import jax
import jax.numpy as jnp
from jax import lax
from jax.sharding import PartitionSpec as P

W_DEV = 512
STEPS = 2


VELOCITY_FLOW = [
    (0, 0, 0),
    (1, 0, 0),
    (-1, 0, 0),
    (0, 1, 0),
    (0, -1, 0),
    (0, 0, 1),
    (0, 0, -1),
    (1, 1, 0),
    (-1, -1, 0),
    (1, -1, 0),
    (-1, 1, 0),
    (1, 0, 1),
    (-1, 0, -1),
    (1, 0, -1),
    (-1, 0, 1),
    (0, 1, 1),
    (0, -1, -1),
    (0, 1, -1),
    (0, -1, 1),
]
WEIGHT_FLOW = [1.0 / 3.0] + [1.0 / 18.0] * 6 + [1.0 / 36.0] * 12
OPPOSITE_FLOW = [0, 2, 1, 4, 3, 6, 5, 8, 7, 10, 9, 12, 11, 14, 13, 16, 15, 18, 17]
VELOCITY_HEAT = VELOCITY_FLOW[:7]
WEIGHT_HEAT = [0.25] + [0.125] * 6
OPPOSITE_HEAT = [0, 2, 1, 4, 3, 6, 5]
ALL_VELOCITIES = VELOCITY_FLOW + VELOCITY_HEAT
RELAX_FLOW = 0.8
RELAX_HEAT = 0.9
WALL_COEFF = 0.5
METAL_GAIN = 0.5


def with_halo(block, sides, width):
    for axis, dim in sides:
        count = lax.axis_size(axis)
        forward = [(i, i + 1) for i in range(count - 1)]
        forward.append((count - 1, 0))
        backward = [(target, source) for source, target in forward]
        low = lax.ppermute(
            lax.slice_in_dim(block, block.shape[dim] - width, None, axis=dim), axis, forward
        )
        high = lax.ppermute(lax.slice_in_dim(block, 0, width, axis=dim), axis, backward)
        block = jnp.concatenate([low, block, high], axis=dim)
    return block


def exact_dot(left, right):
    return jnp.dot(left, right, precision=lax.Precision.HIGHEST, preferred_element_type=jnp.float32)


def one_hot_table(values, width):
    return (values[:, None] == jnp.arange(width, dtype=jnp.int32)[None, :]).astype(jnp.float32)


def collide(flow, heat, solid, source):
    density = jnp.sum(flow, axis=0)
    velocity_parts = []
    for axis_pick in range(3):
        positive = sum(
            [flow[component] for component in range(19) if VELOCITY_FLOW[component][axis_pick] == 1]
        )
        negative = sum(
            [
                flow[component]
                for component in range(19)
                if VELOCITY_FLOW[component][axis_pick] == -1
            ]
        )
        velocity_parts.append((positive - negative) / density)
    speed_sq = velocity_parts[0] ** 2 + velocity_parts[1] ** 2 + velocity_parts[2] ** 2
    projections = []
    for velocity in VELOCITY_FLOW:
        projections.append(
            velocity[0] * velocity_parts[0]
            + velocity[1] * velocity_parts[1]
            + velocity[2] * velocity_parts[2]
        )
    flow_eq = jnp.stack(
        [
            WEIGHT_FLOW[component]
            * density
            * (
                1.0
                + 3.0 * projections[component]
                + 4.5 * projections[component] * projections[component]
                - 1.5 * speed_sq
            )
            for component in range(19)
        ]
    )
    fluid = (solid == 0)[None]
    flow_back = jnp.stack([flow[other] for other in OPPOSITE_FLOW])
    flow_post = jnp.where(fluid, flow - (flow - flow_eq) / RELAX_FLOW, flow_back)
    temper = jnp.sum(heat, axis=0)
    heat_eq = jnp.stack(
        [
            WEIGHT_HEAT[component] * temper * (1.0 + 4.0 * projections[component])
            for component in range(7)
        ]
    )
    heat_back = jnp.stack([heat[other] for other in OPPOSITE_HEAT])
    heat_post = jnp.where(fluid, heat - (heat - heat_eq) / RELAX_HEAT, heat_back)
    heat_post = heat_post + jnp.stack([WEIGHT_HEAT[component] * source for component in range(7)])
    return (flow_post, heat_post)


def stream_halo(joined):
    width_x = joined.shape[1]
    width_z = joined.shape[2]
    padded = with_halo(joined, (("span", 2), ("blk", 1)), 1)
    moved = []
    for component, velocity in enumerate(ALL_VELOCITIES):
        start_x = 1 - velocity[0]
        start_z = 1 - velocity[2]
        piece = padded[component, start_x : start_x + width_x, start_z : start_z + width_z]
        moved.append(jnp.roll(piece, velocity[1], axis=2))
    return jnp.stack(moved)


def local(
    populations,
    thermal,
    solid_mask,
    metal_temp,
    conduction,
    wall_count,
    wall_node,
    wall_owner,
    wall_cell,
):
    blocks = lax.axis_size("blk")
    capacity = 3 * W_DEV // (2 * blocks)
    width_x, width_z, width_y = solid_mask.shape
    columns_xz = width_x * width_z
    metal = metal_temp.reshape(-1)
    tile_cells = metal.shape[0]
    live_count = wall_count.reshape(())
    node_list = wall_node.reshape(-1)
    owner_list = wall_owner.reshape(-1)
    cell_list = wall_cell.reshape(-1)
    entries = node_list.shape[0]
    live = jnp.arange(entries, dtype=jnp.int32) < live_count
    column_hot = one_hot_table(node_list // width_y, columns_xz)
    row_hot = one_hot_table(node_list % width_y, width_y)
    onehot = (owner_list[:, None] == jnp.arange(blocks, dtype=jnp.int32)[None, :]) & live[:, None]
    ranks = jnp.cumsum(onehot.astype(jnp.int32), axis=0) - 1
    slot = jnp.sum(jnp.where(onehot, ranks, 0), axis=1)
    place_key = jnp.where(live, owner_list * capacity + slot, blocks * capacity)
    placement = one_hot_table(place_key, blocks * capacity)
    cells_float = exact_dot((cell_list + 1).astype(jnp.float32), placement) - 1.0
    cells_sent = cells_float.astype(jnp.int32).reshape(blocks, capacity)
    received_cells = lax.all_to_all(cells_sent, "blk", split_axis=0, concat_axis=0, tiled=True)
    valid_slots = received_cells >= 0
    cell_hot = one_hot_table(jnp.maximum(received_cells, 0).reshape(-1), tile_cells)
    flow = populations
    heat = thermal
    for tick in range(STEPS):
        temper = jnp.sum(heat, axis=0).reshape(columns_xz, width_y)
        wall_temp = jnp.sum(exact_dot(column_hot, temper) * row_hot, axis=1)
        sent = exact_dot(wall_temp, placement).reshape(blocks, capacity)
        arrived = lax.all_to_all(sent, "blk", split_axis=0, concat_axis=0, tiled=True)
        metal_at = exact_dot(cell_hot, metal).reshape(blocks, capacity)
        slot_flux = jnp.where(valid_slots, WALL_COEFF * (arrived - metal_at), 0.0)
        gained = exact_dot(slot_flux.reshape(-1), cell_hot)
        returned = lax.all_to_all(slot_flux, "blk", split_axis=0, concat_axis=0, tiled=True)
        flux = exact_dot(placement, returned.reshape(-1))
        metal = jnp.dot(conduction, metal + METAL_GAIN * gained, precision=lax.Precision.HIGHEST)
        source = exact_dot(jnp.transpose(column_hot * (-flux)[:, None]), row_hot).reshape(
            width_x, width_z, width_y
        )
        flow_post, heat_post = collide(flow, heat, solid_mask, source)
        joined = jnp.concatenate([flow_post, heat_post], axis=0)
        moved = stream_halo(joined)
        flow = moved[:19]
        heat = moved[19:]
    return (flow, heat, metal.reshape(1, tile_cells))


def solution(mesh):
    in_specs = (
        P(None, "blk", "span", None),
        P(None, "blk", "span", None),
        P("blk", "span", None),
        P("span", "blk"),
        P("span", "blk"),
        P("span", "blk"),
        P("span", "blk"),
        P("span", "blk", None),
        P("span", "blk"),
    )
    out_specs = (P(None, "blk", "span", None), P(None, "blk", "span", None), P("span", "blk"))
    return jax.shard_map(local, mesh=mesh, in_specs=in_specs, out_specs=out_specs, check_vma=False)
```

profile of v0, /device:TPU:0, one launch (start us, length us, event | category | flops | bytes accessed | tf_op | source)
XLA Modules:
  0.0 98.2 jit_solution(4267183926275051219)
XLA Ops:
  1.4 0.7 fusion.175
  2.1 1.1 %reduce-window.6 = s32[8,4,128]{2,0,1:T(8,128)S(1)} reduce-window(s32[8,4,128]{2,0,1:T(8,128)S(1)} %fusion.175, s32[]{:T(128)} %constant.32.clone.1), window={size=1x1x128 pad=0_0x0_0x127_0}, to_apply=%region_2.3 | reduce-window | flops 520192 | bytes 32772 | tf_op jit(solution)/shard_map/reduce-window
  3.2 0.2 slice_reduce_fusion
  3.5 0.8 fusion.172
  4.3 0.7 add_select_fusion.2
  5.0 1.4 %fusion.15 = f32[768]{0:T(1024)S(1)} fusion(s32[512]{0:T(512)S(1)} %add_select_fusion.2, s32[1,512]{1,0:T(1,128)} %param.17), kind=kOutput, calls=%fused_computation.14 | convolution fusion | flops 5112832 | bytes 7168 | tf_op jit(solution)/shard_map/dot_general | solution.py:58
  6.3 0.7 all_to_all.32
  7.0 5.2 %all-to-all-start = ((s32[8,1,96]{2,1,0:T(1,128)}), s32[8,1,96]{2,1,0:T(1,128)S(1)}, u32[]{:S(2)}, u32[]{:S(2)}) async-start(s32[8,1,96]{2,1,0:T(1,128)} %all_to_all.32), calls=%async_computation | async-start | bytes 8192 | tf_op jit(solution)/shard_map/all_to_all | solution.py:162
  12.2 0.8 constant_dynamic-update-slice_fusion.51
  13.3 0.6 copy-done.20
  14.7 0.4 fusion.7
  15.1 0.1 subtract_select_fusion.1
  15.3 1.5 %fusion.9 = f32[8,1,96]{2,1,0:T(1,128)} fusion(f32[512,1,1]{0,1,2:T(1,128)S(1)} %bitcast.476, s32[8,96]{1,0:T(8,128)S(1)} %multiply_add_fusion.22, s32[512]{0:T(512)S(1)} %add_select_fusion.2), kind=kOutput, calls=%fused_computation.12 | convolution fusion | flops 5111808 | bytes 10240 | tf_op jit(solution)/shard_map/dot_general | solution.py:58
  16.8 4.2 %all-to-all-start.1 = ((f32[8,1,96]{2,1,0:T(1,128)}), f32[8,1,96]{2,1,0:T(1,128)S(1)}, u32[]{:S(2)}, u32[]{:S(2)}) async-start(f32[8,1,96]{2,1,0:T(1,128)} %fusion.9), calls=%async_computation.1 | async-start | bytes 8192 | tf_op jit(solution)/shard_map/all_to_all | solution.py:171
  21.0 0.5 fusion.26
  21.6 4.0 %all-to-all-done.1 = f32[8,1,96]{2,1,0:T(1,128)S(1)} async-done(((f32[8,1,96]{2,1,0:T(1,128)}), f32[8,1,96]{2,1,0:T(1,128)S(1)}, u32[]{:S(2)}, u32[]{:S(2)}) %all-to-all-start.1) | async-done | bytes 3104 | tf_op jit(solution)/shard_map/all_to_all | solution.py:171
  25.6 0.6 multiply_select_fusion.2
  26.2 0.8 reshape.1398
  27.0 3.3 %all-to-all-start.2 = ((f32[8,1,96]{2,1,0:T(1,128)}), f32[8,1,96]{2,1,0:T(1,128)S(1)}, u32[]{:S(2)}, u32[]{:S(2)}) async-start(f32[8,1,96]{2,1,0:T(1,128)} %bitcast.27), calls=%async_computation.2 | async-start | bytes 8192 | tf_op jit(solution)/shard_map/all_to_all | solution.py:175
  30.4 0.4 fusion.17
  30.8 4.0 %all-to-all-done.2 = f32[8,1,96]{2,1,0:T(1,128)S(1)} async-done(((f32[8,1,96]{2,1,0:T(1,128)}), f32[8,1,96]{2,1,0:T(1,128)S(1)}, u32[]{:S(2)}, u32[]{:S(2)}) %all-to-all-start.2) | async-done | bytes 3104 | tf_op jit(solution)/shard_map/all_to_all | solution.py:175
  34.8 0.6 broadcast.1065
  35.4 0.7 reduce.42
  36.2 0.9 fusion.5
  37.1 0.5 constant_dynamic-update-slice_fusion.58
  37.7 0.1 pad_maximum_fusion.11
  37.9 3.7 %collective-permute-start.1 = (f32[26,8,1,128]{3,2,1,0:T(1,128)S(1)}, f32[26,8,1,128]{3,2,1,0:T(1,128)S(1)}, u32[]{:S(2)}, u32[]{:S(2)}) collective-permute-start(f32[26,8,1,128]{3,2,1,0:T(1,128)S(1)} %get-tuple-element.85), channel_id=1, source_target_pairs={{8,0},{16,8},{24,16},{0,24},{9,1},{17,9},{25,17},{1,25},{10,2},{18... | collective-permute-start | bytes 319496 | tf_op jit(solution)/shard_map/ppermute | solution.py:52
  41.5 3.4 %collective-permute-done.1 = f32[26,8,1,128]{3,2,1,0:T(1,128)S(1)} collective-permute-done((f32[26,8,1,128]{3,2,1,0:T(1,128)S(1)}, f32[26,8,1,128]{3,2,1,0:T(1,128)S(1)}, u32[]{:S(2)}, u32[]{:S(2)}) %collective-permute-start.1) | collective-permute-done | bytes 106528 | tf_op jit(solution)/shard_map/ppermute | solution.py:52
  44.9 3.1 %collective-permute-done = f32[26,8,1,128]{3,2,1,0:T(1,128)S(1)} collective-permute-done((f32[26,8,1,128]{3,2,1,0:T(1,128)S(1)}, f32[26,8,1,128]{3,2,1,0:T(1,128)S(1)}, u32[]{:S(2)}, u32[]{:S(2)}) %collective-permute-start) | collective-permute-done | bytes 106528 | tf_op jit(solution)/shard_map/ppermute | solution.py:49
  48.2 0.3 fusion.209
  48.5 0.5 convolution_reduce_fusion
  49.2 0.7 ge.13
  49.8 0.5 collective-permute-start.2
  50.3 1.8 %collective-permute-done.3 = f32[26,1,10,128]{3,2,1,0:T(8,128)S(1)} collective-permute-done((f32[26,1,10,128]{3,2,1,0:T(8,128)S(1)}, f32[26,1,10,128]{3,2,1,0:T(8,128)S(1)}, u32[]{:S(2)}, u32[]{:S(2)}) %collective-permute-start.3) | collective-permute-done | bytes 133152 | tf_op jit(solution)/shard_map/ppermute | solution.py:52
  52.3 3.7 %collective-permute-done.2 = f32[26,1,10,128]{3,2,1,0:T(8,128)S(1)} collective-permute-done((f32[26,1,10,128]{3,2,1,0:T(8,128)S(1)}, f32[26,1,10,128]{3,2,1,0:T(8,128)S(1)}, u32[]{:S(2)}, u32[]{:S(2)}) %collective-permute-start.2) | collective-permute-done | bytes 133152 | tf_op jit(solution)/shard_map/ppermute | solution.py:49
  56.9 1.0 %constant_dynamic-update-slice_fusion.129 = (f32[7,8,8,128]{3,2,1,0:T(8,128)S(1)}, f32[1,8,8,128]{3,2,1,0:T(8,128)S(1)}, f32[1,8,8,128]{3,2,1,0:T(8,128)S(1)}, f...) fusion(f32[7,8,8,128]{3,2,1,0:T(8,128)S(1)} %select_add_fusion., ...), kind=kLoop, calls=%fused_computation.164 | loop fusion | flops 1023999 | bytes 3686400
  58.0 0.4 fusion.8
  58.5 0.1 copy-done.7
  58.6 1.5 %fusion.12 = f32[8,1,96]{2,1,0:T(1,128)} fusion(f32[512,1,1]{0,1,2:T(1,128)S(1)} %bitcast.477, s32[8,96]{1,0:T(8,128)S(1)} %copy-done.29, s32[512]{0:T(512)S(1)} %copy-done.39), kind=kOutput, calls=%fused_computation.13 | convolution fusion | flops 5111808 | bytes 10240 | tf_op jit(solution)/shard_map/dot_general | solution.py:58
  60.2 3.4 %all-to-all-start.3 = ((f32[8,1,96]{2,1,0:T(1,128)}), f32[8,1,96]{2,1,0:T(1,128)S(1)}, u32[]{:S(2)}, u32[]{:S(2)}) async-start(f32[8,1,96]{2,1,0:T(1,128)} %fusion.12), calls=%async_computation.3 | async-start | bytes 8192 | tf_op jit(solution)/shard_map/all_to_all | solution.py:171
  63.6 0.8 constant_dynamic-update-slice_fusion.121
  64.4 0.8 constant_dynamic-update-slice_fusion.120
  65.4 0.7 copy-done.6
  66.9 0.2 copy-done.13
  68.2 0.1 subtract_select_fusion
  68.3 0.5 copy-done.12
  68.9 0.6 multiply_select_fusion.1
  69.5 4.1 %all-to-all-start.4 = ((f32[8,1,96]{2,1,0:T(1,128)}), f32[8,1,96]{2,1,0:T(1,128)S(1)}, u32[]{:S(2)}, u32[]{:S(2)}) async-start(f32[8,1,96]{2,1,0:T(1,128)} %bitcast.89), calls=%async_computation.4 | async-start | bytes 8192 | tf_op jit(solution)/shard_map/all_to_all | solution.py:175
  73.6 0.7 reduce.44
  74.4 0.4 fusion.16
  74.8 3.4 %all-to-all-done.4 = f32[8,1,96]{2,1,0:T(1,128)S(1)} async-done(((f32[8,1,96]{2,1,0:T(1,128)}), f32[8,1,96]{2,1,0:T(1,128)S(1)}, u32[]{:S(2)}, u32[]{:S(2)}) %all-to-all-start.4) | async-done | bytes 3104 | tf_op jit(solution)/shard_map/all_to_all | solution.py:175
  78.2 0.7 reduce.43
  79.0 0.9 fusion.4
  79.9 0.5 constant_dynamic-update-slice_fusion.143
  80.6 0.1 pad_maximum_fusion.9
  80.7 1.2 %collective-permute-start.5 = (f32[26,8,1,128]{3,2,1,0:T(1,128)S(1)}, f32[26,8,1,128]{3,2,1,0:T(1,128)S(1)}, u32[]{:S(2)}, u32[]{:S(2)}) collective-permute-start(f32[26,8,1,128]{3,2,1,0:T(1,128)S(1)} %get-tuple-element.83), channel_id=1, source_target_pairs={{8,0},{16,8},{24,16},{0,24},{9,1},{17,9},{25,17},{1,25},{10,2},{18... | collective-permute-start | bytes 319496 | tf_op jit(solution)/shard_map/ppermute | solution.py:52
  81.9 0.9 collective-permute-start.4
  82.8 2.7 %collective-permute-done.5 = f32[26,8,1,128]{3,2,1,0:T(1,128)S(1)} collective-permute-done((f32[26,8,1,128]{3,2,1,0:T(1,128)S(1)}, f32[26,8,1,128]{3,2,1,0:T(1,128)S(1)}, u32[]{:S(2)}, u32[]{:S(2)}) %collective-permute-start.5) | collective-permute-done | bytes 106528 | tf_op jit(solution)/shard_map/ppermute | solution.py:52
  85.5 3.0 %collective-permute-done.4 = f32[26,8,1,128]{3,2,1,0:T(1,128)S(1)} collective-permute-done((f32[26,8,1,128]{3,2,1,0:T(1,128)S(1)}, f32[26,8,1,128]{3,2,1,0:T(1,128)S(1)}, u32[]{:S(2)}, u32[]{:S(2)}) %collective-permute-start.4) | collective-permute-done | bytes 106528 | tf_op jit(solution)/shard_map/ppermute | solution.py:49
  88.6 0.5 collective-permute-start.6
  89.1 0.9 fusion.210
  90.0 5.3 %collective-permute-done.6 = f32[26,1,10,128]{3,2,1,0:T(8,128)S(1)} collective-permute-done((f32[26,1,10,128]{3,2,1,0:T(8,128)S(1)}, f32[26,1,10,128]{3,2,1,0:T(8,128)S(1)}, u32[]{:S(2)}, u32[]{:S(2)}) %collective-permute-start.6) | collective-permute-done | bytes 133152 | tf_op jit(solution)/shard_map/ppermute | solution.py:49
  97.4 0.1 copy-done.23
  97.5 0.7 copy-done.41
  (287 shorter events, 6.8 us)
Async XLA Ops:
  0.6 47.6 %copy-start = (f32[256,256]{1,0:T(8,128)S(1)}, f32[256,256]{1,0:T(8,128)}, u32[]{:S(2)}) copy-start(f32[256,256]{1,0:T(8,128)} %param.13) | copy-start | bytes 786436
  0.6 12.3 %copy-start.2 = (f32[7,8,8,128]{3,2,1,0:T(8,128)S(1)}, f32[7,8,8,128]{3,2,1,0:T(8,128)}, u32[]{:S(2)}) copy-start(f32[7,8,8,128]{3,2,1,0:T(8,128)} %param.10) | copy-start | bytes 688132
  0.7 12.3 %copy-start.1 = (f32[19,8,8,128]{3,2,1,0:T(8,128)S(1)}, f32[19,8,8,128]{3,2,1,0:T(8,128)}, u32[]{:S(2)}) copy-start(f32[19,8,8,128]{3,2,1,0:T(8,128)} %param.9) | copy-start | bytes 1867780
  5.0 31.2 %copy-start.38 = (s32[512]{0:T(512)}, s32[512]{0:T(512)S(1)}, u32[]{:S(2)}) copy-start(s32[512]{0:T(512)S(1)} %add_select_fusion.2) | copy-start | bytes 6148
  6.3 6.7 %copy-start.31 = (s32[1,512]{1,0:T(1,128)S(1)}, s32[1,512]{1,0:T(1,128)}, u32[]{:S(2)}) copy-start(s32[1,512]{1,0:T(1,128)} %param.15) | copy-start | bytes 6148
  7.0 9.8 %all-to-all-start = ((s32[8,1,96]{2,1,0:T(1,128)}), s32[8,1,96]{2,1,0:T(1,128)S(1)}, u32[]{:S(2)}, u32[]{:S(2)}) async-start(s32[8,1,96]{2,1,0:T(1,128)} %all_to_all.32), calls=%async_computation | async-start | bytes 8192 | tf_op jit(solution)/shard_map/all_to_all | solution.py:162
  12.2 3.1 %copy-start.28 = (s32[8,96]{1,0:T(8,128)}, s32[8,96]{1,0:T(8,128)S(1)}, u32[]{:S(2)}) copy-start(s32[8,96]{1,0:T(8,128)S(1)} %multiply_add_fusion.22) | copy-start | bytes 9220
  13.1 24.0 %copy-start.32 = (s32[512]{0:T(512)}, s32[512]{0:T(512)S(1)}, u32[]{:S(2)}) copy-start(s32[512]{0:T(512)S(1)} %get-tuple-element.176) | copy-start | bytes 6148
  13.1 24.0 %copy-start.35 = (s32[512]{0:T(512)}, s32[512]{0:T(512)S(1)}, u32[]{:S(2)}) copy-start(s32[512]{0:T(512)S(1)} %get-tuple-element.177) | copy-start | bytes 6148
  13.2 0.8 copy-start.20
  15.1 5.9 %copy-start.42 = (f32[1,256]{1,0:T(1,128)S(1)}, f32[1,256]{1,0:T(1,128)}, u32[]{:S(2)}) copy-start(f32[1,256]{1,0:T(1,128)} %param.12) | copy-start | bytes 3076
  16.8 8.8 %all-to-all-start.1 = ((f32[8,1,96]{2,1,0:T(1,128)}), f32[8,1,96]{2,1,0:T(1,128)S(1)}, u32[]{:S(2)}, u32[]{:S(2)}) async-start(f32[8,1,96]{2,1,0:T(1,128)} %fusion.9), calls=%async_computation.1 | async-start | bytes 8192 | tf_op jit(solution)/shard_map/all_to_all | solution.py:171
  26.2 23.0 %copy-start.21 = (pred[8,1,96]{2,0,1:T(8,128)(4,1)}, pred[8,1,96]{2,0,1:T(8,128)(4,1)S(1)}, u32[]{:S(2)}) copy-start(pred[8,1,96]{2,0,1:T(8,128)(4,1)S(1)} %get-tuple-element.51) | copy-start | bytes 2308
  27.0 7.8 %all-to-all-start.2 = ((f32[8,1,96]{2,1,0:T(1,128)}), f32[8,1,96]{2,1,0:T(1,128)S(1)}, u32[]{:S(2)}, u32[]{:S(2)}) async-start(f32[8,1,96]{2,1,0:T(1,128)} %bitcast.27), calls=%async_computation.2 | async-start | bytes 8192 | tf_op jit(solution)/shard_map/all_to_all | solution.py:175
  30.4 18.1 %copy-start.26 = (s32[768]{0:T(1024)}, s32[768]{0:T(1024)S(1)}, u32[]{:S(2)}) copy-start(s32[768]{0:T(1024)S(1)} %max.16) | copy-start | bytes 9220
  37.9 7.0 %collective-permute-start.1 = (f32[26,8,1,128]{3,2,1,0:T(1,128)S(1)}, f32[26,8,1,128]{3,2,1,0:T(1,128)S(1)}, u32[]{:S(2)}, u32[]{:S(2)}) collective-permute-start(f32[26,8,1,128]{3,2,1,0:T(1,128)S(1)} %get-tuple-element.85), channel_id=1, source_target_pairs={{8,0},{16,8},{24,16},{0,24},{9,1},{17,9},{25,17},{1,25},{10,2},{18... | collective-permute-start | bytes 319496 | tf_op jit(solution)/shard_map/ppermute | solution.py:52
  41.5 6.5 %collective-permute-start = (f32[26,8,1,128]{3,2,1,0:T(1,128)S(1)}, f32[26,8,1,128]{3,2,1,0:T(1,128)S(1)}, u32[]{:S(2)}, u32[]{:S(2)}) collective-permute-start(f32[26,8,1,128]{3,2,1,0:T(1,128)S(1)} %get-tuple-element.84), channel_id=1, source_target_pairs={{0,8},{8,16},{16,24},{24,0},{1,9},{9,17},{17,25},{25,1},{2,10},{10... | collective-permute-start | bytes 319496 | tf_op jit(solution)/shard_map/ppermute | solution.py:49
  48.1 4.0 %collective-permute-start.3 = (f32[26,1,10,128]{3,2,1,0:T(8,128)S(1)}, f32[26,1,10,128]{3,2,1,0:T(8,128)S(1)}, u32[]{:S(2)}, u32[]{:S(2)}) collective-permute-start(f32[26,1,10,128]{3,2,1,0:T(8,128)S(1)} %get-tuple-element.70), channel_id=1, source_target_pairs={{1,0},{2,1},{3,2},{4,3},{5,4},{6,5},{7,6},{0,7},{9,8},{10,9},{11,1... | collective-permute-start | bytes 399368 | tf_op jit(solution)/shard_map/ppermute | solution.py:52
  48.5 3.7 %copy-start.24 = (f32[1,256]{1,0:T(1,128)}, f32[1,256]{1,0:T(1,128)S(1)}, u32[]{:S(2)}) copy-start(f32[1,256]{1,0:T(1,128)S(1)} %fusion.209) | copy-start | bytes 3076
  49.8 6.2 %collective-permute-start.2 = (f32[26,1,10,128]{3,2,1,0:T(8,128)S(1)}, f32[26,1,10,128]{3,2,1,0:T(8,128)S(1)}, u32[]{:S(2)}, u32[]{:S(2)}) collective-permute-start(f32[26,1,10,128]{3,2,1,0:T(8,128)S(1)} %get-tuple-element.71), channel_id=1, source_target_pairs={{0,1},{1,2},{2,3},{3,4},{4,5},{5,6},{6,7},{7,0},{8,9},{9,10},{10,1... | collective-permute-start | bytes 399368 | tf_op jit(solution)/shard_map/ppermute | solution.py:49
  56.5 1.5 %copy-start.3 = (f32[8,8,127]{2,1,0:T(8,128)}, f32[8,8,127]{2,1,0:T(8,128)S(1)}, u32[]{:S(2)}) copy-start(f32[8,8,127]{2,1,0:T(8,128)S(1)} %get-tuple-element.138) | copy-start | bytes 97540
  56.9 1.1 %copy-start.33 = (s32[512]{0:T(512)S(1)}, s32[512]{0:T(512)}, u32[]{:S(2)}) copy-start(s32[512]{0:T(512)} %copy-done.32) | copy-start | bytes 6148
  56.9 1.1 %copy-start.36 = (s32[512]{0:T(512)S(1)}, s32[512]{0:T(512)}, u32[]{:S(2)}) copy-start(s32[512]{0:T(512)} %copy-done.35) | copy-start | bytes 6148
  56.9 1.7 %copy-start.29 = (s32[8,96]{1,0:T(8,128)S(1)}, s32[8,96]{1,0:T(8,128)}, u32[]{:S(2)}) copy-start(s32[8,96]{1,0:T(8,128)} %copy-done.28) | copy-start | bytes 9220
  56.9 1.7 %copy-start.39 = (s32[512]{0:T(512)S(1)}, s32[512]{0:T(512)}, u32[]{:S(2)}) copy-start(s32[512]{0:T(512)} %copy-done.38) | copy-start | bytes 6148
  58.0 0.6 copy-start.7
  58.0 0.6 copy-start.9
  58.0 0.6 copy-start.11
  58.0 0.6 copy-start.17
  58.0 0.6 copy-start.19
  58.6 6.5 %copy-start.8 = (f32[8,8,128]{2,1,0:T(8,128)S(1)}, f32[8,8,128]{2,1,0:T(8,128)}, u32[]{:S(2)}) copy-start(f32[8,8,128]{2,1,0:T(8,128)} %copy-done.7) | copy-start | bytes 98308
  60.1 5.0 %copy-start.10 = (f32[1,8,8,128]{3,2,1,0:T(8,128)S(1)}, f32[1,8,8,128]{3,2,1,0:T(8,128)}, u32[]{:S(2)}) copy-start(f32[1,8,8,128]{3,2,1,0:T(8,128)} %copy-done.9) | copy-start | bytes 98308
  60.2 5.0 %copy-start.18 = (f32[8,8,128]{2,1,0:T(8,128)S(1)}, f32[8,8,128]{2,1,0:T(8,128)}, u32[]{:S(2)}) copy-start(f32[8,8,128]{2,1,0:T(8,128)} %copy-done.17) | copy-start | bytes 98308
  60.2 8.7 %all-to-all-start.3 = ((f32[8,1,96]{2,1,0:T(1,128)}), f32[8,1,96]{2,1,0:T(1,128)S(1)}, u32[]{:S(2)}, u32[]{:S(2)}) async-start(f32[8,1,96]{2,1,0:T(1,128)} %fusion.12), calls=%async_computation.3 | async-start | bytes 8192 | tf_op jit(solution)/shard_map/all_to_all | solution.py:171
  65.3 0.8 copy-start.6
  65.3 0.8 copy-start.16
  65.3 0.9 copy-start.4
  65.3 1.0 %copy-start.5 = (f32[1,8,8,128]{3,2,1,0:T(8,128)S(1)}, f32[1,8,8,128]{3,2,1,0:T(8,128)}, u32[]{:S(2)}) copy-start(f32[1,8,8,128]{3,2,1,0:T(8,128)} %get-tuple-element.31) | copy-start | bytes 98308
  65.4 1.0 copy-start.15
  66.1 0.8 copy-start.14
  66.3 0.8 copy-start.13
  68.1 0.8 copy-start.12
  68.1 0.8 copy-start.22
  68.1 6.3 %copy-start.30 = (pred[768]{0:T(1024)(128)(4,1)S(1)}, pred[768]{0:T(1024)(128)(4,1)}, u32[]{:S(2)}) copy-start(pred[768]{0:T(1024)(128)(4,1)} %ge.13) | copy-start | bytes 2308
  68.1 6.3 %copy-start.27 = (s32[768]{0:T(1024)S(1)}, s32[768]{0:T(1024)}, u32[]{:S(2)}) copy-start(s32[768]{0:T(1024)} %copy-done.26) | copy-start | bytes 9220
  68.2 10.8 %copy-start.40 = (s32[512]{0:T(512)S(1)}, s32[512]{0:T(512)}, u32[]{:S(2)}) copy-start(s32[512]{0:T(512)} %copy-done.38) | copy-start | bytes 6148
  68.3 11.5 %copy-start.34 = (s32[512]{0:T(512)S(1)}, s32[512]{0:T(512)}, u32[]{:S(2)}) copy-start(s32[512]{0:T(512)} %copy-done.32) | copy-start | bytes 6148
  68.3 11.5 %copy-start.37 = (s32[512]{0:T(512)S(1)}, s32[512]{0:T(512)}, u32[]{:S(2)}) copy-start(s32[512]{0:T(512)} %copy-done.35) | copy-start | bytes 6148
  69.5 8.7 %all-to-all-start.4 = ((f32[8,1,96]{2,1,0:T(1,128)}), f32[8,1,96]{2,1,0:T(1,128)S(1)}, u32[]{:S(2)}, u32[]{:S(2)}) async-start(f32[8,1,96]{2,1,0:T(1,128)} %bitcast.89), calls=%async_computation.4 | async-start | bytes 8192 | tf_op jit(solution)/shard_map/all_to_all | solution.py:175
  80.6 2.2 %copy-start.25 = (f32[1,256]{1,0:T(1,128)S(1)}, f32[1,256]{1,0:T(1,128)}, u32[]{:S(2)}) copy-start(f32[1,256]{1,0:T(1,128)} %copy-done.24) | copy-start | bytes 3076
  80.7 4.8 %collective-permute-start.5 = (f32[26,8,1,128]{3,2,1,0:T(1,128)S(1)}, f32[26,8,1,128]{3,2,1,0:T(1,128)S(1)}, u32[]{:S(2)}, u32[]{:S(2)}) collective-permute-start(f32[26,8,1,128]{3,2,1,0:T(1,128)S(1)} %get-tuple-element.83), channel_id=1, source_target_pairs={{8,0},{16,8},{24,16},{0,24},{9,1},{17,9},{25,17},{1,25},{10,2},{18... | collective-permute-start | bytes 319496 | tf_op jit(solution)/shard_map/ppermute | solution.py:52
  81.9 6.5 %collective-permute-start.4 = (f32[26,8,1,128]{3,2,1,0:T(1,128)S(1)}, f32[26,8,1,128]{3,2,1,0:T(1,128)S(1)}, u32[]{:S(2)}, u32[]{:S(2)}) collective-permute-start(f32[26,8,1,128]{3,2,1,0:T(1,128)S(1)} %get-tuple-element.82), channel_id=1, source_target_pairs={{0,8},{8,16},{16,24},{24,0},{1,9},{9,17},{17,25},{25,1},{2,10},{10... | collective-permute-start | bytes 319496 | tf_op jit(solution)/shard_map/ppermute | solution.py:49
  88.5 6.7 %collective-permute-start.7 = (f32[26,1,10,128]{3,2,1,0:T(8,128)S(1)}, f32[26,1,10,128]{3,2,1,0:T(8,128)S(1)}, u32[]{:S(2)}, u32[]{:S(2)}) collective-permute-start(f32[26,1,10,128]{3,2,1,0:T(8,128)S(1)} %get-tuple-element.68), channel_id=1, source_target_pairs={{1,0},{2,1},{3,2},{4,3},{5,4},{6,5},{7,6},{0,7},{9,8},{10,9},{11,1... | collective-permute-start | bytes 399368 | tf_op jit(solution)/shard_map/ppermute | solution.py:52
  88.6 6.7 %collective-permute-start.6 = (f32[26,1,10,128]{3,2,1,0:T(8,128)S(1)}, f32[26,1,10,128]{3,2,1,0:T(8,128)S(1)}, u32[]{:S(2)}, u32[]{:S(2)}) collective-permute-start(f32[26,1,10,128]{3,2,1,0:T(8,128)S(1)} %get-tuple-element.69), channel_id=1, source_target_pairs={{0,1},{1,2},{2,3},{3,4},{4,5},{5,6},{6,7},{7,0},{8,9},{9,10},{10,1... | collective-permute-start | bytes 399368 | tf_op jit(solution)/shard_map/ppermute | solution.py:49
  96.8 0.7 copy-start.23
  97.4 0.8 copy-start.41
where the time goes:
time: 99.3 us; the launch traced here: 98.2 us
  waiting for transfers between devices  34.3 us (35%)
  starting transfers between devices  27 us (27%)
  other arithmetic  12 us (12%)
  local copies, waits for them, and re-layouts  11 us (11%)
  matrix products  11 us (11%)
  between operations  2.87 us (3%)
    ppermute x4, waiting for transfers between devices, with_halo(): lax.ppermute(lax.slice_in_dim(block, block.shape[dim] - width, None, axis...  15 us
    dot_general x13, matrix products, exact_dot(): jnp.dot(left, right, precision=lax.Precision.HIGHEST, preferred_element_t...  9.87 us
    ppermute x4, waiting for transfers between devices, with_halo(): lax.ppermute(lax.slice_in_dim(block, 0, width, axis=dim), axis, backward)  7.85 us
    all_to_all x2, starting transfers between devices, local(): lax.all_to_all(sent, 'blk', split_axis=0, concat_axis=0, tiled=True)  7.6 us
    all_to_all x2, starting transfers between devices, local(): lax.all_to_all(slot_flux, 'blk', split_axis=0, concat_axis=0, tiled=True)  7.44 us
    all_to_all x2, waiting for transfers between devices, local(): lax.all_to_all(slot_flux, 'blk', split_axis=0, concat_axis=0, tiled=True)  7.41 us
    unnamed x132, local copies, waits for them, and re-layouts  5.8 us
    all_to_all x1, starting transfers between devices, local(): lax.all_to_all(cells_sent, 'blk', split_axis=0, concat_axis=0, tiled=True)  5.17 us
  transfers between devices with their start and end apart: 13, of which 10 were waited for; matrix products, arithmetic and copies ran while one was open for 12% of the time, Pallas kernels for 0%

commit v1 on v0

v1 whole, which is shorter than its diff:
```python
import functools

import jax
import jax.numpy as jnp
from jax import lax
from jax.experimental import pallas as pl
from jax.experimental.pallas import tpu as pltpu
from jax.sharding import PartitionSpec as P

VELOCITY_FLOW = [
    (0, 0, 0),
    (1, 0, 0),
    (-1, 0, 0),
    (0, 1, 0),
    (0, -1, 0),
    (0, 0, 1),
    (0, 0, -1),
    (1, 1, 0),
    (-1, -1, 0),
    (1, -1, 0),
    (-1, 1, 0),
    (1, 0, 1),
    (-1, 0, -1),
    (1, 0, -1),
    (-1, 0, 1),
    (0, 1, 1),
    (0, -1, -1),
    (0, 1, -1),
    (0, -1, 1),
]
WEIGHT_FLOW = [1.0 / 3.0] + [1.0 / 18.0] * 6 + [1.0 / 36.0] * 12
OPPOSITE = [0, 2, 1, 4, 3, 6, 5, 8, 7, 10, 9, 12, 11, 14, 13, 16, 15, 18, 17]
WEIGHT_HEAT = [0.25] + [0.125] * 6
VELOCITY = VELOCITY_FLOW + VELOCITY_FLOW[:7]
FLOWS, HEATS = 19, 7
ALL = FLOWS + HEATS
RELAX_FLOW = 0.8
RELAX_HEAT = 0.9
WALL_COEFF = 0.5
METAL_GAIN = 0.5

FACE_RIGHT = [(i, 0) for i in range(ALL) if VELOCITY[i][0] >= 0] + [
    (i, 1) for i in range(ALL) if VELOCITY[i][0] == 1
]
FACE_LEFT = [(i, 0) for i in range(ALL) if VELOCITY[i][0] <= 0] + [
    (i, 1) for i in range(ALL) if VELOCITY[i][0] == -1
]
FACES = len(FACE_RIGHT)
UP = [i for i in range(ALL) if VELOCITY[i][2] == 1]
DOWN = [i for i in range(ALL) if VELOCITY[i][2] == -1]
EDGES = len(UP)

ROW_TEMPER, ROW_OWNER, ROW_CELL, ROW_NODE, ROW_SUMS = 2, 6, 10, 14, 24
LANES = 128
F32 = jnp.float32
BF16 = jnp.bfloat16


def params(mebibytes=32):
    return pltpu.CompilerParams(vmem_limit_bytes=mebibytes * 1024 * 1024)


def in_vmem(count):
    return [pl.BlockSpec(memory_space=pltpu.VMEM)] * count


def shape(*dims):
    return jax.ShapeDtypeStruct(dims, F32)


def split(value):
    high = value.astype(BF16)
    rest = value - high.astype(F32)
    middle = rest.astype(BF16)
    low = (rest - middle.astype(F32)).astype(BF16)
    return high, middle, low


def dot(left, right, dims):
    return lax.dot_general(left, right, (dims, ((), ())), preferred_element_type=F32)


def rows_of(row, count):
    return lax.broadcasted_iota(jnp.int32, (count, row.shape[1]), 0) == row


def hot(mask):
    return jnp.where(mask, 1.0, 0.0).astype(BF16)


def look_up(table, row_hot, lane_mask):
    turned = jnp.transpose(table)
    found = sum([dot(part, row_hot, ((1,), (0,))) for part in split(turned)])
    return jnp.sum(jnp.where(lane_mask, found, 0.0), axis=0, keepdims=True)


def add_up(values, row_mask, lane_hot):
    count = row_mask.shape[0]
    stacked = jnp.concatenate(
        [jnp.where(row_mask, part.astype(F32), 0.0) for part in split(values)], axis=0
    ).astype(BF16)
    sums = dot(stacked, lane_hot, ((1,), (1,)))
    return sums[:count] + sums[count : 2 * count] + sums[2 * count :]


def one_row(block):
    return jnp.concatenate([block[r : r + 1] for r in range(block.shape[0])], axis=1)


def put_rows(ref, start, row):
    for r in range(row.shape[1] // LANES):
        ref[start + r : start + r + 1, :] = row[:, r * LANES : (r + 1) * LANES]


def lists_of(packet):
    owner = one_row(packet[ROW_OWNER : ROW_OWNER + 4]).astype(jnp.int32)
    cell = one_row(packet[ROW_CELL : ROW_CELL + 4]).astype(jnp.int32)
    node = one_row(packet[ROW_NODE : ROW_NODE + 4]).astype(jnp.int32)
    return owner, cell, node


def packet_kernel(count_ref, heat_ref, metal_ref, node_ref, owner_ref, cell_ref, out_ref, *, blocks):
    wide, deep, lanes = heat_ref.shape[1:]
    temper = heat_ref[0]
    for k in range(1, HEATS):
        temper = temper + heat_ref[k]
    temper = temper.reshape(wide * deep, lanes)
    node = node_ref[...]
    cell = cell_ref[...]
    entries = node.shape[1]
    live = lax.broadcasted_iota(jnp.int32, (1, entries), 1) < count_ref[0, 0]
    owner = jnp.where(live, owner_ref[...], -1)
    wall = look_up(temper, hot(rows_of(node >> 7, wide * deep)), rows_of(node & 127, lanes))
    cell_hot = hot(rows_of(cell & 127, lanes))
    row_mask = rows_of(owner * 2 + (cell >> 7), 2 * blocks)
    out_ref[0:ROW_SUMS, :] = jnp.zeros((ROW_SUMS, lanes), F32)
    put_rows(out_ref, 0, metal_ref[...])
    put_rows(out_ref, ROW_TEMPER, wall)
    put_rows(out_ref, ROW_OWNER, owner.astype(F32))
    put_rows(out_ref, ROW_CELL, cell.astype(F32))
    put_rows(out_ref, ROW_NODE, node.astype(F32))
    out_ref[ROW_SUMS : ROW_SUMS + 2 * blocks, :] = add_up(wall, row_mask, cell_hot)
    out_ref[ROW_SUMS + 2 * blocks : ROW_SUMS + 4 * blocks, :] = dot(
        hot(row_mask), cell_hot, ((1,), (1,))
    )


def collide_flow(flow, solid):
    density = flow[0]
    for i in range(1, FLOWS):
        density = density + flow[i]
    inverse = 1.0 / density
    speed = []
    for axis in range(3):
        ahead = [flow[i] for i in range(FLOWS) if VELOCITY[i][axis] == 1]
        behind = [flow[i] for i in range(FLOWS) if VELOCITY[i][axis] == -1]
        speed.append((sum(ahead[1:], ahead[0]) - sum(behind[1:], behind[0])) * inverse)
    base = 1.0 - 1.5 * (speed[0] * speed[0] + speed[1] * speed[1] + speed[2] * speed[2])
    scaled = {w: density * (w / RELAX_FLOW) for w in set(WEIGHT_FLOW)}
    keep = 1.0 - 1.0 / RELAX_FLOW
    post = [None] * FLOWS
    rest = scaled[WEIGHT_FLOW[0]] * base + keep * flow[0]
    post[0] = jnp.where(solid, flow[0], rest)
    for i in range(1, FLOWS, 2):
        along = None
        for axis in range(3):
            c = VELOCITY[i][axis]
            if c == 0:
                continue
            term = speed[axis]
            if along is None:
                along = term if c == 1 else -term
            else:
                along = along + term if c == 1 else along - term
        weight = scaled[WEIGHT_FLOW[i]]
        even = weight * (base + 4.5 * along * along)
        odd = weight * (3.0 * along)
        j = OPPOSITE[i]
        post[i] = jnp.where(solid, flow[j], even + odd + keep * flow[i])
        post[j] = jnp.where(solid, flow[i], even - odd + keep * flow[j])
    return post, speed


def collide_heat(heat, temper, speed, solid):
    keep = 1.0 - 1.0 / RELAX_HEAT
    post = [None] * HEATS
    post[0] = jnp.where(
        solid, heat[0], temper * (WEIGHT_HEAT[0] / RELAX_HEAT) + keep * heat[0]
    )
    scaled = temper * (WEIGHT_HEAT[1] / RELAX_HEAT)
    for axis in range(3):
        i = 2 * axis + 1
        j = i + 1
        odd = scaled * (4.0 * speed[axis])
        post[i] = jnp.where(solid, heat[j], scaled + odd + keep * heat[i])
        post[j] = jnp.where(solid, heat[i], scaled - odd + keep * heat[j])
    return post


def collide_kernel(
    place_ref, flow_ref, heat_ref, solid_ref, postf_ref, posth_ref, senda_ref, sendb_ref
):
    wide = flow_ref.shape[1]
    odd = place_ref[0] % 2 == 1
    for x in range(wide):
        flow = [flow_ref[i, x] for i in range(FLOWS)]
        heat = [heat_ref[k, x] for k in range(HEATS)]
        solid = solid_ref[x] != 0
        temper = heat[0]
        for k in range(1, HEATS):
            temper = temper + heat[k]
        post, speed = collide_flow(flow, solid)
        post = post + collide_heat(heat, temper, speed, solid)
        for i in range(FLOWS):
            postf_ref[i, x] = post[i]
        for k in range(HEATS):
            posth_ref[k, x] = post[FLOWS + k]

    def plane(i, x):
        return postf_ref[i, x] if i < FLOWS else posth_ref[i - FLOWS, x]

    def fill(right_ref, left_ref):
        for n, (i, depth) in enumerate(FACE_RIGHT):
            right_ref[n] = plane(i, wide - 1 - depth)
        right_ref[FACES] = solid_ref[wide - 1].astype(F32)
        for n, (i, depth) in enumerate(FACE_LEFT):
            left_ref[n] = plane(i, depth)
        left_ref[FACES] = solid_ref[0].astype(F32)

    @pl.when(odd)
    def _():
        fill(sendb_ref, senda_ref)

    @pl.when(jnp.logical_not(odd))
    def _():
        fill(senda_ref, sendb_ref)


def sides(odd, a_ref, b_ref):
    def low(n):
        return jnp.where(odd, a_ref[n], b_ref[n])

    def high(n):
        return jnp.where(odd, b_ref[n], a_ref[n])

    return low, high


def planes(postf_ref, posth_ref, low, high, wide, source_ref):
    def get(i, x):
        if x < 0:
            value = low(FACE_RIGHT.index((i, -1 - x)))
        elif x >= wide:
            value = high(FACE_LEFT.index((i, x - wide)))
        elif i < FLOWS:
            value = postf_ref[i, x]
        else:
            value = posth_ref[i - FLOWS, x]
        if i >= FLOWS and source_ref is not None:
            value = value + WEIGHT_HEAT[i - FLOWS] * source_ref[x + 2]
        return value

    return get


def wall_flux(table, lists, wall, blocks):
    owner, cell, node = lists
    row = jnp.where(owner < 0, -1, owner * 8 + (cell >> 7))
    row_mask = rows_of(row, blocks * 8)
    at = look_up(table, hot(row_mask), rows_of(cell & 127, LANES))
    return jnp.where(owner < 0, 0.0, WALL_COEFF * (wall - at))


def tile_sums(value, block):
    rows = lax.broadcasted_iota(jnp.int32, value.shape, 0)
    return [
        jnp.sum(jnp.where(rows == 2 * block + h, value, 0.0), axis=0, keepdims=True)
        for h in range(2)
    ]


def conduct(conduction, halves):
    vector = jnp.concatenate(halves, axis=1)
    parts = split(vector)
    rows = lax.broadcasted_iota(jnp.int32, (16, vector.shape[1]), 0)
    stacked = jnp.zeros((16, vector.shape[1]), F32)
    for r, part in enumerate(parts):
        stacked = jnp.where(rows == r, part.astype(F32), stacked)
    stacked = stacked.astype(BF16)
    out = sum([dot(stacked, part, ((1,), (1,))) for part in split(conduction)])
    return out[0:1] + out[1:2] + out[2:3]


def source_kernel(
    place_ref,
    postf_ref,
    posth_ref,
    recva_ref,
    recvb_ref,
    gathered_ref,
    conduction_ref,
    senda_ref,
    sendb_ref,
    metal_ref,
    source_ref,
    *,
    blocks,
):
    wide, deep, lanes = postf_ref.shape[1:]
    block = place_ref[0]
    left = lax.rem(block + blocks - 1, blocks)
    right = lax.rem(block + 1, blocks)
    table = jnp.concatenate([gathered_ref[d, 0:8] for d in range(blocks)], axis=0)
    packets = [gathered_ref[d, 0:ROW_SUMS] for d in (left, block, right)]
    lists = [lists_of(packet) for packet in packets]
    joined = [jnp.concatenate([item[n] for item in lists], axis=1) for n in range(3)]
    wall = jnp.concatenate(
        [one_row(packet[ROW_TEMPER : ROW_TEMPER + 4]) for packet in packets], axis=1
    )
    flux = -wall_flux(table, joined, wall, blocks)
    entries = lists[0][0].shape[1]
    columns = wide * deep
    for n, (first, count, start) in enumerate(
        ((columns - 2 * deep, 2 * deep, 0), (0, columns, 2), (0, 2 * deep, wide + 2))
    ):
        node = lists[n][2]
        source = add_up(
            flux[:, n * entries : (n + 1) * entries],
            rows_of((node >> 7) - first, count),
            hot(rows_of(node & 127, lanes)),
        )
        source_ref[start : start + count // deep] = source.reshape(count // deep, deep, lanes)

    low, high = sides(block % 2 == 1, recva_ref, recvb_ref)
    get = planes(postf_ref, posth_ref, low, high, wide, source_ref)

    def fill(up_ref, down_ref):
        for ref, comps, row in ((up_ref, UP, deep - 1), (down_ref, DOWN, 0)):
            for j in range(wide + 2):
                for n, i in enumerate(comps):
                    value = get(i, j - 1 - VELOCITY[i][0])
                    at = j * EDGES + n
                    ref[at : at + 1, :] = value[row : row + 1, :]

    for ref in (senda_ref, sendb_ref):
        ref[ref.shape[0] - 8 :, :] = jnp.zeros((8, lanes), F32)

    @pl.when(place_ref[1] % 2 == 1)
    def _():
        fill(sendb_ref, senda_ref)

    @pl.when(place_ref[1] % 2 == 0)
    def _():
        fill(senda_ref, sendb_ref)

    sums = gathered_ref[0, ROW_SUMS : ROW_SUMS + 4 * blocks]
    for d in range(1, blocks):
        sums = sums + gathered_ref[d, ROW_SUMS : ROW_SUMS + 4 * blocks]
    total = tile_sums(sums[: 2 * blocks], block)
    count = tile_sums(sums[2 * blocks :], block)
    own = gathered_ref[block, 0:8]
    halves = []
    for h in range(2):
        metal = own[h : h + 1]
        halves.append(metal + METAL_GAIN * WALL_COEFF * (total[h] - count[h] * metal))
    metal_ref[...] = jnp.zeros(metal_ref.shape, F32)
    put_rows(metal_ref, 0, conduct(conduction_ref[...], halves))


def stream(get, edge, deep, i, x):
    cx, cy, cz = VELOCITY[i]
    value = get(i, x - cx)
    if cz != 0:
        rows = lax.broadcasted_iota(jnp.int32, value.shape, 0)
        if cz == 1:
            value = jnp.where(rows == 0, edge(i, x), pltpu.roll(value, 1, 0))
        else:
            value = jnp.where(rows == deep - 1, edge(i, x), pltpu.roll(value, deep - 1, 0))
    if cy != 0:
        value = pltpu.roll(value, cy % value.shape[1], 1)
    return value


def edge_rows(odd, a_ref, b_ref, first):
    def edge(i, x):
        comps = UP if VELOCITY[i][2] == 1 else DOWN
        at = (x - first) * EDGES + comps.index(i)
        a = a_ref[at : at + 1, :]
        b = b_ref[at : at + 1, :]
        if VELOCITY[i][2] == 1:
            return jnp.where(odd, a, b)
        return jnp.where(odd, b, a)

    return edge


def heat_kernel(
    place_ref,
    posth_ref,
    recva_ref,
    recvb_ref,
    source_ref,
    edgea_ref,
    edgeb_ref,
    gathered_ref,
    heat_ref,
    temper_ref,
    wall_ref,
    sums_ref,
    *,
    blocks,
):
    wide, deep, lanes = posth_ref.shape[1:]
    block = place_ref[0]
    left = lax.rem(block + blocks - 1, blocks)
    right = lax.rem(block + 1, blocks)
    low, high = sides(block % 2 == 1, recva_ref, recvb_ref)
    get = planes(None, posth_ref, low, high, wide, source_ref)
    edge = edge_rows(place_ref[1] % 2 == 1, edgea_ref, edgeb_ref, -1)
    for x in range(-1, wide + 1):
        temper = None
        for k in range(HEATS):
            value = stream(get, edge, deep, FLOWS + k, x)
            heat_ref[k, x + 1] = value
            temper = value if temper is None else temper + value
        temper_ref[x + 1] = temper
    columns = wide * deep
    walls = []
    own = None
    for n, (device, first, count, start) in enumerate(
        ((left, columns - deep, deep, 0), (block, 0, columns, 1), (right, 0, deep, wide + 1))
    ):
        owner, cell, node = lists_of(gathered_ref[device, 0:ROW_SUMS])
        table = temper_ref[start : start + count // deep].reshape(count, lanes)
        wall = look_up(
            table, hot(rows_of((node >> 7) - first, count)), rows_of(node & 127, lanes)
        )
        put_rows(wall_ref, 4 * n, wall)
        if n == 1:
            row_mask = rows_of(owner * 2 + (cell >> 7), 2 * blocks)
            sums_ref[...] = add_up(wall, row_mask, hot(rows_of(cell & 127, lanes)))
    wall_ref[12:16] = jnp.zeros((4, lanes), F32)


def flow_kernel(
    place_ref,
    postf_ref,
    recva_ref,
    recvb_ref,
    edgea_ref,
    edgeb_ref,
    heat_ref,
    temper_ref,
    solid_ref,
    outf_ref,
    outh_ref,
):
    wide, deep, lanes = postf_ref.shape[1:]
    low, high = sides(place_ref[0] % 2 == 1, recva_ref, recvb_ref)
    get = planes(postf_ref, None, low, high, wide, None)
    edge = edge_rows(place_ref[1] % 2 == 1, edgea_ref, edgeb_ref, -1)
    for x in range(-1, wide + 1):
        flow = [stream(get, edge, deep, i, x) for i in range(FLOWS)]
        if x < 0:
            solid = low(FACES) != 0
        elif x >= wide:
            solid = high(FACES) != 0
        else:
            solid = solid_ref[x] != 0
        post, speed = collide_flow(flow, solid)
        heat = [heat_ref[k, x + 1] for k in range(HEATS)]
        posth = collide_heat(heat, temper_ref[x + 1], speed, solid)
        for i in range(FLOWS):
            outf_ref[i, x + 1] = post[i]
        for k in range(HEATS):
            outh_ref[k, x + 1] = posth[k]


def edge_kernel(
    place_ref,
    postf_ref,
    posth_ref,
    wall_ref,
    metals_ref,
    gathered_ref,
    senda_ref,
    sendb_ref,
    source_ref,
    *,
    blocks,
):
    wide = postf_ref.shape[1] - 2
    deep, lanes = postf_ref.shape[2:]
    block = place_ref[0]
    left = lax.rem(block + blocks - 1, blocks)
    right = lax.rem(block + 1, blocks)
    table = jnp.concatenate([metals_ref[d] for d in range(blocks)], axis=0)
    lists = [lists_of(gathered_ref[d, 0:ROW_SUMS]) for d in (left, block, right)]
    joined = [jnp.concatenate([item[n] for item in lists], axis=1) for n in range(3)]
    wall = one_row(wall_ref[0:12])
    flux = -wall_flux(table, joined, wall, blocks)
    entries = lists[0][0].shape[1]
    columns = wide * deep
    for n, (first, count, start) in enumerate(
        ((columns - deep, deep, 0), (0, columns, 1), (0, deep, wide + 1))
    ):
        node = lists[n][2]
        source = add_up(
            flux[:, n * entries : (n + 1) * entries],
            rows_of((node >> 7) - first, count),
            hot(rows_of(node & 127, lanes)),
        )
        source_ref[start : start + count // deep] = source.reshape(count // deep, deep, lanes)

    def fill(up_ref, down_ref):
        for ref, comps, row in ((up_ref, UP, deep - 1), (down_ref, DOWN, 0)):
            for x in range(wide):
                for n, i in enumerate(comps):
                    at = x + 1 - VELOCITY[i][0]
                    if i < FLOWS:
                        value = postf_ref[i, at]
                    else:
                        value = posth_ref[i - FLOWS, at]
                        value = value + WEIGHT_HEAT[i - FLOWS] * source_ref[at]
                    where = x * EDGES + n
                    ref[where : where + 1, :] = value[row : row + 1, :]

    @pl.when(place_ref[1] % 2 == 1)
    def _():
        fill(sendb_ref, senda_ref)

    @pl.when(place_ref[1] % 2 == 0)
    def _():
        fill(senda_ref, sendb_ref)


def final_kernel(
    place_ref, postf_ref, posth_ref, source_ref, edgea_ref, edgeb_ref, flow_ref, heat_ref
):
    wide, deep, lanes = flow_ref.shape[1:]

    def get(i, x):
        if i < FLOWS:
            return postf_ref[i, x + 1]
        return posth_ref[i - FLOWS, x + 1] + WEIGHT_HEAT[i - FLOWS] * source_ref[x + 1]

    edge = edge_rows(place_ref[1] % 2 == 1, edgea_ref, edgeb_ref, 0)
    for x in range(wide):
        for i in range(FLOWS):
            flow_ref[i, x] = stream(get, edge, deep, i, x)
        for k in range(HEATS):
            heat_ref[k, x] = stream(get, edge, deep, FLOWS + k, x)


def metal_kernel(place_ref, metal_ref, sums_ref, gathered_ref, conduction_ref, out_ref, *, blocks):
    block = place_ref[0]
    sums = sums_ref[0]
    counts = gathered_ref[0, ROW_SUMS + 2 * blocks : ROW_SUMS + 4 * blocks]
    for d in range(1, blocks):
        sums = sums + sums_ref[d]
        counts = counts + gathered_ref[d, ROW_SUMS + 2 * blocks : ROW_SUMS + 4 * blocks]
    total = tile_sums(sums, block)
    count = tile_sums(counts, block)
    halves = []
    for h in range(2):
        metal = metal_ref[h : h + 1]
        halves.append(metal + METAL_GAIN * WALL_COEFF * (total[h] - count[h] * metal))
    out_ref[...] = conduct(conduction_ref[...], halves)


def swap(value, axis, offset):
    count = lax.axis_size(axis)
    pairs = []
    for first in range(offset, count + offset, 2):
        one, other = first % count, (first + 1) % count
        pairs += [(one, other), (other, one)]
    return lax.ppermute(value, axis, pairs)


def local(
    populations,
    thermal,
    solid_mask,
    metal_temp,
    conduction,
    wall_count,
    wall_node,
    wall_owner,
    wall_cell,
):
    blocks = lax.axis_size("blk")
    wide, deep, lanes = solid_mask.shape
    place = jnp.stack([lax.axis_index("blk"), lax.axis_index("span")]).astype(jnp.int32)
    smem = pl.BlockSpec(memory_space=pltpu.SMEM)
    rows = ROW_SUMS + 4 * blocks

    def call(kernel, count, outs, name, flops=1000000):
        return pl.pallas_call(
            kernel,
            in_specs=[smem] + in_vmem(count),
            out_specs=jax.tree.map(lambda _: in_vmem(1)[0], outs),
            out_shape=outs,
            compiler_params=params(),
            name=name,
        )

    packet = call(
        functools.partial(packet_kernel, blocks=blocks), 5, shape(rows, lanes), "wall_packet"
    )(wall_count, thermal, metal_temp, wall_node, wall_owner.reshape(1, -1), wall_cell)
    gathered = lax.all_gather(packet, "blk")
    postf, posth, senda, sendb = call(
        collide_kernel,
        3,
        (
            shape(FLOWS, wide, deep, lanes),
            shape(HEATS, wide, deep, lanes),
            shape(FACES + 1, deep, lanes),
            shape(FACES + 1, deep, lanes),
        ),
        "collide_first",
    )(place, populations, thermal, solid_mask)
    recva = swap(senda, "blk", 0)
    recvb = swap(sendb, "blk", 1)
    edge_count = -(-(wide + 2) * EDGES // 8) * 8
    edgea, edgeb, metal, source = call(
        functools.partial(source_kernel, blocks=blocks),
        6,
        (
            shape(edge_count, lanes),
            shape(edge_count, lanes),
            shape(8, lanes),
            shape(wide + 4, deep, lanes),
        ),
        "source_first",
    )(place, postf, posth, recva, recvb, gathered, conduction)
    metals = lax.all_gather(metal, "blk")
    edgea = swap(edgea, "span", 0)
    edgeb = swap(edgeb, "span", 1)
    heat, temper, wall, sums = call(
        functools.partial(heat_kernel, blocks=blocks),
        7,
        (
            shape(HEATS, wide + 2, deep, lanes),
            shape(wide + 2, deep, lanes),
            shape(16, lanes),
            shape(2 * blocks, lanes),
        ),
        "heat_second",
    )(place, posth, recva, recvb, source, edgea, edgeb, gathered)
    sums = lax.all_gather(sums, "blk")
    postf, posth = call(
        flow_kernel,
        8,
        (shape(FLOWS, wide + 2, deep, lanes), shape(HEATS, wide + 2, deep, lanes)),
        "collide_second",
    )(place, postf, recva, recvb, edgea, edgeb, heat, temper, solid_mask)
    edgea, edgeb, source = call(
        functools.partial(edge_kernel, blocks=blocks),
        5,
        (
            shape(wide * EDGES, lanes),
            shape(wide * EDGES, lanes),
            shape(wide + 2, deep, lanes),
        ),
        "source_second",
    )(place, postf, posth, wall, metals, gathered)
    edgea = swap(edgea, "span", 0)
    edgeb = swap(edgeb, "span", 1)
    flow, heat = call(
        final_kernel,
        5,
        (shape(FLOWS, wide, deep, lanes), shape(HEATS, wide, deep, lanes)),
        "stream_last",
    )(place, postf, posth, source, edgea, edgeb)
    metal = call(
        functools.partial(metal_kernel, blocks=blocks), 4, shape(1, metal_temp.shape[1]), "metal_last"
    )(place, metal, sums, gathered, conduction)
    return (flow, heat, metal)


def solution(mesh):
    in_specs = (
        P(None, "blk", "span", None),
        P(None, "blk", "span", None),
        P("blk", "span", None),
        P("span", "blk"),
        P("span", "blk"),
        P("span", "blk"),
        P("span", "blk"),
        P("span", "blk", None),
        P("span", "blk"),
    )
    out_specs = (P(None, "blk", "span", None), P(None, "blk", "span", None), P("span", "blk"))
    return jax.shard_map(local, mesh=mesh, in_specs=in_specs, out_specs=out_specs, check_vma=False)
```

time: 99.3 us -> 50.2 us (0.51)
  waiting for transfers between devices: 34.3 us -> 0.02 us
  blocking collectives: 0 us -> 25.6 us
  starting transfers between devices: 27 us -> 9.87 us
  other arithmetic: 12 us -> 0.08 us
  matrix products: 11 us -> 0 us
  Pallas kernels: 0 us -> 9.57 us
  local copies, waits for them, and re-layouts: 11 us -> 3.43 us
  between operations: 2.87 us -> 1.36 us
    all_gather x0 -> x3, blocking collectives: none -> 25.6 us  [the longest x1 9.05 us: local(): metals = lax.all_gather(metal, 'blk')]
    ppermute x8 -> x6, waiting for transfers between devices: 22.9 us -> 0.02 us  [swap(): return lax.ppermute(value, axis, pairs)]
    all_to_all x5 -> x0, starting transfers between devices: 20.2 us -> none  [the longest x2 7.6 us: local(): lax.all_to_all(sent, 'blk', split_axis=0, concat_axis=0, tiled=True)]
    all_to_all x5 -> x0, waiting for transfers between devices: 11.4 us -> none  [the longest x2 7.41 us: local(): lax.all_to_all(slot_flux, 'blk', split_axis=0, concat_axis=0, tiled=True)]
    dot_general x15 -> x0, matrix products: 11 us -> none  [the longest x13 9.87 us: exact_dot(): jnp.dot(left, right, precision=lax.Precision.HIGHEST, preferred_element_t...]
    pallas_call x0 -> x8, Pallas kernels: none -> 9.57 us  [the longest x1 1.61 us: local(): call(final_kernel, 5, (shape(FLOWS, wide, deep, lanes), shape(HEATS, wide...]
    unnamed x82 -> x0, other arithmetic: 3.94 us -> none
    ppermute x8 -> x6, starting transfers between devices: 6.84 us -> 9.87 us  [swap(): return lax.ppermute(value, axis, pairs)]
  transfers between devices with their start and end apart: 13 -> 6, of which waited for: 10 -> 0; matrix products, arithmetic and copies ran while one was open for 12% -> 0% of each run, Pallas kernels for 0% -> 4%
where the time goes in v1:
time: 50.2 us; the launch traced here: 49.9 us
  blocking collectives  25.6 us (51%)
  starting transfers between devices  9.87 us (20%)
  Pallas kernels  9.57 us (19%)
  local copies, waits for them, and re-layouts  3.43 us (7%)
  between operations  1.36 us (3%)
    ppermute x6, starting transfers between devices, swap(): return lax.ppermute(value, axis, pairs)  9.87 us
    all_gather x1, blocking collectives, local(): metals = lax.all_gather(metal, 'blk')  9.05 us
    all_gather x1, blocking collectives, local(): gathered = lax.all_gather(packet, 'blk')  8.32 us
    all_gather x1, blocking collectives, local(): sums = lax.all_gather(sums, 'blk')  8.21 us
    unnamed x18, local copies, waits for them, and re-layouts  3.43 us
    pallas_call x1, Pallas kernels, local(): call(final_kernel, 5, (shape(FLOWS, wide, deep, lanes), shape(HEATS, wide...  1.61 us
    pallas_call x1, Pallas kernels, local(): call(functools.partial(source_kernel, blocks=blocks), 6, (shape(edge_coun...  1.57 us
    pallas_call x1, Pallas kernels, local(): call(functools.partial(metal_kernel, blocks=blocks), 4, shape(1, metal_te...  1.37 us
  transfers between devices with their start and end apart: 6, of which 0 were waited for; matrix products, arithmetic and copies ran while one was open for 0% of the time, Pallas kernels for 4%

profile of v1, /device:TPU:0, one launch (start us, length us, event | category | flops | bytes accessed | tf_op | source)
XLA Modules:
  0.0 49.9 jit_solution(12258251808349748169)
XLA Ops:
  0.6 0.1 pad_add_fusion.place_ref
  0.7 0.0 copy-start.1
  0.7 0.9 %copy-done.1 = f32[7,8,8,128]{3,2,1,0:T(8,128)S(1)} copy-done((f32[7,8,8,128]{3,2,1,0:T(8,128)S(1)}, f32[7,8,8,128]{3,2,1,0:T(8,128)}, u32[]{:S(2)}) %copy-start.1) | copy-done | bytes 229400
  1.6 0.0 copy-start.2
  1.7 1.1 %copy-done.2 = f32[19,8,8,128]{3,2,1,0:T(8,128)S(1)} copy-done((f32[19,8,8,128]{3,2,1,0:T(8,128)S(1)}, f32[19,8,8,128]{3,2,1,0:T(8,128)}, u32[]{:S(2)}) %copy-start.2) | copy-done | bytes 622616
  2.7 0.0 copy-start.3
  2.7 0.8 %copy-done.3 = s32[8,8,128]{2,1,0:T(8,128)S(1)} copy-done((s32[8,8,128]{2,1,0:T(8,128)S(1)}, s32[8,8,128]{2,1,0:T(8,128)}, u32[]{:S(2)}) %copy-start.3) | copy-done | bytes 32792
  3.5 0.0 copy-start.7
  3.5 0.9 %collide_first.1 = (f32[19,8,8,128]{3,2,1,0:T(8,128)S(1)}, f32[7,8,8,128]{3,2,1,0:T(8,128)S(1)}, f32[27,8,128]{2,1,0:T(8,128)S(1)}, f32[27,8,128]{2,1,0:T(8,128)S(1)}) custom-call(s32[2]{0:T(128)S(1)} %pad_add_fusion.place_ref, f32[19,8,8,128]{3,2,1,0:T(8,128)S(1)} %copy-done.2, f32[7,8,8,128]{3,2,1,0:T(8,128)S(1)} %copy-done.1, s32[8,8,128]{2,1,0:T(8,128)S(1)} %copy-done.3), custom_call_target="tpu_custom_call" | custom-call | tf_op jit(solution)/shard_map/collide_first/pallas_call | solution.py:611
  4.4 0.5 %collective-permute-start = (f32[27,8,128]{2,1,0:T(8,128)S(1)}, f32[27,8,128]{2,1,0:T(8,128)S(1)}, u32[]{:S(2)}, u32[]{:S(2)}) collective-permute-start(f32[27,8,128]{2,1,0:T(8,128)S(1)} %get-tuple-element.23), channel_id=1, source_target_pairs={{0,1},{1,0},{2,3},{3,2},{4,5},{5,4},{6,7},{7,6},{8,9},{9,8},{10,11... | collective-permute-start | bytes 331784 | tf_op jit(solution)/shard_map/ppermute | solution.py:577
  4.9 0.0 copy-start.6
  4.9 0.0 copy-start.5
  4.9 3.6 %collective-permute-start.1 = (f32[27,8,128]{2,1,0:T(8,128)S(1)}, f32[27,8,128]{2,1,0:T(8,128)S(1)}, u32[]{:S(2)}, u32[]{:S(2)}) collective-permute-start(f32[27,8,128]{2,1,0:T(8,128)S(1)} %get-tuple-element.24), channel_id=1, source_target_pairs={{1,2},{2,1},{3,4},{4,3},{5,6},{6,5},{7,0},{0,7},{9,10},{10,9},{11,... | collective-permute-start | bytes 331784 | tf_op jit(solution)/shard_map/ppermute | solution.py:577
  9.1 0.0 copy-start.8
  9.1 0.0 copy-done.7
  9.1 0.0 copy-done.6
  9.1 0.0 copy-done.5
  9.2 0.6 %copy-done.8 = f32[1,256]{1,0:T(1,128)S(1)} copy-done((f32[1,256]{1,0:T(1,128)S(1)}, f32[1,256]{1,0:T(1,128)}, u32[]{:S(2)}) %copy-start.8) | copy-done | bytes 1048
  9.8 0.0 copy-start
  9.8 0.5 wall_packet.1
  10.3 8.3 %all-gather = f32[448,128]{1,0:T(8,128)S(1)} all-gather(f32[56,128]{1,0:T(8,128)S(1)} %wall_packet.1), channel_id=2, replica_groups=mesh['span'=4,'blk'=8] {'blk'}, dimensions={0}, use_global_device_ids=true | all-gather | bytes 258048 | tf_op jit(solution)/shard_map/all_gather | solution.py:610
  18.6 0.0 collective-permute-done.recva_ref
  18.6 0.0 collective-permute-done.1.recvb_ref
  18.6 0.0 copy-done
  18.6 1.6 %source_first.1 = (f32[64,128]{1,0:T(8,128)S(1)}, f32[64,128]{1,0:T(8,128)S(1)}, f32[8,128]{1,0:T(8,128)S(1)}, f32[12,8,128]{2,1,0:T(8,128)S(1)}) custom-call(s32[2]{0:T(128)S(1)} %pad_add_fusion.place_ref, f32[19,8,8,128]{3,2,1,0:T(8,128)S(1)} %get-tuple-element.22.postf_ref, f32[7,8,8,128]{3,2,1,0:T(8,128)S(1)} %get-tuple-element.25.posth_ref, ...), custom_call_target="tpu_custom_call" | custom-call | tf_op jit(solution)/shard_map/source_first/pallas_call | solution.py:625
  20.2 1.6 %collective-permute-start.2 = (f32[64,128]{1,0:T(8,128)S(1)}, f32[64,128]{1,0:T(8,128)S(1)}, u32[]{:S(2)}, u32[]{:S(2)}) collective-permute-start(f32[64,128]{1,0:T(8,128)S(1)} %get-tuple-element.26), channel_id=1, source_target_pairs={{0,8},{8,0},{16,24},{24,16},{1,9},{9,1},{17,25},{25,17},{2,10},{10... | collective-permute-start | bytes 98312 | tf_op jit(solution)/shard_map/ppermute | solution.py:577
  21.8 2.5 %collective-permute-start.3 = (f32[64,128]{1,0:T(8,128)S(1)}, f32[64,128]{1,0:T(8,128)S(1)}, u32[]{:S(2)}, u32[]{:S(2)}) collective-permute-start(f32[64,128]{1,0:T(8,128)S(1)} %get-tuple-element.27), channel_id=1, source_target_pairs={{8,16},{16,8},{24,0},{0,24},{9,17},{17,9},{25,1},{1,25},{10,18},{1... | collective-permute-start | bytes 98312 | tf_op jit(solution)/shard_map/ppermute | solution.py:577
  24.3 9.1 %all-gather.1 = f32[64,128]{1,0:T(8,128)S(1)} all-gather(f32[8,128]{1,0:T(8,128)S(1)} %get-tuple-element.34.metal_ref), channel_id=3, replica_groups=mesh['span'=4,'blk'=8] {'blk'}, dimensions={0}, use_global_device_ids=true | all-gather | bytes 36864 | tf_op jit(solution)/shard_map/all_gather | solution.py:636
  33.3 0.0 collective-permute-done.2.edgea_ref
  33.4 0.0 collective-permute-done.3.edgeb_ref
  33.4 0.0 copy-start.4
  33.4 1.3 %heat_second.1 = (f32[7,10,8,128]{3,2,1,0:T(8,128)S(1)}, f32[10,8,128]{2,1,0:T(8,128)S(1)}, f32[16,128]{1,0:T(8,128)S(1)}, f32[16,128]{1,0:T(8,128)S(1)}) custom-call(s32[2]{0:T(128)S(1)} %pad_add_fusion.place_ref, f32[7,8,8,128]{3,2,1,0:T(8,128)S(1)} %get-tuple-element.25.posth_ref, f32[27,8,128]{2,1,0:T(8,128)S(1)} %collective-permute-done.recva_ref, ...), custom_call_target="tpu_custom_call" | custom-call | tf_op jit(solution)/shard_map/heat_second/pallas_call | solution.py:639
  34.6 0.0 copy-done.4
  34.6 1.0 %collide_second.1 = (f32[19,10,8,128]{3,2,1,0:T(8,128)S(1)}, f32[7,10,8,128]{3,2,1,0:T(8,128)S(1)}) custom-call(s32[2]{0:T(128)S(1)} %pad_add_fusion.place_ref, f32[19,8,8,128]{3,2,1,0:T(8,128)S(1)} %get-tuple-element.22.postf_ref, f32[27,8,128]{2,1,0:T(8,128)S(1)} %collective-permute-done.recva_ref, f32[27,8,128]{2,1,0:T(8,128)S(1)} %collective-permute-done.1.recvb_ref, ...), custom_call_target="tpu_custom_call" | custom-call | tf_op jit(solution)/shard_map/collide_second/pallas_call | solution.py:651
  35.7 1.4 %source_second.1 = (f32[48,128]{1,0:T(8,128)S(1)}, f32[48,128]{1,0:T(8,128)S(1)}, f32[10,8,128]{2,1,0:T(8,128)S(1)}) custom-call(s32[2]{0:T(128)S(1)} %pad_add_fusion.place_ref, f32[19,10,8,128]{3,2,1,0:T(8,128)S(1)} %get-tuple-element.31.postf_ref, f32[7,10,8,128]{3,2,1,0:T(8,128)S(1)} %get-tuple-element.32.posth_ref, ...), custom_call_target="tpu_custom_call" | custom-call | tf_op jit(solution)/shard_map/source_second/pallas_call | solution.py:657
  37.1 0.7 %collective-permute-start.4 = (f32[48,128]{1,0:T(8,128)S(1)}, f32[48,128]{1,0:T(8,128)S(1)}, u32[]{:S(2)}, u32[]{:S(2)}) collective-permute-start(f32[48,128]{1,0:T(8,128)S(1)} %get-tuple-element.36), channel_id=1, source_target_pairs={{0,8},{8,0},{16,24},{24,16},{1,9},{9,1},{17,25},{25,17},{2,10},{10... | collective-permute-start | bytes 73736 | tf_op jit(solution)/shard_map/ppermute | solution.py:577
  37.8 0.9 %collective-permute-start.5 = (f32[48,128]{1,0:T(8,128)S(1)}, f32[48,128]{1,0:T(8,128)S(1)}, u32[]{:S(2)}, u32[]{:S(2)}) collective-permute-start(f32[48,128]{1,0:T(8,128)S(1)} %get-tuple-element.37), channel_id=1, source_target_pairs={{8,16},{16,8},{24,0},{0,24},{9,17},{17,9},{25,1},{1,25},{10,18},{1... | collective-permute-start | bytes 73736 | tf_op jit(solution)/shard_map/ppermute | solution.py:577
  38.7 8.2 %all-gather.2 = f32[128,128]{1,0:T(8,128)S(1)} all-gather(f32[16,128]{1,0:T(8,128)S(1)} %get-tuple-element.40), channel_id=4, replica_groups=mesh['span'=4,'blk'=8] {'blk'}, dimensions={0}, use_global_device_ids=true | all-gather | bytes 73728 | tf_op jit(solution)/shard_map/all_gather | solution.py:650
  46.9 1.4 %metal_last.1 = f32[1,256]{1,0:T(1,128)} custom-call(s32[2]{0:T(128)S(1)} %pad_add_fusion.place_ref, f32[8,128]{1,0:T(8,128)S(1)} %get-tuple-element.34.metal_ref, f32[8,16,128]{2,1,0:T(8,128)S(1)} %bitcast.10, f32[8,56,128]{2,1,0:T(8,128)S(1)} %bitcast.9, f32[256,256]{1,0:T(8,128)S(1)} %copy-done), custom_call_target="tpu_custom_call" | custom-call | tf_op jit(solution)/shard_map/metal_last/pallas_call | solution.py:675
  48.3 0.0 collective-permute-done.4.edgea_ref
  48.3 0.0 collective-permute-done.5.edgeb_ref
  48.3 1.6 %stream_last.1 = (f32[19,8,8,128]{3,2,1,0:T(8,128)}, f32[7,8,8,128]{3,2,1,0:T(8,128)}) custom-call(s32[2]{0:T(128)S(1)} %pad_add_fusion.place_ref, f32[19,10,8,128]{3,2,1,0:T(8,128)S(1)} %get-tuple-element.31.postf_ref, f32[7,10,8,128]{3,2,1,0:T(8,128)S(1)} %get-tuple-element.32.posth_ref, f32[10,8,128]{2,1,0:T(8,128)S(1)} %get-tuple-element.35.source_ref, ...), custom_call_target="tpu_custom_call" | custom-call | tf_op jit(solution)/shard_map/stream_last/pallas_call | solution.py:669
Async XLA Ops:
  0.7 0.9 %copy-start.1 = (f32[7,8,8,128]{3,2,1,0:T(8,128)S(1)}, f32[7,8,8,128]{3,2,1,0:T(8,128)}, u32[]{:S(2)}) copy-start(f32[7,8,8,128]{3,2,1,0:T(8,128)} %heat_ref.3) | copy-start | bytes 688132
  1.6 1.1 %copy-start.2 = (f32[19,8,8,128]{3,2,1,0:T(8,128)S(1)}, f32[19,8,8,128]{3,2,1,0:T(8,128)}, u32[]{:S(2)}) copy-start(f32[19,8,8,128]{3,2,1,0:T(8,128)} %flow_ref.1) | copy-start | bytes 1867780
  2.7 0.8 %copy-start.3 = (s32[8,8,128]{2,1,0:T(8,128)S(1)}, s32[8,8,128]{2,1,0:T(8,128)}, u32[]{:S(2)}) copy-start(s32[8,8,128]{2,1,0:T(8,128)} %solid_ref.3) | copy-start | bytes 98308
  3.5 5.6 %copy-start.7 = (s32[1,512]{1,0:T(1,128)S(1)}, s32[1,512]{1,0:T(1,128)}, u32[]{:S(2)}) copy-start(s32[1,512]{1,0:T(1,128)} %cell_ref.1) | copy-start | bytes 6148
  4.4 14.2 %collective-permute-start = (f32[27,8,128]{2,1,0:T(8,128)S(1)}, f32[27,8,128]{2,1,0:T(8,128)S(1)}, u32[]{:S(2)}, u32[]{:S(2)}) collective-permute-start(f32[27,8,128]{2,1,0:T(8,128)S(1)} %get-tuple-element.23), channel_id=1, source_target_pairs={{0,1},{1,0},{2,3},{3,2},{4,5},{5,4},{6,7},{7,6},{8,9},{9,8},{10,11... | collective-permute-start | bytes 331784 | tf_op jit(solution)/shard_map/ppermute | solution.py:577
  4.9 4.2 %copy-start.6 = (s32[1,512,1]{1,2,0:T(1,128)S(1)}, s32[1,512,1]{1,2,0:T(1,128)}, u32[]{:S(2)}) copy-start(s32[1,512,1]{1,2,0:T(1,128)} %param.16) | copy-start | bytes 6148
  4.9 4.2 %copy-start.5 = (s32[1,512]{1,0:T(1,128)S(1)}, s32[1,512]{1,0:T(1,128)}, u32[]{:S(2)}) copy-start(s32[1,512]{1,0:T(1,128)} %node_ref.1) | copy-start | bytes 6148
  4.9 13.7 %collective-permute-start.1 = (f32[27,8,128]{2,1,0:T(8,128)S(1)}, f32[27,8,128]{2,1,0:T(8,128)S(1)}, u32[]{:S(2)}, u32[]{:S(2)}) collective-permute-start(f32[27,8,128]{2,1,0:T(8,128)S(1)} %get-tuple-element.24), channel_id=1, source_target_pairs={{1,2},{2,1},{3,4},{4,3},{5,6},{6,5},{7,0},{0,7},{9,10},{10,9},{11,... | collective-permute-start | bytes 331784 | tf_op jit(solution)/shard_map/ppermute | solution.py:577
  9.1 0.7 %copy-start.8 = (f32[1,256]{1,0:T(1,128)S(1)}, f32[1,256]{1,0:T(1,128)}, u32[]{:S(2)}) copy-start(f32[1,256]{1,0:T(1,128)} %metal_ref.1) | copy-start | bytes 3076
  9.8 8.8 %copy-start = (f32[256,256]{1,0:T(8,128)S(1)}, f32[256,256]{1,0:T(8,128)}, u32[]{:S(2)}) copy-start(f32[256,256]{1,0:T(8,128)} %conduction_ref.3) | copy-start | bytes 786436
  20.2 13.2 %collective-permute-start.2 = (f32[64,128]{1,0:T(8,128)S(1)}, f32[64,128]{1,0:T(8,128)S(1)}, u32[]{:S(2)}, u32[]{:S(2)}) collective-permute-start(f32[64,128]{1,0:T(8,128)S(1)} %get-tuple-element.26), channel_id=1, source_target_pairs={{0,8},{8,0},{16,24},{24,16},{1,9},{9,1},{17,25},{25,17},{2,10},{10... | collective-permute-start | bytes 98312 | tf_op jit(solution)/shard_map/ppermute | solution.py:577
  21.8 11.5 %collective-permute-start.3 = (f32[64,128]{1,0:T(8,128)S(1)}, f32[64,128]{1,0:T(8,128)S(1)}, u32[]{:S(2)}, u32[]{:S(2)}) collective-permute-start(f32[64,128]{1,0:T(8,128)S(1)} %get-tuple-element.27), channel_id=1, source_target_pairs={{8,16},{16,8},{24,0},{0,24},{9,17},{17,9},{25,1},{1,25},{10,18},{1... | collective-permute-start | bytes 98312 | tf_op jit(solution)/shard_map/ppermute | solution.py:577
  33.4 1.3 %copy-start.4 = (s32[8,8,128]{2,1,0:T(8,128)S(1)}, s32[8,8,128]{2,1,0:T(8,128)}, u32[]{:S(2)}) copy-start(s32[8,8,128]{2,1,0:T(8,128)} %solid_ref.3) | copy-start | bytes 98308
  37.1 11.2 %collective-permute-start.4 = (f32[48,128]{1,0:T(8,128)S(1)}, f32[48,128]{1,0:T(8,128)S(1)}, u32[]{:S(2)}, u32[]{:S(2)}) collective-permute-start(f32[48,128]{1,0:T(8,128)S(1)} %get-tuple-element.36), channel_id=1, source_target_pairs={{0,8},{8,0},{16,24},{24,16},{1,9},{9,1},{17,25},{25,17},{2,10},{10... | collective-permute-start | bytes 73736 | tf_op jit(solution)/shard_map/ppermute | solution.py:577
  37.8 10.5 %collective-permute-start.5 = (f32[48,128]{1,0:T(8,128)S(1)}, f32[48,128]{1,0:T(8,128)S(1)}, u32[]{:S(2)}, u32[]{:S(2)}) collective-permute-start(f32[48,128]{1,0:T(8,128)S(1)} %get-tuple-element.37), channel_id=1, source_target_pairs={{8,16},{16,8},{24,0},{0,24},{9,17},{17,9},{25,1},{1,25},{10,18},{1... | collective-permute-start | bytes 73736 | tf_op jit(solution)/shard_map/ppermute | solution.py:577

commit v2 on v1

v2 whole, which is shorter than its diff:
```python
import jax
import jax.numpy as jnp
from jax import lax
from jax.experimental import pallas as pl
from jax.experimental.pallas import tpu as pltpu
from jax.sharding import PartitionSpec as P

VELOCITY_FLOW = [
    (0, 0, 0),
    (1, 0, 0),
    (-1, 0, 0),
    (0, 1, 0),
    (0, -1, 0),
    (0, 0, 1),
    (0, 0, -1),
    (1, 1, 0),
    (-1, -1, 0),
    (1, -1, 0),
    (-1, 1, 0),
    (1, 0, 1),
    (-1, 0, -1),
    (1, 0, -1),
    (-1, 0, 1),
    (0, 1, 1),
    (0, -1, -1),
    (0, 1, -1),
    (0, -1, 1),
]
WEIGHT_FLOW = [1.0 / 3.0] + [1.0 / 18.0] * 6 + [1.0 / 36.0] * 12
OPPOSITE = [0, 2, 1, 4, 3, 6, 5, 8, 7, 10, 9, 12, 11, 14, 13, 16, 15, 18, 17]
WEIGHT_HEAT = [0.25] + [0.125] * 6
VELOCITY = VELOCITY_FLOW + VELOCITY_FLOW[:7]
FLOWS, HEATS = 19, 7
ALL = FLOWS + HEATS
RELAX_FLOW = 0.8
RELAX_HEAT = 0.9
WALL_COEFF = 0.5
METAL_GAIN = 0.5

FACE_RIGHT = [(i, 0) for i in range(ALL) if VELOCITY[i][0] >= 0] + [
    (i, 1) for i in range(ALL) if VELOCITY[i][0] == 1
]
FACE_LEFT = [(i, 0) for i in range(ALL) if VELOCITY[i][0] <= 0] + [
    (i, 1) for i in range(ALL) if VELOCITY[i][0] == -1
]
FACES = len(FACE_RIGHT)
UP = [i for i in range(ALL) if VELOCITY[i][2] == 1]
DOWN = [i for i in range(ALL) if VELOCITY[i][2] == -1]
EDGES = len(UP)

SOLID, COUNTS, LISTS = FACES, FACES + 1, FACES + 2
SIDE_PLANES = FACES + 4
LIST_ROWS = 12
LANES = 128
F32 = jnp.float32
BF16 = jnp.bfloat16


def params(mebibytes=32):
    return pltpu.CompilerParams(vmem_limit_bytes=mebibytes * 1024 * 1024)


def in_vmem(count):
    return [pl.BlockSpec(memory_space=pltpu.VMEM)] * count


def shape(*dims):
    return jax.ShapeDtypeStruct(dims, F32)


def split(value):
    high = value.astype(BF16)
    rest = value - high.astype(F32)
    middle = rest.astype(BF16)
    low = (rest - middle.astype(F32)).astype(BF16)
    return high, middle, low


def dot(left, right, dims):
    return lax.dot_general(left, right, (dims, ((), ())), preferred_element_type=F32)


def rows_of(row, count):
    return lax.broadcasted_iota(jnp.int32, (count, row.shape[1]), 0) == row


def hot(mask):
    return jnp.where(mask, 1.0, 0.0).astype(BF16)


def look_up(table, row_hot, lane_mask):
    turned = jnp.transpose(table)
    found = sum([dot(part, row_hot, ((1,), (0,))) for part in split(turned)])
    return jnp.sum(jnp.where(lane_mask, found, 0.0), axis=0, keepdims=True)


def add_up(values, row_mask, lane_hot):
    count = row_mask.shape[0]
    stacked = jnp.concatenate(
        [jnp.where(row_mask, part.astype(F32), 0.0) for part in split(values)], axis=0
    ).astype(BF16)
    sums = dot(stacked, lane_hot, ((1,), (1,)))
    return sums[:count] + sums[count : 2 * count] + sums[2 * count :]


def one_row(block):
    return jnp.concatenate([block[r : r + 1] for r in range(block.shape[0])], axis=1)


def put_rows(ref, start, row):
    for r in range(row.shape[1] // LANES):
        ref[start + r : start + r + 1, :] = row[:, r * LANES : (r + 1) * LANES]


def lists_of(block):
    return [one_row(block[4 * n : 4 * n + 4]).astype(jnp.int32) for n in range(3)]


def packet_kernel(
    count_ref, heat_ref, metal_ref, node_ref, owner_ref, cell_ref, out_ref, list_ref, counts_ref
):
    blocks = out_ref.shape[0]
    wide, deep, lanes = heat_ref.shape[1:]
    temper = heat_ref[0]
    for k in range(1, HEATS):
        temper = temper + heat_ref[k]
    temper = temper.reshape(wide * deep, lanes)
    node = node_ref[...]
    cell = cell_ref[...]
    entries = node.shape[1]
    live = lax.broadcasted_iota(jnp.int32, (1, entries), 1) < count_ref[0, 0]
    owner = jnp.where(live, owner_ref[...], -1)
    list_ref[8:16, :] = jnp.zeros((8, lanes), F32)
    put_rows(list_ref, 0, owner.astype(F32))
    put_rows(list_ref, 4, cell.astype(F32))
    put_rows(list_ref, 8, node.astype(F32))
    put_rows(list_ref, LIST_ROWS, metal_ref[...])
    column_hot = hot(rows_of(node >> 7, wide * deep))
    lane_mask = rows_of(node & 127, lanes)
    wall = look_up(temper, column_hot, lane_mask)
    cell_hot = hot(rows_of(cell & 127, lanes))
    row_mask = rows_of(owner * 2 + (cell >> 7), 2 * blocks)
    sums = add_up(wall, row_mask, cell_hot)
    counts = dot(hot(row_mask), cell_hot, ((1,), (1,)))
    for d in range(blocks):
        put_rows(out_ref.at[d], 0, metal_ref[...])
        out_ref[d, 2:4, :] = sums[2 * d : 2 * d + 2]
        out_ref[d, 4:6, :] = counts[2 * d : 2 * d + 2]
        out_ref[d, 6:8, :] = jnp.zeros((2, lanes), F32)
    at_nodes = dot(
        hot(rows_of(jnp.where(live, node >> 7, -1), wide * deep)), hot(lane_mask), ((1,), (1,))
    )
    counts_ref[...] = at_nodes.reshape(wide, deep, lanes)


def collide_flow(flow, solid):
    density = flow[0]
    for i in range(1, FLOWS):
        density = density + flow[i]
    inverse = 1.0 / density
    speed = []
    for axis in range(3):
        ahead = [flow[i] for i in range(FLOWS) if VELOCITY[i][axis] == 1]
        behind = [flow[i] for i in range(FLOWS) if VELOCITY[i][axis] == -1]
        speed.append((sum(ahead[1:], ahead[0]) - sum(behind[1:], behind[0])) * inverse)
    base = 1.0 - 1.5 * (speed[0] * speed[0] + speed[1] * speed[1] + speed[2] * speed[2])
    scaled = {w: density * (w / RELAX_FLOW) for w in sorted(set(WEIGHT_FLOW))}
    keep = 1.0 - 1.0 / RELAX_FLOW
    post = [None] * FLOWS
    rest = scaled[WEIGHT_FLOW[0]] * base + keep * flow[0]
    post[0] = jnp.where(solid, flow[0], rest)
    for i in range(1, FLOWS, 2):
        along = None
        for axis in range(3):
            c = VELOCITY[i][axis]
            if c == 0:
                continue
            term = speed[axis]
            if along is None:
                along = term if c == 1 else -term
            else:
                along = along + term if c == 1 else along - term
        weight = scaled[WEIGHT_FLOW[i]]
        even = weight * (base + 4.5 * along * along)
        odd = weight * (3.0 * along)
        j = OPPOSITE[i]
        post[i] = jnp.where(solid, flow[j], even + odd + keep * flow[i])
        post[j] = jnp.where(solid, flow[i], even - odd + keep * flow[j])
    return post, speed


def collide_heat(heat, temper, speed, solid):
    keep = 1.0 - 1.0 / RELAX_HEAT
    post = [None] * HEATS
    post[0] = jnp.where(
        solid, heat[0], temper * (WEIGHT_HEAT[0] / RELAX_HEAT) + keep * heat[0]
    )
    scaled = temper * (WEIGHT_HEAT[1] / RELAX_HEAT)
    for axis in range(3):
        i = 2 * axis + 1
        j = i + 1
        odd = scaled * (4.0 * speed[axis])
        post[i] = jnp.where(solid, heat[j], scaled + odd + keep * heat[i])
        post[j] = jnp.where(solid, heat[i], scaled - odd + keep * heat[j])
    return post


def lose(post, counts, temper):
    lost = counts * temper * -WALL_COEFF
    return [post[k] + WEIGHT_HEAT[k] * lost for k in range(HEATS)]


def collide_kernel(
    place_ref,
    flow_ref,
    heat_ref,
    solid_ref,
    counts_ref,
    list_ref,
    postf_ref,
    posth_ref,
    senda_ref,
    sendb_ref,
):
    wide = flow_ref.shape[1]
    odd = place_ref[0] % 2 == 1
    for x in range(wide):
        flow = [flow_ref[i, x] for i in range(FLOWS)]
        heat = [heat_ref[k, x] for k in range(HEATS)]
        solid = solid_ref[x] != 0
        temper = heat[0]
        for k in range(1, HEATS):
            temper = temper + heat[k]
        post, speed = collide_flow(flow, solid)
        posth = lose(collide_heat(heat, temper, speed, solid), counts_ref[x], temper)
        for i in range(FLOWS):
            postf_ref[i, x] = post[i]
        for k in range(HEATS):
            posth_ref[k, x] = posth[k]

    def plane(i, x):
        return postf_ref[i, x] if i < FLOWS else posth_ref[i - FLOWS, x]

    def fill(right_ref, left_ref):
        for ref, faces, edge in ((right_ref, FACE_RIGHT, wide - 1), (left_ref, FACE_LEFT, 0)):
            for n, (i, depth) in enumerate(faces):
                ref[n] = plane(i, abs(edge - depth))
            ref[SOLID] = solid_ref[edge].astype(F32)
            ref[COUNTS] = counts_ref[edge]
            ref[LISTS] = list_ref[0:8]
            ref[LISTS + 1] = list_ref[8:16]

    @pl.when(odd)
    def _():
        fill(sendb_ref, senda_ref)

    @pl.when(jnp.logical_not(odd))
    def _():
        fill(senda_ref, sendb_ref)


def sides(odd, a_ref, b_ref):
    def low(n):
        return jnp.where(odd, a_ref[n], b_ref[n])

    def high(n):
        return jnp.where(odd, b_ref[n], a_ref[n])

    return low, high


def side_lists(get):
    return lists_of(jnp.concatenate([get(LISTS), get(LISTS + 1)], axis=0))


def planes(postf_ref, posth_ref, low, high, wide, source_ref):
    def get(i, x):
        if x < 0:
            value = low(FACE_RIGHT.index((i, -1 - x)))
        elif x >= wide:
            value = high(FACE_LEFT.index((i, x - wide)))
        elif i < FLOWS:
            value = postf_ref[i, x]
        else:
            value = posth_ref[i - FLOWS, x]
        if i >= FLOWS and source_ref is not None:
            value = value + WEIGHT_HEAT[i - FLOWS] * source_ref[x + 2]
        return value

    return get


def metal_at(table, lists, shift=0):
    owner, cell, node = lists
    row = jnp.where(owner < 0, -1, owner * 8 + (cell >> 7) + shift)
    return look_up(table, hot(rows_of(row, table.shape[0])), rows_of(cell & 127, LANES))


def give(metal, row, node, count):
    return add_up(WALL_COEFF * metal, rows_of(row, count), hot(rows_of(node & 127, LANES)))


def join(lists):
    return [jnp.concatenate([item[n] for item in lists], axis=1) for n in range(3)]


def give_planes(table, lists, parts, deep, source_ref):
    metal = metal_at(table, join(lists))
    entries = lists[0][0].shape[1]
    for n, (first, count, start) in enumerate(parts):
        node = lists[n][2]
        source = give(metal[:, n * entries : (n + 1) * entries], (node >> 7) - first, node, count)
        source_ref[start : start + count // deep] = source.reshape(count // deep, deep, LANES)


def conduct(conduction, halves):
    vector = jnp.concatenate(halves, axis=1)
    parts = split(vector)
    rows = lax.broadcasted_iota(jnp.int32, (16, vector.shape[1]), 0)
    stacked = jnp.zeros((16, vector.shape[1]), F32)
    for r, part in enumerate(parts):
        stacked = jnp.where(rows == r, part.astype(F32), stacked)
    stacked = stacked.astype(BF16)
    out = sum([dot(stacked, part, ((1,), (1,))) for part in split(conduction)])
    return out[0:1] + out[1:2] + out[2:3]


def next_metal(conduction, metal, total, count):
    gained = WALL_COEFF * (total - count * metal)
    value = metal + METAL_GAIN * gained
    return conduct(conduction, [value[0:1], value[1:2]])


def source_kernel(
    place_ref,
    postf_ref,
    posth_ref,
    recva_ref,
    recvb_ref,
    list_ref,
    chunks_ref,
    conduction_ref,
    senda_ref,
    sendb_ref,
    metal_ref,
    source_ref,
):
    wide, deep, lanes = postf_ref.shape[1:]
    blocks = chunks_ref.shape[0]
    low, high = sides(place_ref[0] % 2 == 1, recva_ref, recvb_ref)
    table = chunks_ref[...].reshape(blocks * 8, lanes)
    columns = wide * deep
    give_planes(
        table,
        [side_lists(low), lists_of(list_ref[...]), side_lists(high)],
        ((columns - 2 * deep, 2 * deep, 0), (0, columns, 2), (0, 2 * deep, wide + 2)),
        deep,
        source_ref,
    )
    get = planes(postf_ref, posth_ref, low, high, wide, source_ref)
    sums = chunks_ref[0]
    for d in range(1, blocks):
        sums = sums + chunks_ref[d]
    count = sums[4:6]
    metal = next_metal(conduction_ref[...], list_ref[LIST_ROWS : LIST_ROWS + 2], sums[2:4], count)
    metal_ref[...] = jnp.zeros(metal_ref.shape, F32)
    put_rows(metal_ref, 0, metal)
    metal_ref[2:4, :] = count

    def fill(up_ref, down_ref):
        for ref, comps, row in ((up_ref, UP, deep - 1), (down_ref, DOWN, 0)):
            for j in range(wide + 2):
                for n, i in enumerate(comps):
                    value = get(i, j - 1 - VELOCITY[i][0])
                    at = j * EDGES + n
                    ref[at : at + 1, :] = value[row : row + 1, :]
            at = (wide + 2) * EDGES
            put_rows(ref, at, metal)
            ref[at + 2 : at + 2 + LIST_ROWS, :] = list_ref[0:LIST_ROWS]

    for ref in (senda_ref, sendb_ref):
        ref[ref.shape[0] - 8 :, :] = jnp.zeros((8, lanes), F32)

    @pl.when(place_ref[1] % 2 == 1)
    def _():
        fill(sendb_ref, senda_ref)

    @pl.when(place_ref[1] % 2 == 0)
    def _():
        fill(senda_ref, sendb_ref)


def stream(get, edge, deep, i, x):
    cx, cy, cz = VELOCITY[i]
    value = get(i, x - cx)
    if cz != 0:
        rows = lax.broadcasted_iota(jnp.int32, value.shape, 0)
        if cz == 1:
            value = jnp.where(rows == 0, edge(i, x), pltpu.roll(value, 1, 0))
        else:
            value = jnp.where(rows == deep - 1, edge(i, x), pltpu.roll(value, deep - 1, 0))
    if cy != 0:
        value = pltpu.roll(value, cy % value.shape[1], 1)
    return value


def edge_rows(odd, a_ref, b_ref, first):
    def edge(i, x):
        comps = UP if VELOCITY[i][2] == 1 else DOWN
        at = (x - first) * EDGES + comps.index(i)
        a = a_ref[at : at + 1, :]
        b = b_ref[at : at + 1, :]
        if VELOCITY[i][2] == 1:
            return jnp.where(odd, a, b)
        return jnp.where(odd, b, a)

    return edge


def heat_kernel(
    place_ref,
    posth_ref,
    recva_ref,
    recvb_ref,
    source_ref,
    edgea_ref,
    edgeb_ref,
    list_ref,
    metal_ref,
    heat_ref,
    out_ref,
):
    wide, deep, lanes = posth_ref.shape[1:]
    blocks = out_ref.shape[0]
    low, high = sides(place_ref[0] % 2 == 1, recva_ref, recvb_ref)
    get = planes(None, posth_ref, low, high, wide, source_ref)
    odd = place_ref[1] % 2 == 1
    edge = edge_rows(odd, edgea_ref, edgeb_ref, -1)
    tempers = []
    for x in range(-1, wide + 1):
        temper = None
        for k in range(HEATS):
            value = stream(get, edge, deep, FLOWS + k, x)
            heat_ref[k, x + 1] = value
            temper = value if temper is None else temper + value
        if 0 <= x < wide:
            tempers.append(temper)
    columns = wide * deep
    owner, cell, node = lists_of(list_ref[...])
    wall = look_up(
        jnp.concatenate(tempers, axis=0),
        hot(rows_of(node >> 7, columns)),
        rows_of(node & 127, lanes),
    )
    row_mask = rows_of(owner * 2 + (cell >> 7), 2 * blocks)
    sums = add_up(wall, row_mask, hot(rows_of(cell & 127, lanes)))
    at = (wide + 2) * EDGES
    a = edgea_ref[at : at + 2, :]
    b = edgeb_ref[at : at + 2, :]
    for d in range(blocks):
        out_ref[d, 0:2, :] = metal_ref[0:2]
        out_ref[d, 2:4, :] = jnp.where(odd, a, b)
        out_ref[d, 4:6, :] = jnp.where(odd, b, a)
        out_ref[d, 6:8, :] = sums[2 * d : 2 * d + 2]


def flow_kernel(
    place_ref,
    postf_ref,
    recva_ref,
    recvb_ref,
    edgea_ref,
    edgeb_ref,
    heat_ref,
    solid_ref,
    counts_ref,
    outf_ref,
    outh_ref,
    senda_ref,
    sendb_ref,
):
    wide, deep, lanes = postf_ref.shape[1:]
    low, high = sides(place_ref[0] % 2 == 1, recva_ref, recvb_ref)
    get = planes(postf_ref, None, low, high, wide, None)
    edge = edge_rows(place_ref[1] % 2 == 1, edgea_ref, edgeb_ref, -1)
    for x in range(-1, wide + 1):
        flow = [stream(get, edge, deep, i, x) for i in range(FLOWS)]
        if x < 0:
            solid, counts = low(SOLID) != 0, low(COUNTS)
        elif x >= wide:
            solid, counts = high(SOLID) != 0, high(COUNTS)
        else:
            solid, counts = solid_ref[x] != 0, counts_ref[x]
        post, speed = collide_flow(flow, solid)
        heat = [heat_ref[k, x + 1] for k in range(HEATS)]
        temper = heat[0]
        for k in range(1, HEATS):
            temper = temper + heat[k]
        posth = lose(collide_heat(heat, temper, speed, solid), counts, temper)
        for i in range(FLOWS):
            outf_ref[i, x + 1] = post[i]
        for k in range(HEATS):
            outh_ref[k, x + 1] = posth[k]

    def fill(up_ref, down_ref):
        for ref, comps, row in ((up_ref, UP, deep - 1), (down_ref, DOWN, 0)):
            for x in range(wide):
                for n, i in enumerate(comps):
                    at = x + 1 - VELOCITY[i][0]
                    value = outf_ref[i, at] if i < FLOWS else outh_ref[i - FLOWS, at]
                    where = x * EDGES + n
                    ref[where : where + 1, :] = value[row : row + 1, :]

    @pl.when(place_ref[1] % 2 == 1)
    def _():
        fill(sendb_ref, senda_ref)

    @pl.when(place_ref[1] % 2 == 0)
    def _():
        fill(senda_ref, sendb_ref)


def last_metal_kernel(
    place_ref,
    recva_ref,
    recvb_ref,
    list_ref,
    chunks_ref,
    edgea_ref,
    edgeb_ref,
    metal_ref,
    conduction_ref,
    source_ref,
    row_ref,
    out_ref,
):
    blocks = chunks_ref.shape[0]
    wide, deep, lanes = source_ref.shape
    wide = wide - 2
    low, high = sides(place_ref[0] % 2 == 1, recva_ref, recvb_ref)
    table = chunks_ref[...].reshape(blocks * 8, lanes)
    columns = wide * deep
    give_planes(
        table,
        [side_lists(low), lists_of(list_ref[...]), side_lists(high)],
        ((columns - deep, deep, 0), (0, columns, 1), (0, deep, wide + 1)),
        deep,
        source_ref,
    )
    odd = place_ref[1] % 2 == 1
    at = (wide + 2) * EDGES + 2
    a = edgea_ref[at : at + LIST_ROWS, :]
    b = edgeb_ref[at : at + LIST_ROWS, :]
    for n, (block, shift, z) in enumerate(
        ((jnp.where(odd, a, b), 2, deep - 1), (jnp.where(odd, b, a), 4, 0))
    ):
        lists = lists_of(block)
        node = lists[2]
        column = node >> 7
        row = jnp.where(lax.rem(column, deep) == z, lax.div(column, deep), -1)
        row_ref[wide * n : wide * (n + 1), :] = give(
            metal_at(table, lists, shift), row, node, wide
        )
    sums = chunks_ref[0]
    for d in range(1, blocks):
        sums = sums + chunks_ref[d]
    out_ref[...] = next_metal(conduction_ref[...], metal_ref[0:2], sums[6:8], metal_ref[2:4])


def final_kernel(
    place_ref, postf_ref, posth_ref, source_ref, row_ref, edgea_ref, edgeb_ref, flow_ref, heat_ref
):
    wide, deep, lanes = flow_ref.shape[1:]

    def get(i, x):
        if i < FLOWS:
            return postf_ref[i, x + 1]
        return posth_ref[i - FLOWS, x + 1] + WEIGHT_HEAT[i - FLOWS] * source_ref[x + 1]

    sent = edge_rows(place_ref[1] % 2 == 1, edgea_ref, edgeb_ref, 0)

    def edge(i, x):
        value = sent(i, x)
        if i < FLOWS:
            return value
        at = x if VELOCITY[i][2] == 1 else wide + x
        return value + WEIGHT_HEAT[i - FLOWS] * row_ref[at : at + 1, :]

    for x in range(wide):
        for i in range(FLOWS):
            flow_ref[i, x] = stream(get, edge, deep, i, x)
        for k in range(HEATS):
            heat_ref[k, x] = stream(get, edge, deep, FLOWS + k, x)


def swap(value, axis, offset):
    count = lax.axis_size(axis)
    pairs = []
    for first in range(offset, count + offset, 2):
        one, other = first % count, (first + 1) % count
        pairs += [(one, other), (other, one)]
    return lax.ppermute(value, axis, pairs)


def local(
    populations,
    thermal,
    solid_mask,
    metal_temp,
    conduction,
    wall_count,
    wall_node,
    wall_owner,
    wall_cell,
):
    blocks = lax.axis_size("blk")
    wide, deep, lanes = solid_mask.shape
    place = jnp.stack([lax.axis_index("blk"), lax.axis_index("span")]).astype(jnp.int32)
    smem = pl.BlockSpec(memory_space=pltpu.SMEM)

    def call(kernel, name, outs, scalars, *args):
        return pl.pallas_call(
            kernel,
            in_specs=[smem] + in_vmem(len(args)),
            out_specs=jax.tree.map(lambda _: in_vmem(1)[0], outs),
            out_shape=outs,
            compiler_params=params(),
            name=name,
        )(scalars, *args)

    def to_all(chunks):
        return lax.all_to_all(chunks, "blk", 0, 0, tiled=True)

    chunks, lists, counts = call(
        packet_kernel,
        "wall_packet",
        (shape(blocks, 8, lanes), shape(16, lanes), shape(wide, deep, lanes)),
        wall_count,
        thermal,
        metal_temp,
        wall_node,
        wall_owner.reshape(1, -1),
        wall_cell,
    )
    chunks = to_all(chunks)
    side = shape(SIDE_PLANES, deep, lanes)
    postf, posth, senda, sendb = call(
        collide_kernel,
        "collide_first",
        (shape(FLOWS, wide, deep, lanes), shape(HEATS, wide, deep, lanes), side, side),
        place,
        populations,
        thermal,
        solid_mask,
        counts,
        lists,
    )
    recva = swap(senda, "blk", 0)
    recvb = swap(sendb, "blk", 1)
    edge_count = -(-((wide + 2) * EDGES + 2 + LIST_ROWS) // 8) * 8
    edges = shape(edge_count, lanes)
    senda, sendb, metal, source = call(
        source_kernel,
        "source_first",
        (edges, edges, shape(8, lanes), shape(wide + 4, deep, lanes)),
        place,
        postf,
        posth,
        recva,
        recvb,
        lists,
        chunks,
        conduction,
    )
    edgea = swap(senda, "span", 0)
    edgeb = swap(sendb, "span", 1)
    heat, chunks = call(
        heat_kernel,
        "heat_second",
        (shape(HEATS, wide + 2, deep, lanes), shape(blocks, 8, lanes)),
        place,
        posth,
        recva,
        recvb,
        source,
        edgea,
        edgeb,
        lists,
        metal,
    )
    chunks = to_all(chunks)
    edges = shape(wide * EDGES, lanes)
    postf, posth, senda, sendb = call(
        flow_kernel,
        "collide_second",
        (
            shape(FLOWS, wide + 2, deep, lanes),
            shape(HEATS, wide + 2, deep, lanes),
            edges,
            edges,
        ),
        place,
        postf,
        recva,
        recvb,
        edgea,
        edgeb,
        heat,
        solid_mask,
        counts,
    )
    lasta = swap(senda, "span", 0)
    lastb = swap(sendb, "span", 1)
    source, rows, metal = call(
        last_metal_kernel,
        "source_second",
        (
            shape(wide + 2, deep, lanes),
            shape(2 * wide, lanes),
            shape(1, metal_temp.shape[1]),
        ),
        place,
        recva,
        recvb,
        lists,
        chunks,
        edgea,
        edgeb,
        metal,
        conduction,
    )
    flow, heat = call(
        final_kernel,
        "stream_last",
        (shape(FLOWS, wide, deep, lanes), shape(HEATS, wide, deep, lanes)),
        place,
        postf,
        posth,
        source,
        rows,
        lasta,
        lastb,
    )
    return (flow, heat, metal)


def solution(mesh):
    in_specs = (
        P(None, "blk", "span", None),
        P(None, "blk", "span", None),
        P("blk", "span", None),
        P("span", "blk"),
        P("span", "blk"),
        P("span", "blk"),
        P("span", "blk"),
        P("span", "blk", None),
        P("span", "blk"),
    )
    out_specs = (P(None, "blk", "span", None), P(None, "blk", "span", None), P("span", "blk"))
    return jax.shard_map(local, mesh=mesh, in_specs=in_specs, out_specs=out_specs, check_vma=False)
```

time: 50.2 us -> 40.2 us (0.80)
  blocking collectives: 25.6 us -> 7.2 us
  waiting for transfers between devices: 0.02 us -> 4.38 us
  starting transfers between devices: 9.87 us -> 14.2 us
    all_gather x3 -> x0, blocking collectives: 25.6 us -> none  [the longest x1 9.05 us: local(): metals = lax.all_gather(metal, 'blk')]
    all_to_all x0 -> x1, blocking collectives: none -> 7.2 us  [to_all(): return lax.all_to_all(chunks, 'blk', 0, 0, tiled=True)]
    all_to_all x0 -> x1, starting transfers between devices: none -> 3.34 us  [to_all(): return lax.all_to_all(chunks, 'blk', 0, 0, tiled=True)]
    ppermute x6, waiting for transfers between devices: 0.02 us -> 3.32 us  [swap(): return lax.ppermute(value, axis, pairs)]
    all_to_all x0 -> x1, waiting for transfers between devices: none -> 1.06 us  [to_all(): return lax.all_to_all(chunks, 'blk', 0, 0, tiled=True)]
    ppermute x6, starting transfers between devices: 9.87 us -> 10.8 us  [swap(): return lax.ppermute(value, axis, pairs)]
    unnamed x18 -> x16, local copies, waits for them, and re-layouts: 3.43 us -> 2.93 us
    pallas_call x8 -> x7, Pallas kernels: 9.57 us -> 9.73 us  [call(): pl.pallas_call(kernel, in_specs=[smem] + in_vmem(len(args)), out_specs=ja...]
  transfers between devices with their start and end apart: 6 -> 7, of which waited for: 0 -> 2; matrix products, arithmetic and copies ran while one was open for 0% -> 0% of each run, Pallas kernels for 4% -> 9%
where the time goes in v2:
time: 40.2 us; the launch traced here: 39.8 us
  starting transfers between devices  14.2 us (35%)
  Pallas kernels  9.73 us (24%)
  blocking collectives  7.2 us (18%)
  waiting for transfers between devices  4.38 us (11%)
  local copies, waits for them, and re-layouts  2.93 us (7%)
  between operations  1.36 us (3%)
    ppermute x6, starting transfers between devices, swap(): return lax.ppermute(value, axis, pairs)  10.8 us
    pallas_call x7, Pallas kernels, call(): pl.pallas_call(kernel, in_specs=[smem] + in_vmem(len(args)), out_specs=ja...  9.73 us
    all_to_all x1, blocking collectives, to_all(): return lax.all_to_all(chunks, 'blk', 0, 0, tiled=True)  7.2 us
    all_to_all x1, starting transfers between devices, to_all(): return lax.all_to_all(chunks, 'blk', 0, 0, tiled=True)  3.34 us
    ppermute x6, waiting for transfers between devices, swap(): return lax.ppermute(value, axis, pairs)  3.32 us
    unnamed x16, local copies, waits for them, and re-layouts  2.93 us
    all_to_all x1, waiting for transfers between devices, to_all(): return lax.all_to_all(chunks, 'blk', 0, 0, tiled=True)  1.06 us
  transfers between devices with their start and end apart: 7, of which 2 were waited for; matrix products, arithmetic and copies ran while one was open for 0% of the time, Pallas kernels for 9%

profile of v2, /device:TPU:0, one launch (start us, length us, event | category | flops | bytes accessed | tf_op | source)
XLA Modules:
  0.0 39.8 jit_solution(17545167084218442818)
XLA Ops:
  1.3 0.0 copy-start.6
  1.3 0.0 copy-start.5
  1.3 0.0 copy-start.4
  1.3 0.1 pad_add_fusion.place_ref
  1.4 0.0 copy-start.7
  1.4 0.6 %copy-done.6 = s32[1,512]{1,0:T(1,128)S(1)} copy-done((s32[1,512]{1,0:T(1,128)S(1)}, s32[1,512]{1,0:T(1,128)}, u32[]{:S(2)}) %copy-start.6) | copy-done | bytes 2072
  2.0 0.0 copy-done.5
  2.0 0.0 copy-done.4
  2.0 0.1 copy-done.7
  2.1 0.0 copy-start.1
  2.1 0.9 %copy-done.1 = f32[7,8,8,128]{3,2,1,0:T(8,128)S(1)} copy-done((f32[7,8,8,128]{3,2,1,0:T(8,128)S(1)}, f32[7,8,8,128]{3,2,1,0:T(8,128)}, u32[]{:S(2)}) %copy-start.1) | copy-done | bytes 229400
  3.0 0.0 copy-start.3
  3.0 0.5 %wall_packet.1 = (f32[8,8,128]{2,1,0:T(8,128)S(1)}, f32[16,128]{1,0:T(8,128)S(1)}, f32[8,8,128]{2,1,0:T(8,128)S(1)}) custom-call(s32[1,1]{1,0:T(1,128)S(6)} %copy.12.count_ref, f32[7,8,8,128]{3,2,1,0:T(8,128)S(1)} %copy-done.1, f32[1,256]{1,0:T(1,128)S(1)} %copy-done.7, s32[1,512]{1,0:T(1,128)S(1)} %copy-done.4, s32[1,512]{1,0:T(1,128)S(1)} %bitcast.3, ...), custom_call_target="tpu_custom_call" | custom-call | tf_op jit(solution)/shard_map/wall_packet/pallas_call | solution.py:622
  3.5 0.2 copy-done.3
  3.8 0.0 copy-start.2
  3.8 1.1 %copy-done.2 = f32[19,8,8,128]{3,2,1,0:T(8,128)S(1)} copy-done((f32[19,8,8,128]{3,2,1,0:T(8,128)S(1)}, f32[19,8,8,128]{3,2,1,0:T(8,128)}, u32[]{:S(2)}) %copy-start.2) | copy-done | bytes 622616
  4.8 0.0 copy-start
  4.8 0.9 %collide_first.1 = (f32[19,8,8,128]{3,2,1,0:T(8,128)S(1)}, f32[7,8,8,128]{3,2,1,0:T(8,128)S(1)}, f32[30,8,128]{2,1,0:T(8,128)S(1)}, f32[30,8,128]{2,1,0:T(8,128)S(1)}) custom-call(s32[2]{0:T(128)S(1)} %pad_add_fusion.place_ref, f32[19,8,8,128]{3,2,1,0:T(8,128)S(1)} %copy-done.2, f32[7,8,8,128]{3,2,1,0:T(8,128)S(1)} %copy-done.1, s32[8,8,128]{2,1,0:T(8,128)S(1)} %copy-done.3, ...), custom_call_target="tpu_custom_call" | custom-call | tf_op jit(solution)/shard_map/collide_first/pallas_call | solution.py:622
  5.8 0.5 %collective-permute-start = (f32[30,8,128]{2,1,0:T(8,128)S(1)}, f32[30,8,128]{2,1,0:T(8,128)S(1)}, u32[]{:S(2)}, u32[]{:S(2)}) collective-permute-start(f32[30,8,128]{2,1,0:T(8,128)S(1)} %get-tuple-element.28), channel_id=1, source_target_pairs={{0,1},{1,0},{2,3},{3,2},{4,5},{5,4},{6,7},{7,6},{8,9},{9,8},{10,11... | collective-permute-start | bytes 368648 | tf_op jit(solution)/shard_map/ppermute | solution.py:602
  6.3 3.6 %collective-permute-start.1 = (f32[30,8,128]{2,1,0:T(8,128)S(1)}, f32[30,8,128]{2,1,0:T(8,128)S(1)}, u32[]{:S(2)}, u32[]{:S(2)}) collective-permute-start(f32[30,8,128]{2,1,0:T(8,128)S(1)} %get-tuple-element.29), channel_id=1, source_target_pairs={{1,2},{2,1},{3,4},{4,3},{5,6},{6,5},{7,0},{0,7},{9,10},{10,9},{11,... | collective-permute-start | bytes 368648 | tf_op jit(solution)/shard_map/ppermute | solution.py:602
  9.8 7.2 %all_to_all.10.chunks_ref = f32[8,8,128]{2,1,0:T(8,128)S(1)} all-to-all(f32[8,8,128]{2,1,0:T(8,128)S(1)} %get-tuple-element.31), channel_id=1, replica_groups=mesh['span'=4,'blk'=8] {'blk'}, dimensions={0} | all-to-all | bytes 65536 | tf_op jit(solution)/shard_map/all_to_all | solution.py:632
  17.0 0.0 collective-permute-done.recva_ref
  17.0 0.0 collective-permute-done.1.recvb_ref
  17.0 0.0 copy-done
  17.1 1.5 %source_first.1 = (f32[80,128]{1,0:T(8,128)S(1)}, f32[80,128]{1,0:T(8,128)S(1)}, f32[8,128]{1,0:T(8,128)S(1)}, f32[12,8,128]{2,1,0:T(8,128)S(1)}) custom-call(s32[2]{0:T(128)S(1)} %pad_add_fusion.place_ref, f32[19,8,8,128]{3,2,1,0:T(8,128)S(1)} %get-tuple-element.27.postf_ref, f32[7,8,8,128]{3,2,1,0:T(8,128)S(1)} %get-tuple-element.30.posth_ref, ...), custom_call_target="tpu_custom_call" | custom-call | tf_op jit(solution)/shard_map/source_first/pallas_call | solution.py:622
  18.5 1.6 %collective-permute-start.2 = (f32[80,128]{1,0:T(8,128)S(1)}, f32[80,128]{1,0:T(8,128)S(1)}, u32[]{:S(2)}, u32[]{:S(2)}) collective-permute-start(f32[80,128]{1,0:T(8,128)S(1)} %get-tuple-element.32), channel_id=1, source_target_pairs={{0,8},{8,0},{16,24},{24,16},{1,9},{9,1},{17,25},{25,17},{2,10},{10... | collective-permute-start | bytes 122888 | tf_op jit(solution)/shard_map/ppermute | solution.py:602
  20.2 2.5 %collective-permute-start.3 = (f32[80,128]{1,0:T(8,128)S(1)}, f32[80,128]{1,0:T(8,128)S(1)}, u32[]{:S(2)}, u32[]{:S(2)}) collective-permute-start(f32[80,128]{1,0:T(8,128)S(1)} %get-tuple-element.33), channel_id=1, source_target_pairs={{8,16},{16,8},{24,0},{0,24},{9,17},{17,9},{25,1},{1,25},{10,18},{1... | collective-permute-start | bytes 122888 | tf_op jit(solution)/shard_map/ppermute | solution.py:602
  22.6 0.0 collective-permute-done.2.edgea_ref
  22.6 3.3 %collective-permute-done.3.edgeb_ref = f32[80,128]{1,0:T(8,128)S(1)} collective-permute-done((f32[80,128]{1,0:T(8,128)S(1)}, f32[80,128]{1,0:T(8,128)S(1)}, u32[]{:S(2)}, u32[]{:S(2)}) %collective-permute-start.3) | collective-permute-done | bytes 40992 | tf_op jit(solution)/shard_map/ppermute | solution.py:602
  26.0 1.7 %heat_second.1 = (f32[7,10,8,128]{3,2,1,0:T(8,128)S(1)}, f32[8,8,128]{2,1,0:T(8,128)}) custom-call(s32[2]{0:T(128)S(1)} %pad_add_fusion.place_ref, f32[7,8,8,128]{3,2,1,0:T(8,128)S(1)} %get-tuple-element.30.posth_ref, f32[30,8,128]{2,1,0:T(8,128)S(1)} %collective-permute-done.recva_ref, f32[30,8,128]{2,1,0:T(8,128)S(1)} %collective-permute-done.1.recvb_ref, ...), custom_call_target="tpu_custom_call" | custom-call | tf_op jit(solution)/shard_map/heat_second/pallas_call | solution.py:622
  27.6 3.3 %all-to-all-start.1 = ((f32[8,8,128]{2,1,0:T(8,128)}), f32[8,8,128]{2,1,0:T(8,128)S(1)}, u32[]{:S(2)}, u32[]{:S(2)}) async-start(f32[8,8,128]{2,1,0:T(8,128)} %get-tuple-element.39), calls=%async_computation.1 | async-start | bytes 65536 | tf_op jit(solution)/shard_map/all_to_all | solution.py:632
  31.0 1.1 %collide_second.1 = (f32[19,10,8,128]{3,2,1,0:T(8,128)S(1)}, f32[7,10,8,128]{3,2,1,0:T(8,128)S(1)}, f32[48,128]{1,0:T(8,128)S(1)}, f32[48,128]{1,0:T(8,128)S(1)}) custom-call(s32[2]{0:T(128)S(1)} %pad_add_fusion.place_ref, f32[19,8,8,128]{3,2,1,0:T(8,128)S(1)} %get-tuple-element.27.postf_ref, f32[30,8,128]{2,1,0:T(8,128)S(1)} %collective-permute-done.recva_ref, ...), custom_call_target="tpu_custom_call" | custom-call | tf_op jit(solution)/shard_map/collide_second/pallas_call | solution.py:622
  32.1 0.1 collective-permute-start.4
  32.1 2.6 %collective-permute-start.5 = (f32[48,128]{1,0:T(8,128)S(1)}, f32[48,128]{1,0:T(8,128)S(1)}, u32[]{:S(2)}, u32[]{:S(2)}) collective-permute-start(f32[48,128]{1,0:T(8,128)S(1)} %get-tuple-element.43), channel_id=1, source_target_pairs={{8,16},{16,8},{24,0},{0,24},{9,17},{17,9},{25,1},{1,25},{10,18},{1... | collective-permute-start | bytes 73736 | tf_op jit(solution)/shard_map/ppermute | solution.py:602
  34.7 1.1 %all-to-all-done.1.chunks_ref = f32[8,8,128]{2,1,0:T(8,128)S(1)} async-done(((f32[8,8,128]{2,1,0:T(8,128)}), f32[8,8,128]{2,1,0:T(8,128)S(1)}, u32[]{:S(2)}, u32[]{:S(2)}) %all-to-all-start.1) | async-done | bytes 32800 | tf_op jit(solution)/shard_map/all_to_all | solution.py:632
  35.8 2.5 %source_second.1 = (f32[10,8,128]{2,1,0:T(8,128)S(1)}, f32[16,128]{1,0:T(8,128)S(1)}, f32[1,256]{1,0:T(1,128)}) custom-call(s32[2]{0:T(128)S(1)} %pad_add_fusion.place_ref, f32[30,8,128]{2,1,0:T(8,128)S(1)} %collective-permute-done.recva_ref, f32[30,8,128]{2,1,0:T(8,128)S(1)} %collective-permute-done.1.recvb_ref, f32[16,128]{1,0:T(8,128)S(1)} %get-tuple-element.26.list_ref, ...), custom_call_target="tpu_custom_call" | custom-call | tf_op jit(solution)/shard_map/source_second/pallas_call | solution.py:622
  38.2 0.0 collective-permute-done.4.edgea_ref
  38.2 0.0 collective-permute-done.5.edgeb_ref
  38.2 1.6 %stream_last.1 = (f32[19,8,8,128]{3,2,1,0:T(8,128)}, f32[7,8,8,128]{3,2,1,0:T(8,128)}) custom-call(s32[2]{0:T(128)S(1)} %pad_add_fusion.place_ref, f32[19,10,8,128]{3,2,1,0:T(8,128)S(1)} %get-tuple-element.37.postf_ref, f32[7,10,8,128]{3,2,1,0:T(8,128)S(1)} %get-tuple-element.38.posth_ref, f32[10,8,128]{2,1,0:T(8,128)S(1)} %get-tuple-element.40.source_ref, ...), custom_call_target="tpu_custom_call" | custom-call | tf_op jit(solution)/shard_map/stream_last/pallas_call | solution.py:622
Async XLA Ops:
  1.3 0.7 %copy-start.6 = (s32[1,512]{1,0:T(1,128)S(1)}, s32[1,512]{1,0:T(1,128)}, u32[]{:S(2)}) copy-start(s32[1,512]{1,0:T(1,128)} %cell_ref.1) | copy-start | bytes 6148
  1.3 0.7 %copy-start.5 = (s32[1,512,1]{1,2,0:T(1,128)S(1)}, s32[1,512,1]{1,2,0:T(1,128)}, u32[]{:S(2)}) copy-start(s32[1,512,1]{1,2,0:T(1,128)} %param.16) | copy-start | bytes 6148
  1.3 0.7 %copy-start.4 = (s32[1,512]{1,0:T(1,128)S(1)}, s32[1,512]{1,0:T(1,128)}, u32[]{:S(2)}) copy-start(s32[1,512]{1,0:T(1,128)} %node_ref.1) | copy-start | bytes 6148
  1.4 0.7 %copy-start.7 = (f32[1,256]{1,0:T(1,128)S(1)}, f32[1,256]{1,0:T(1,128)}, u32[]{:S(2)}) copy-start(f32[1,256]{1,0:T(1,128)} %metal_ref.1) | copy-start | bytes 3076
  2.1 0.9 %copy-start.1 = (f32[7,8,8,128]{3,2,1,0:T(8,128)S(1)}, f32[7,8,8,128]{3,2,1,0:T(8,128)}, u32[]{:S(2)}) copy-start(f32[7,8,8,128]{3,2,1,0:T(8,128)} %heat_ref.3) | copy-start | bytes 688132
  3.0 0.8 %copy-start.3 = (s32[8,8,128]{2,1,0:T(8,128)S(1)}, s32[8,8,128]{2,1,0:T(8,128)}, u32[]{:S(2)}) copy-start(s32[8,8,128]{2,1,0:T(8,128)} %solid_ref.3) | copy-start | bytes 98308
  3.8 1.1 %copy-start.2 = (f32[19,8,8,128]{3,2,1,0:T(8,128)S(1)}, f32[19,8,8,128]{3,2,1,0:T(8,128)}, u32[]{:S(2)}) copy-start(f32[19,8,8,128]{3,2,1,0:T(8,128)} %flow_ref.1) | copy-start | bytes 1867780
  4.8 12.2 %copy-start = (f32[256,256]{1,0:T(8,128)S(1)}, f32[256,256]{1,0:T(8,128)}, u32[]{:S(2)}) copy-start(f32[256,256]{1,0:T(8,128)} %conduction_ref.3) | copy-start | bytes 786436
  5.8 11.3 %collective-permute-start = (f32[30,8,128]{2,1,0:T(8,128)S(1)}, f32[30,8,128]{2,1,0:T(8,128)S(1)}, u32[]{:S(2)}, u32[]{:S(2)}) collective-permute-start(f32[30,8,128]{2,1,0:T(8,128)S(1)} %get-tuple-element.28), channel_id=1, source_target_pairs={{0,1},{1,0},{2,3},{3,2},{4,5},{5,4},{6,7},{7,6},{8,9},{9,8},{10,11... | collective-permute-start | bytes 368648 | tf_op jit(solution)/shard_map/ppermute | solution.py:602
  6.3 10.8 %collective-permute-start.1 = (f32[30,8,128]{2,1,0:T(8,128)S(1)}, f32[30,8,128]{2,1,0:T(8,128)S(1)}, u32[]{:S(2)}, u32[]{:S(2)}) collective-permute-start(f32[30,8,128]{2,1,0:T(8,128)S(1)} %get-tuple-element.29), channel_id=1, source_target_pairs={{1,2},{2,1},{3,4},{4,3},{5,6},{6,5},{7,0},{0,7},{9,10},{10,9},{11,... | collective-permute-start | bytes 368648 | tf_op jit(solution)/shard_map/ppermute | solution.py:602
  18.5 4.1 %collective-permute-start.2 = (f32[80,128]{1,0:T(8,128)S(1)}, f32[80,128]{1,0:T(8,128)S(1)}, u32[]{:S(2)}, u32[]{:S(2)}) collective-permute-start(f32[80,128]{1,0:T(8,128)S(1)} %get-tuple-element.32), channel_id=1, source_target_pairs={{0,8},{8,0},{16,24},{24,16},{1,9},{9,1},{17,25},{25,17},{2,10},{10... | collective-permute-start | bytes 122888 | tf_op jit(solution)/shard_map/ppermute | solution.py:602
  20.2 5.8 %collective-permute-start.3 = (f32[80,128]{1,0:T(8,128)S(1)}, f32[80,128]{1,0:T(8,128)S(1)}, u32[]{:S(2)}, u32[]{:S(2)}) collective-permute-start(f32[80,128]{1,0:T(8,128)S(1)} %get-tuple-element.33), channel_id=1, source_target_pairs={{8,16},{16,8},{24,0},{0,24},{9,17},{17,9},{25,1},{1,25},{10,18},{1... | collective-permute-start | bytes 122888 | tf_op jit(solution)/shard_map/ppermute | solution.py:602
  27.6 8.1 %all-to-all-start.1 = ((f32[8,8,128]{2,1,0:T(8,128)}), f32[8,8,128]{2,1,0:T(8,128)S(1)}, u32[]{:S(2)}, u32[]{:S(2)}) async-start(f32[8,8,128]{2,1,0:T(8,128)} %get-tuple-element.39), calls=%async_computation.1 | async-start | bytes 65536 | tf_op jit(solution)/shard_map/all_to_all | solution.py:632
  32.1 6.2 %collective-permute-start.4 = (f32[48,128]{1,0:T(8,128)S(1)}, f32[48,128]{1,0:T(8,128)S(1)}, u32[]{:S(2)}, u32[]{:S(2)}) collective-permute-start(f32[48,128]{1,0:T(8,128)S(1)} %get-tuple-element.42), channel_id=1, source_target_pairs={{0,8},{8,0},{16,24},{24,16},{1,9},{9,1},{17,25},{25,17},{2,10},{10... | collective-permute-start | bytes 73736 | tf_op jit(solution)/shard_map/ppermute | solution.py:602
  32.1 6.1 %collective-permute-start.5 = (f32[48,128]{1,0:T(8,128)S(1)}, f32[48,128]{1,0:T(8,128)S(1)}, u32[]{:S(2)}, u32[]{:S(2)}) collective-permute-start(f32[48,128]{1,0:T(8,128)S(1)} %get-tuple-element.43), channel_id=1, source_target_pairs={{8,16},{16,8},{24,0},{0,24},{9,17},{17,9},{25,1},{1,25},{10,18},{1... | collective-permute-start | bytes 73736 | tf_op jit(solution)/shard_map/ppermute | solution.py:602

commit v3 on v2

--- a/solution.py
+++ b/solution.py
@@ -70,6 +70,12 @@
 
 def split(value):
     high = value.astype(BF16)
+    low = (value - high.astype(F32)).astype(BF16)
+    return high, low
+
+
+def split_three(value):
+    high = value.astype(BF16)
     rest = value - high.astype(F32)
     middle = rest.astype(BF16)
     low = (rest - middle.astype(F32)).astype(BF16)
@@ -88,10 +94,19 @@
     return jnp.where(mask, 1.0, 0.0).astype(BF16)
 
 
-def look_up(table, row_hot, lane_mask):
-    turned = jnp.transpose(table)
-    found = sum([dot(part, row_hot, ((1,), (0,))) for part in split(turned)])
-    return jnp.sum(jnp.where(lane_mask, found, 0.0), axis=0, keepdims=True)
+def pick(rows, row_index, lane_index):
+    found = jnp.zeros(lane_index.shape, F32)
+    for r, row in enumerate(rows):
+        whole = jnp.broadcast_to(row, lane_index.shape)
+        value = jnp.take_along_axis(whole, lane_index, axis=1, mode="promise_in_bounds")
+        found = jnp.where(row_index == r, value, found)
+    return found
+
+
+def pick_twice(rows, row_index, lane_index):
+    first, second = (row_index, lane_index) if len(row_index) == 2 else (row_index * 2, lane_index * 2)
+    found = pick(rows, jnp.concatenate(first, axis=0), jnp.concatenate(second, axis=0))
+    return [found[4 * n : 4 * n + 4] for n in range(len(row_index))]
 
 
 def add_up(values, row_mask, lane_hot):
@@ -100,7 +115,7 @@
         [jnp.where(row_mask, part.astype(F32), 0.0) for part in split(values)], axis=0
     ).astype(BF16)
     sums = dot(stacked, lane_hot, ((1,), (1,)))
-    return sums[:count] + sums[count : 2 * count] + sums[2 * count :]
+    return sums[:count] + sums[count:]
 
 
 def one_row(block):
@@ -113,18 +128,25 @@
 
 
 def lists_of(block):
-    return [one_row(block[4 * n : 4 * n + 4]).astype(jnp.int32) for n in range(3)]
-
-
-def packet_kernel(
+    return [block[4 * n : 4 * n + 4].astype(jnp.int32) for n in range(3)]
+
+
+def wall_temper(tempers, node):
+    rows = [temper[z : z + 1] for temper in tempers for z in range(temper.shape[0])]
+    return pick_twice(rows, [node >> 7], [node & 127])[0]
+
+
+def pack(
     count_ref, heat_ref, metal_ref, node_ref, owner_ref, cell_ref, out_ref, list_ref, counts_ref
 ):
     blocks = out_ref.shape[0]
     wide, deep, lanes = heat_ref.shape[1:]
-    temper = heat_ref[0]
-    for k in range(1, HEATS):
-        temper = temper + heat_ref[k]
-    temper = temper.reshape(wide * deep, lanes)
+    tempers = []
+    for x in range(wide):
+        temper = heat_ref[0, x]
+        for k in range(1, HEATS):
+            temper = temper + heat_ref[k, x]
+        tempers.append(temper)
     node = node_ref[...]
     cell = cell_ref[...]
     entries = node.shape[1]
@@ -135,9 +157,9 @@
     put_rows(list_ref, 4, cell.astype(F32))
     put_rows(list_ref, 8, node.astype(F32))
     put_rows(list_ref, LIST_ROWS, metal_ref[...])
-    column_hot = hot(rows_of(node >> 7, wide * deep))
     lane_mask = rows_of(node & 127, lanes)
-    wall = look_up(temper, column_hot, lane_mask)
+    nodes = list_ref[8:12].astype(jnp.int32)
+    wall = one_row(wall_temper(tempers, nodes))
     cell_hot = hot(rows_of(cell & 127, lanes))
     row_mask = rows_of(owner * 2 + (cell >> 7), 2 * blocks)
     sums = add_up(wall, row_mask, cell_hot)
@@ -210,24 +232,82 @@
     return [post[k] + WEIGHT_HEAT[k] * lost for k in range(HEATS)]
 
 
-def collide_kernel(
+STRIPS = 4
+
+
+def first_kernel(
     place_ref,
-    flow_ref,
-    heat_ref,
+    count_ref,
+    flow_hbm,
+    heat_hbm,
+    solid_hbm,
+    metal_hbm,
+    node_hbm,
+    owner_hbm,
+    cell_hbm,
+    chunks_ref,
+    list_ref,
+    counts_ref,
     solid_ref,
-    counts_ref,
-    list_ref,
     postf_ref,
     posth_ref,
     senda_ref,
     sendb_ref,
+    flow_ref,
+    heat_ref,
+    mask_ref,
+    metal_ref,
+    node_ref,
+    owner_ref,
+    cell_ref,
+    sems,
 ):
     wide = flow_ref.shape[1]
+    strip = wide // STRIPS
     odd = place_ref[0] % 2 == 1
+    small = [
+        pltpu.make_async_copy(source, target, sems.at[n])
+        for n, (source, target) in enumerate(
+            (
+                (heat_hbm, heat_ref),
+                (node_hbm, node_ref),
+                (owner_hbm, owner_ref),
+                (cell_hbm, cell_ref),
+                (metal_hbm, metal_ref),
+                (solid_hbm, mask_ref),
+            )
+        )
+    ]
+    strips = [
+        pltpu.make_async_copy(
+            flow_hbm.at[:, pl.ds(n * strip, strip)],
+            flow_ref.at[:, pl.ds(n * strip, strip)],
+            sems.at[len(small) + n],
+        )
+        for n in range(STRIPS)
+    ]
+    for copy in small + strips:
+        copy.start()
+    for copy in small:
+        copy.wait()
+    pack(
+        count_ref,
+        heat_ref,
+        metal_ref,
+        node_ref,
+        owner_ref,
+        cell_ref,
+        chunks_ref,
+        list_ref,
+        counts_ref,
+    )
+    solid_ref[...] = mask_ref[...].astype(F32)
     for x in range(wide):
+        if x % strip == 0:
+            strips[x // strip].wait()
         flow = [flow_ref[i, x] for i in range(FLOWS)]
         heat = [heat_ref[k, x] for k in range(HEATS)]
-        solid = solid_ref[x] != 0
+        solid = mask_ref[x] != 0
         temper = heat[0]
         for k in range(1, HEATS):
             temper = temper + heat[k]
@@ -245,7 +325,7 @@
         for ref, faces, edge in ((right_ref, FACE_RIGHT, wide - 1), (left_ref, FACE_LEFT, 0)):
             for n, (i, depth) in enumerate(faces):
                 ref[n] = plane(i, abs(edge - depth))
-            ref[SOLID] = solid_ref[edge].astype(F32)
+            ref[SOLID] = solid_ref[edge]
             ref[COUNTS] = counts_ref[edge]
             ref[LISTS] = list_ref[0:8]
             ref[LISTS + 1] = list_ref[8:16]
@@ -290,38 +370,41 @@
     return get
 
 
-def metal_at(table, lists, shift=0):
-    owner, cell, node = lists
-    row = jnp.where(owner < 0, -1, owner * 8 + (cell >> 7) + shift)
-    return look_up(table, hot(rows_of(row, table.shape[0])), rows_of(cell & 127, LANES))
+def metal_rows(chunks_ref, shift):
+    blocks = chunks_ref.shape[0]
+    return [chunks_ref[d, shift + h : shift + h + 1] for d in range(blocks) for h in range(2)]
+
+
+def metal_at(rows, *lists):
+    return pick_twice(
+        rows,
+        [owner * 2 + (cell >> 7) for owner, cell, node in lists],
+        [cell & 127 for owner, cell, node in lists],
+    )
 
 
 def give(metal, row, node, count):
-    return add_up(WALL_COEFF * metal, rows_of(row, count), hot(rows_of(node & 127, LANES)))
-
-
-def join(lists):
-    return [jnp.concatenate([item[n] for item in lists], axis=1) for n in range(3)]
-
-
-def give_planes(table, lists, parts, deep, source_ref):
-    metal = metal_at(table, join(lists))
-    entries = lists[0][0].shape[1]
-    for n, (first, count, start) in enumerate(parts):
-        node = lists[n][2]
-        source = give(metal[:, n * entries : (n + 1) * entries], (node >> 7) - first, node, count)
-        source_ref[start : start + count // deep] = source.reshape(count // deep, deep, LANES)
+    return add_up(
+        WALL_COEFF * one_row(metal),
+        rows_of(one_row(row), count),
+        hot(rows_of(one_row(node) & 127, LANES)),
+    )
+
+
+def give_planes(metal, node, first, planes, deep):
+    count = planes * deep
+    return give(metal, (node >> 7) - first * deep, node, count).reshape(planes, deep, LANES)
 
 
 def conduct(conduction, halves):
     vector = jnp.concatenate(halves, axis=1)
-    parts = split(vector)
+    parts = split_three(vector)
     rows = lax.broadcasted_iota(jnp.int32, (16, vector.shape[1]), 0)
     stacked = jnp.zeros((16, vector.shape[1]), F32)
     for r, part in enumerate(parts):
         stacked = jnp.where(rows == r, part.astype(F32), stacked)
     stacked = stacked.astype(BF16)
-    out = sum([dot(stacked, part, ((1,), (1,))) for part in split(conduction)])
+    out = sum([dot(stacked, part, ((1,), (1,))) for part in split_three(conduction)])
     return out[0:1] + out[1:2] + out[2:3]
 
 
@@ -329,6 +412,22 @@
     gained = WALL_COEFF * (total - count * metal)
     value = metal + METAL_GAIN * gained
     return conduct(conduction, [value[0:1], value[1:2]])
+
+
+def metal_kernel(list_ref, chunks_ref, conduction_ref, metal_ref, source_ref):
+    blocks = chunks_ref.shape[0]
+    wide, deep, lanes = source_ref.shape
+    lists = lists_of(list_ref[...])
+    found = metal_at(metal_rows(chunks_ref, 0), lists)[0]
+    source_ref[...] = give_planes(found, lists[2], 0, wide, deep)
+    sums = chunks_ref[0]
+    for d in range(1, blocks):
+        sums = sums + chunks_ref[d]
+    count = sums[4:6]
+    metal = next_metal(conduction_ref[...], list_ref[LIST_ROWS : LIST_ROWS + 2], sums[2:4], count)
+    metal_ref[...] = jnp.zeros(metal_ref.shape, F32)
+    put_rows(metal_ref, 0, metal)
+    metal_ref[2:4, :] = count
 
 
 def source_kernel(
@@ -339,33 +438,20 @@
     recvb_ref,
     list_ref,
     chunks_ref,
-    conduction_ref,
+    metal_ref,
+    own_ref,
     senda_ref,
     sendb_ref,
-    metal_ref,
     source_ref,
 ):
     wide, deep, lanes = postf_ref.shape[1:]
-    blocks = chunks_ref.shape[0]
     low, high = sides(place_ref[0] % 2 == 1, recva_ref, recvb_ref)
-    table = chunks_ref[...].reshape(blocks * 8, lanes)
-    columns = wide * deep
-    give_planes(
-        table,
-        [side_lists(low), lists_of(list_ref[...]), side_lists(high)],
-        ((columns - 2 * deep, 2 * deep, 0), (0, columns, 2), (0, 2 * deep, wide + 2)),
-        deep,
-        source_ref,
-    )
+    before, after = side_lists(low), side_lists(high)
+    found = metal_at(metal_rows(chunks_ref, 0), before, after)
+    source_ref[0:2] = give_planes(found[0], before[2], wide - 2, 2, deep)
+    source_ref[2 : wide + 2] = own_ref[...]
+    source_ref[wide + 2 :] = give_planes(found[1], after[2], 0, 2, deep)
     get = planes(postf_ref, posth_ref, low, high, wide, source_ref)
-    sums = chunks_ref[0]
-    for d in range(1, blocks):
-        sums = sums + chunks_ref[d]
-    count = sums[4:6]
-    metal = next_metal(conduction_ref[...], list_ref[LIST_ROWS : LIST_ROWS + 2], sums[2:4], count)
-    metal_ref[...] = jnp.zeros(metal_ref.shape, F32)
-    put_rows(metal_ref, 0, metal)
-    metal_ref[2:4, :] = count
 
     def fill(up_ref, down_ref):
         for ref, comps, row in ((up_ref, UP, deep - 1), (down_ref, DOWN, 0)):
@@ -375,7 +461,7 @@
                     at = j * EDGES + n
                     ref[at : at + 1, :] = value[row : row + 1, :]
             at = (wide + 2) * EDGES
-            put_rows(ref, at, metal)
+            ref[at : at + 2, :] = metal_ref[0:2]
             ref[at + 2 : at + 2 + LIST_ROWS, :] = list_ref[0:LIST_ROWS]
 
     for ref in (senda_ref, sendb_ref):
@@ -445,13 +531,9 @@
             temper = value if temper is None else temper + value
         if 0 <= x < wide:
             tempers.append(temper)
-    columns = wide * deep
     owner, cell, node = lists_of(list_ref[...])
-    wall = look_up(
-        jnp.concatenate(tempers, axis=0),
-        hot(rows_of(node >> 7, columns)),
-        rows_of(node & 127, lanes),
-    )
+    wall = one_row(wall_temper(tempers, node))
+    owner, cell = one_row(owner), one_row(cell)
     row_mask = rows_of(owner * 2 + (cell >> 7), 2 * blocks)
     sums = add_up(wall, row_mask, hot(rows_of(cell & 127, lanes)))
     at = (wide + 2) * EDGES
@@ -538,15 +620,12 @@
     wide, deep, lanes = source_ref.shape
     wide = wide - 2
     low, high = sides(place_ref[0] % 2 == 1, recva_ref, recvb_ref)
-    table = chunks_ref[...].reshape(blocks * 8, lanes)
-    columns = wide * deep
-    give_planes(
-        table,
-        [side_lists(low), lists_of(list_ref[...]), side_lists(high)],
-        ((columns - deep, deep, 0), (0, columns, 1), (0, deep, wide + 1)),
-        deep,
-        source_ref,
-    )
+    own, before, after = lists_of(list_ref[...]), side_lists(low), side_lists(high)
+    found = metal_at(metal_rows(chunks_ref, 0), own)[0]
+    source_ref[1 : wide + 1] = give_planes(found, own[2], 0, wide, deep)
+    found = metal_at(metal_rows(chunks_ref, 0), before, after)
+    source_ref[0:1] = give_planes(found[0], before[2], wide - 1, 1, deep)
+    source_ref[wide + 1 :] = give_planes(found[1], after[2], 0, 1, deep)
     odd = place_ref[1] % 2 == 1
     at = (wide + 2) * EDGES + 2
     a = edgea_ref[at : at + LIST_ROWS, :]
@@ -558,9 +637,8 @@
         node = lists[2]
         column = node >> 7
         row = jnp.where(lax.rem(column, deep) == z, lax.div(column, deep), -1)
-        row_ref[wide * n : wide * (n + 1), :] = give(
-            metal_at(table, lists, shift), row, node, wide
-        )
+        found = metal_at(metal_rows(chunks_ref, shift), lists)[0]
+        row_ref[wide * n : wide * (n + 1), :] = give(found, row, node, wide)
     sums = chunks_ref[0]
     for d in range(1, blocks):
         sums = sums + chunks_ref[d]
@@ -568,9 +646,23 @@
 
 
 def final_kernel(
-    place_ref, postf_ref, posth_ref, source_ref, row_ref, edgea_ref, edgeb_ref, flow_ref, heat_ref
+    place_ref,
+    postf_ref,
+    posth_ref,
+    source_ref,
+    row_ref,
+    metal_ref,
+    edgea_ref,
+    edgeb_ref,
+    flow_hbm,
+    heat_hbm,
+    metal_hbm,
+    flow_ref,
+    heat_ref,
+    sems,
 ):
     wide, deep, lanes = flow_ref.shape[1:]
+    strip = wide // STRIPS
 
     def get(i, x):
         if i < FLOWS:
@@ -586,11 +678,23 @@
         at = x if VELOCITY[i][2] == 1 else wide + x
         return value + WEIGHT_HEAT[i - FLOWS] * row_ref[at : at + 1, :]
 
-    for x in range(wide):
-        for i in range(FLOWS):
-            flow_ref[i, x] = stream(get, edge, deep, i, x)
-        for k in range(HEATS):
-            heat_ref[k, x] = stream(get, edge, deep, FLOWS + k, x)
+    copies = [pltpu.make_async_copy(metal_ref, metal_hbm, sems.at[2 * STRIPS])]
+    copies[0].start()
+    for n in range(STRIPS):
+        for x in range(n * strip, (n + 1) * strip):
+            for i in range(FLOWS):
+                flow_ref[i, x] = stream(get, edge, deep, i, x)
+            for k in range(HEATS):
+                heat_ref[k, x] = stream(get, edge, deep, FLOWS + k, x)
+        part = pl.ds(n * strip, strip)
+        for m, (source, target) in enumerate(((flow_ref, flow_hbm), (heat_ref, heat_hbm))):
+            copy = pltpu.make_async_copy(
+                source.at[:, part], target.at[:, part], sems.at[2 * n + m]
+            )
+            copy.start()
+            copies.append(copy)
+    for copy in copies:
+        copy.wait()
 
 
 def swap(value, axis, offset):
@@ -617,60 +721,79 @@
     wide, deep, lanes = solid_mask.shape
     place = jnp.stack([lax.axis_index("blk"), lax.axis_index("span")]).astype(jnp.int32)
     smem = pl.BlockSpec(memory_space=pltpu.SMEM)
-
-    def call(kernel, name, outs, scalars, *args):
+    hbm = pl.BlockSpec(memory_space=pltpu.HBM)
+
+    def call(kernel, name, outs, scalars, *args, far=0, scratch=(), out_spec=None):
+        near = len(args) - far
+        held = [pltpu.with_memory_space_constraint(arg, pltpu.HBM) for arg in args[near:]]
+        out_spec = out_spec or in_vmem(1)[0]
         return pl.pallas_call(
             kernel,
-            in_specs=[smem] + in_vmem(len(args)),
-            out_specs=jax.tree.map(lambda _: in_vmem(1)[0], outs),
+            in_specs=[smem] * len(scalars) + in_vmem(near) + [hbm] * far,
+            out_specs=jax.tree.map(lambda _: out_spec, outs),
             out_shape=outs,
+            scratch_shapes=scratch,
             compiler_params=params(),
             name=name,
-        )(scalars, *args)
+        )(*scalars, *args[:near], *held)
 
     def to_all(chunks):
         return lax.all_to_all(chunks, "blk", 0, 0, tiled=True)
 
-    chunks, lists, counts = call(
-        packet_kernel,
-        "wall_packet",
-        (shape(blocks, 8, lanes), shape(16, lanes), shape(wide, deep, lanes)),
-        wall_count,
+    side = shape(SIDE_PLANES, deep, lanes)
+    field = shape(wide, deep, lanes)
+    flows, heats = shape(FLOWS, wide, deep, lanes), shape(HEATS, wide, deep, lanes)
+    chunks, lists, counts, solid, postf, posth, senda, sendb = call(
+        first_kernel,
+        "collide_first",
+        (shape(blocks, 8, lanes), shape(16, lanes), field, field, flows, heats, side, side),
+        (place, wall_count),
+        populations,
         thermal,
+        solid_mask,
         metal_temp,
         wall_node,
         wall_owner.reshape(1, -1),
         wall_cell,
+        far=7,
+        scratch=[
+            pltpu.VMEM(flows.shape, F32),
+            pltpu.VMEM(heats.shape, F32),
+            pltpu.VMEM(field.shape, jnp.int32),
+            pltpu.VMEM(metal_temp.shape, F32),
+            pltpu.VMEM(wall_node.shape, jnp.int32),
+            pltpu.VMEM(wall_node.shape, jnp.int32),
+            pltpu.VMEM(wall_node.shape, jnp.int32),
+            pltpu.SemaphoreType.DMA((6 + STRIPS,)),
+        ],
     )
     chunks = to_all(chunks)
-    side = shape(SIDE_PLANES, deep, lanes)
-    postf, posth, senda, sendb = call(
-        collide_kernel,
-        "collide_first",
-        (shape(FLOWS, wide, deep, lanes), shape(HEATS, wide, deep, lanes), side, side),
-        place,
-        populations,
-        thermal,
-        solid_mask,
-        counts,
-        lists,
-    )
     recva = swap(senda, "blk", 0)
     recvb = swap(sendb, "blk", 1)
     edge_count = -(-((wide + 2) * EDGES + 2 + LIST_ROWS) // 8) * 8
     edges = shape(edge_count, lanes)
-    senda, sendb, metal, source = call(
+    metal, own = call(
+        metal_kernel,
+        "metal_first",
+        (shape(8, lanes), shape(wide, deep, lanes)),
+        (),
+        lists,
+        chunks,
+        conduction,
+    )
+    senda, sendb, source = call(
         source_kernel,
         "source_first",
-        (edges, edges, shape(8, lanes), shape(wide + 4, deep, lanes)),
-        place,
+        (edges, edges, shape(wide + 4, deep, lanes)),
+        (place,),
         postf,
         posth,
         recva,
         recvb,
         lists,
         chunks,
-        conduction,
+        metal,
+        own,
     )
     edgea = swap(senda, "span", 0)
     edgeb = swap(sendb, "span", 1)
@@ -678,7 +801,7 @@
         heat_kernel,
         "heat_second",
         (shape(HEATS, wide + 2, deep, lanes), shape(blocks, 8, lanes)),
-        place,
+        (place,),
         posth,
         recva,
         recvb,
@@ -699,14 +822,14 @@
             edges,
             edges,
         ),
-        place,
+        (place,),
         postf,
         recva,
         recvb,
         edgea,
         edgeb,
         heat,
-        solid_mask,
+        solid,
         counts,
     )
     lasta = swap(senda, "span", 0)
@@ -719,7 +842,7 @@
             shape(2 * wide, lanes),
             shape(1, metal_temp.shape[1]),
         ),
-        place,
+        (place,),
         recva,
         recvb,
         lists,
@@ -729,19 +852,25 @@
         metal,
         conduction,
     )
-    flow, heat = call(
+    return call(
         final_kernel,
         "stream_last",
-        (shape(FLOWS, wide, deep, lanes), shape(HEATS, wide, deep, lanes)),
-        place,
+        (flows, heats, shape(*metal_temp.shape)),
+        (place,),
         postf,
         posth,
         source,
         rows,
+        metal,
         lasta,
         lastb,
-    )
-    return (flow, heat, metal)
+        scratch=[
+            pltpu.VMEM(flows.shape, F32),
+            pltpu.VMEM(heats.shape, F32),
+            pltpu.SemaphoreType.DMA((2 * STRIPS + 1,)),
+        ],
+        out_spec=hbm,
+    )
 
 
 def solution(mesh):

time: 40.2 us -> 37.2 us (0.925)
  local copies, waits for them, and re-layouts: 2.93 us -> 0.01 us
  Pallas kernels: 9.73 us -> 8.65 us
  waiting for transfers between devices: 4.38 us -> 5.45 us
    unnamed x16 -> x2, local copies, waits for them, and re-layouts: 2.93 us -> 0.01 us
    pallas_call x7, Pallas kernels: 9.73 us -> 8.65 us  [call(): pl.pallas_call(kernel, in_specs=[smem] * len(scalars) + in_vmem(near) + [...]
    ppermute x6, waiting for transfers between devices: 3.32 us -> 4.38 us  [swap(): return lax.ppermute(value, axis, pairs)]
  transfers between devices with their start and end apart: 7 -> 7, of which waited for: 2 -> 3; matrix products, arithmetic and copies ran while one was open for 0% -> 0% of each run, Pallas kernels for 9% -> 6%
where the time goes in v3:
time: 37.2 us; the launch traced here: 36.9 us
  starting transfers between devices  14.2 us (38%)
  Pallas kernels  8.65 us (23%)
  blocking collectives  7.2 us (19%)
  waiting for transfers between devices  5.45 us (15%)
  between operations  1.38 us (4%)
    ppermute x6, starting transfers between devices, swap(): return lax.ppermute(value, axis, pairs)  10.8 us
    pallas_call x7, Pallas kernels, call(): pl.pallas_call(kernel, in_specs=[smem] * len(scalars) + in_vmem(near) + [...  8.65 us
    all_to_all x1, blocking collectives, to_all(): return lax.all_to_all(chunks, 'blk', 0, 0, tiled=True)  7.2 us
    ppermute x6, waiting for transfers between devices, swap(): return lax.ppermute(value, axis, pairs)  4.38 us
    all_to_all x1, starting transfers between devices, to_all(): return lax.all_to_all(chunks, 'blk', 0, 0, tiled=True)  3.34 us
    all_to_all x1, waiting for transfers between devices, to_all(): return lax.all_to_all(chunks, 'blk', 0, 0, tiled=True)  1.07 us
  transfers between devices with their start and end apart: 7, of which 3 were waited for; matrix products, arithmetic and copies ran while one was open for 0% of the time, Pallas kernels for 6%

profile of v3, /device:TPU:0, one launch (start us, length us, event | category | flops | bytes accessed | tf_op | source)
XLA Modules:
  0.0 36.9 jit_solution(17946844370947986873)
XLA Ops:
  1.3 0.1 pad_add_fusion.place_ref
  1.4 0.0 copy-start
  1.4 2.3 %collide_first.1 = (f32[8,8,128]{2,1,0:T(8,128)S(1)}, f32[16,128]{1,0:T(8,128)S(1)}, f32[8,8,128]{2,1,0:T(8,128)S(1)}, f32[8,8,128]{2,1,0:T(8,128)S(1)}, f32[19,...) custom-call(s32[2]{0:T(128)S(1)} %pad_add_fusion.place_ref, ...), custom_call_target="tpu_custom_call" | custom-call | tf_op jit(solution)/shard_map/collide_first/pallas_call | solution.py:730
  3.7 0.5 %collective-permute-start = (f32[30,8,128]{2,1,0:T(8,128)S(1)}, f32[30,8,128]{2,1,0:T(8,128)S(1)}, u32[]{:S(2)}, u32[]{:S(2)}) collective-permute-start(f32[30,8,128]{2,1,0:T(8,128)S(1)} %get-tuple-element.26), channel_id=1, source_target_pairs={{0,1},{1,0},{2,3},{3,2},{4,5},{5,4},{6,7},{7,6},{8,9},{9,8},{10,11... | collective-permute-start | bytes 368648 | tf_op jit(solution)/shard_map/ppermute | solution.py:706
  4.2 3.6 %collective-permute-start.1 = (f32[30,8,128]{2,1,0:T(8,128)S(1)}, f32[30,8,128]{2,1,0:T(8,128)S(1)}, u32[]{:S(2)}, u32[]{:S(2)}) collective-permute-start(f32[30,8,128]{2,1,0:T(8,128)S(1)} %get-tuple-element.27), channel_id=1, source_target_pairs={{1,2},{2,1},{3,4},{4,3},{5,6},{6,5},{7,0},{0,7},{9,10},{10,9},{11,... | collective-permute-start | bytes 368648 | tf_op jit(solution)/shard_map/ppermute | solution.py:706
  7.8 7.2 %all_to_all.10.chunks_ref = f32[8,8,128]{2,1,0:T(8,128)S(1)} all-to-all(f32[8,8,128]{2,1,0:T(8,128)S(1)} %get-tuple-element.30), channel_id=1, replica_groups=mesh['span'=4,'blk'=8] {'blk'}, dimensions={0} | all-to-all | bytes 65536 | tf_op jit(solution)/shard_map/all_to_all | solution.py:741
  15.0 0.0 copy-done
  15.0 0.3 metal_first.1
  15.3 0.0 collective-permute-done.recva_ref
  15.3 0.0 collective-permute-done.1.recvb_ref
  15.3 0.9 %source_first.1 = (f32[80,128]{1,0:T(8,128)S(1)}, f32[80,128]{1,0:T(8,128)S(1)}, f32[12,8,128]{2,1,0:T(8,128)S(1)}) custom-call(s32[2]{0:T(128)S(1)} %pad_add_fusion.place_ref, f32[19,8,8,128]{3,2,1,0:T(8,128)S(1)} %get-tuple-element.25.postf_ref, f32[7,8,8,128]{3,2,1,0:T(8,128)S(1)} %get-tuple-element.28.posth_ref, ...), custom_call_target="tpu_custom_call" | custom-call | tf_op jit(solution)/shard_map/source_first/pallas_call | solution.py:730
  16.2 1.6 %collective-permute-start.2 = (f32[80,128]{1,0:T(8,128)S(1)}, f32[80,128]{1,0:T(8,128)S(1)}, u32[]{:S(2)}, u32[]{:S(2)}) collective-permute-start(f32[80,128]{1,0:T(8,128)S(1)} %get-tuple-element.33), channel_id=1, source_target_pairs={{0,8},{8,0},{16,24},{24,16},{1,9},{9,1},{17,25},{25,17},{2,10},{10... | collective-permute-start | bytes 122888 | tf_op jit(solution)/shard_map/ppermute | solution.py:706
  17.8 2.5 %collective-permute-start.3 = (f32[80,128]{1,0:T(8,128)S(1)}, f32[80,128]{1,0:T(8,128)S(1)}, u32[]{:S(2)}, u32[]{:S(2)}) collective-permute-start(f32[80,128]{1,0:T(8,128)S(1)} %get-tuple-element.34), channel_id=1, source_target_pairs={{8,16},{16,8},{24,0},{0,24},{9,17},{17,9},{25,1},{1,25},{10,18},{1... | collective-permute-start | bytes 122888 | tf_op jit(solution)/shard_map/ppermute | solution.py:706
  20.3 0.0 collective-permute-done.2.edgea_ref
  20.3 3.3 %collective-permute-done.3.edgeb_ref = f32[80,128]{1,0:T(8,128)S(1)} collective-permute-done((f32[80,128]{1,0:T(8,128)S(1)}, f32[80,128]{1,0:T(8,128)S(1)}, u32[]{:S(2)}, u32[]{:S(2)}) %collective-permute-start.3) | collective-permute-done | bytes 40992 | tf_op jit(solution)/shard_map/ppermute | solution.py:706
  23.6 1.5 %heat_second.1 = (f32[7,10,8,128]{3,2,1,0:T(8,128)S(1)}, f32[8,8,128]{2,1,0:T(8,128)}) custom-call(s32[2]{0:T(128)S(1)} %pad_add_fusion.place_ref, f32[7,8,8,128]{3,2,1,0:T(8,128)S(1)} %get-tuple-element.28.posth_ref, f32[30,8,128]{2,1,0:T(8,128)S(1)} %collective-permute-done.recva_ref, f32[30,8,128]{2,1,0:T(8,128)S(1)} %collective-permute-done.1.recvb_ref, ...), custom_call_target="tpu_custom_call" | custom-call | tf_op jit(solution)/shard_map/heat_second/pallas_call | solution.py:730
  25.1 3.3 %all-to-all-start.1 = ((f32[8,8,128]{2,1,0:T(8,128)}), f32[8,8,128]{2,1,0:T(8,128)S(1)}, u32[]{:S(2)}, u32[]{:S(2)}) async-start(f32[8,8,128]{2,1,0:T(8,128)} %get-tuple-element.41), calls=%async_computation.1 | async-start | bytes 65536 | tf_op jit(solution)/shard_map/all_to_all | solution.py:741
  28.5 1.1 %collide_second.1 = (f32[19,10,8,128]{3,2,1,0:T(8,128)S(1)}, f32[7,10,8,128]{3,2,1,0:T(8,128)S(1)}, f32[48,128]{1,0:T(8,128)S(1)}, f32[48,128]{1,0:T(8,128)S(1)}) custom-call(s32[2]{0:T(128)S(1)} %pad_add_fusion.place_ref, f32[19,8,8,128]{3,2,1,0:T(8,128)S(1)} %get-tuple-element.25.postf_ref, f32[30,8,128]{2,1,0:T(8,128)S(1)} %collective-permute-done.recva_ref, ...), custom_call_target="tpu_custom_call" | custom-call | tf_op jit(solution)/shard_map/collide_second/pallas_call | solution.py:730
  29.5 0.1 collective-permute-start.4
  29.6 2.6 %collective-permute-start.5 = (f32[48,128]{1,0:T(8,128)S(1)}, f32[48,128]{1,0:T(8,128)S(1)}, u32[]{:S(2)}, u32[]{:S(2)}) collective-permute-start(f32[48,128]{1,0:T(8,128)S(1)} %get-tuple-element.46), channel_id=1, source_target_pairs={{8,16},{16,8},{24,0},{0,24},{9,17},{17,9},{25,1},{1,25},{10,18},{1... | collective-permute-start | bytes 73736 | tf_op jit(solution)/shard_map/ppermute | solution.py:706
  32.2 1.1 %all-to-all-done.1.chunks_ref = f32[8,8,128]{2,1,0:T(8,128)S(1)} async-done(((f32[8,8,128]{2,1,0:T(8,128)}), f32[8,8,128]{2,1,0:T(8,128)S(1)}, u32[]{:S(2)}, u32[]{:S(2)}) %all-to-all-start.1) | async-done | bytes 32800 | tf_op jit(solution)/shard_map/all_to_all | solution.py:741
  33.2 1.0 %source_second.1 = (f32[10,8,128]{2,1,0:T(8,128)S(1)}, f32[16,128]{1,0:T(8,128)S(1)}, f32[1,256]{1,0:T(1,128)S(1)}) custom-call(s32[2]{0:T(128)S(1)} %pad_add_fusion.place_ref, f32[30,8,128]{2,1,0:T(8,128)S(1)} %collective-permute-done.recva_ref, f32[30,8,128]{2,1,0:T(8,128)S(1)} %collective-permute-done.1.recvb_ref, ...), custom_call_target="tpu_custom_call" | custom-call | tf_op jit(solution)/shard_map/source_second/pallas_call | solution.py:730
  34.3 0.0 collective-permute-done.4.edgea_ref
  34.3 1.0 %collective-permute-done.5.edgeb_ref = f32[48,128]{1,0:T(8,128)S(1)} collective-permute-done((f32[48,128]{1,0:T(8,128)S(1)}, f32[48,128]{1,0:T(8,128)S(1)}, u32[]{:S(2)}, u32[]{:S(2)}) %collective-permute-start.5) | collective-permute-done | bytes 24608 | tf_op jit(solution)/shard_map/ppermute | solution.py:706
  35.3 1.6 %stream_last.1 = (f32[19,8,8,128]{3,2,1,0:T(8,128)}, f32[7,8,8,128]{3,2,1,0:T(8,128)}, f32[1,256]{1,0:T(1,128)}) custom-call(s32[2]{0:T(128)S(1)} %pad_add_fusion.place_ref, f32[19,10,8,128]{3,2,1,0:T(8,128)S(1)} %get-tuple-element.39.postf_ref, f32[7,10,8,128]{3,2,1,0:T(8,128)S(1)} %get-tuple-element.40.posth_ref, ...), custom_call_target="tpu_custom_call" | custom-call | tf_op jit(solution)/shard_map/stream_last/pallas_call | solution.py:730
Async XLA Ops:
  1.4 13.6 %copy-start = (f32[256,256]{1,0:T(8,128)S(1)}, f32[256,256]{1,0:T(8,128)}, u32[]{:S(2)}) copy-start(f32[256,256]{1,0:T(8,128)} %conduction_ref.3) | copy-start | bytes 786436
  3.7 11.6 %collective-permute-start = (f32[30,8,128]{2,1,0:T(8,128)S(1)}, f32[30,8,128]{2,1,0:T(8,128)S(1)}, u32[]{:S(2)}, u32[]{:S(2)}) collective-permute-start(f32[30,8,128]{2,1,0:T(8,128)S(1)} %get-tuple-element.26), channel_id=1, source_target_pairs={{0,1},{1,0},{2,3},{3,2},{4,5},{5,4},{6,7},{7,6},{8,9},{9,8},{10,11... | collective-permute-start | bytes 368648 | tf_op jit(solution)/shard_map/ppermute | solution.py:706
  4.2 11.1 %collective-permute-start.1 = (f32[30,8,128]{2,1,0:T(8,128)S(1)}, f32[30,8,128]{2,1,0:T(8,128)S(1)}, u32[]{:S(2)}, u32[]{:S(2)}) collective-permute-start(f32[30,8,128]{2,1,0:T(8,128)S(1)} %get-tuple-element.27), channel_id=1, source_target_pairs={{1,2},{2,1},{3,4},{4,3},{5,6},{6,5},{7,0},{0,7},{9,10},{10,9},{11,... | collective-permute-start | bytes 368648 | tf_op jit(solution)/shard_map/ppermute | solution.py:706
  16.2 4.1 %collective-permute-start.2 = (f32[80,128]{1,0:T(8,128)S(1)}, f32[80,128]{1,0:T(8,128)S(1)}, u32[]{:S(2)}, u32[]{:S(2)}) collective-permute-start(f32[80,128]{1,0:T(8,128)S(1)} %get-tuple-element.33), channel_id=1, source_target_pairs={{0,8},{8,0},{16,24},{24,16},{1,9},{9,1},{17,25},{25,17},{2,10},{10... | collective-permute-start | bytes 122888 | tf_op jit(solution)/shard_map/ppermute | solution.py:706
  17.8 5.8 %collective-permute-start.3 = (f32[80,128]{1,0:T(8,128)S(1)}, f32[80,128]{1,0:T(8,128)S(1)}, u32[]{:S(2)}, u32[]{:S(2)}) collective-permute-start(f32[80,128]{1,0:T(8,128)S(1)} %get-tuple-element.34), channel_id=1, source_target_pairs={{8,16},{16,8},{24,0},{0,24},{9,17},{17,9},{25,1},{1,25},{10,18},{1... | collective-permute-start | bytes 122888 | tf_op jit(solution)/shard_map/ppermute | solution.py:706
  25.1 8.1 %all-to-all-start.1 = ((f32[8,8,128]{2,1,0:T(8,128)}), f32[8,8,128]{2,1,0:T(8,128)S(1)}, u32[]{:S(2)}, u32[]{:S(2)}) async-start(f32[8,8,128]{2,1,0:T(8,128)} %get-tuple-element.41), calls=%async_computation.1 | async-start | bytes 65536 | tf_op jit(solution)/shard_map/all_to_all | solution.py:741
  29.5 4.7 %collective-permute-start.4 = (f32[48,128]{1,0:T(8,128)S(1)}, f32[48,128]{1,0:T(8,128)S(1)}, u32[]{:S(2)}, u32[]{:S(2)}) collective-permute-start(f32[48,128]{1,0:T(8,128)S(1)} %get-tuple-element.45), channel_id=1, source_target_pairs={{0,8},{8,0},{16,24},{24,16},{1,9},{9,1},{17,25},{25,17},{2,10},{10... | collective-permute-start | bytes 73736 | tf_op jit(solution)/shard_map/ppermute | solution.py:706
  29.6 5.7 %collective-permute-start.5 = (f32[48,128]{1,0:T(8,128)S(1)}, f32[48,128]{1,0:T(8,128)S(1)}, u32[]{:S(2)}, u32[]{:S(2)}) collective-permute-start(f32[48,128]{1,0:T(8,128)S(1)} %get-tuple-element.46), channel_id=1, source_target_pairs={{8,16},{16,8},{24,0},{0,24},{9,17},{17,9},{25,1},{1,25},{10,18},{1... | collective-permute-start | bytes 73736 | tf_op jit(solution)/shard_map/ppermute | solution.py:706

commit v4 on v3

--- a/solution.py
+++ b/solution.py
@@ -47,7 +47,6 @@
 UP = [i for i in range(ALL) if VELOCITY[i][2] == 1]
 DOWN = [i for i in range(ALL) if VELOCITY[i][2] == -1]
 EDGES = len(UP)
-
 SOLID, COUNTS, LISTS = FACES, FACES + 1, FACES + 2
 SIDE_PLANES = FACES + 4
 LIST_ROWS = 12
@@ -175,23 +174,30 @@
     counts_ref[...] = at_nodes.reshape(wide, deep, lanes)
 
 
+def tree(values):
+    while len(values) > 1:
+        values = [sum(values[n : n + 2][1:], values[n]) for n in range(0, len(values), 2)]
+    return values[0]
+
+
 def collide_flow(flow, solid):
-    density = flow[0]
-    for i in range(1, FLOWS):
-        density = density + flow[i]
+    pairs = range(1, FLOWS, 2)
+    gap = {i: flow[i] - flow[i + 1] for i in pairs}
+    density = tree([flow[0]] + [flow[i] + flow[i + 1] for i in pairs])
     inverse = 1.0 / density
     speed = []
     for axis in range(3):
-        ahead = [flow[i] for i in range(FLOWS) if VELOCITY[i][axis] == 1]
-        behind = [flow[i] for i in range(FLOWS) if VELOCITY[i][axis] == -1]
-        speed.append((sum(ahead[1:], ahead[0]) - sum(behind[1:], behind[0])) * inverse)
+        terms = [
+            gap[i] if VELOCITY[i][axis] == 1 else -gap[i] for i in pairs if VELOCITY[i][axis] != 0
+        ]
+        speed.append(tree(terms) * inverse)
     base = 1.0 - 1.5 * (speed[0] * speed[0] + speed[1] * speed[1] + speed[2] * speed[2])
     scaled = {w: density * (w / RELAX_FLOW) for w in sorted(set(WEIGHT_FLOW))}
     keep = 1.0 - 1.0 / RELAX_FLOW
     post = [None] * FLOWS
     rest = scaled[WEIGHT_FLOW[0]] * base + keep * flow[0]
     post[0] = jnp.where(solid, flow[0], rest)
-    for i in range(1, FLOWS, 2):
+    for i in pairs:
         along = None
         for axis in range(3):
             c = VELOCITY[i][axis]
@@ -236,7 +242,6 @@
 
 
 def first_kernel(
-    place_ref,
     count_ref,
     flow_hbm,
     heat_hbm,
@@ -264,7 +269,7 @@
 ):
     wide = flow_ref.shape[1]
     strip = wide // STRIPS
-    odd = place_ref[0] % 2 == 1
+    odd = lax.axis_index("blk") % 2 == 1
     small = [
         pltpu.make_async_copy(source, target, sems.at[n])
         for n, (source, target) in enumerate(
@@ -414,12 +419,21 @@
     return conduct(conduction, [value[0:1], value[1:2]])
 
 
-def metal_kernel(list_ref, chunks_ref, conduction_ref, metal_ref, source_ref):
+def source_kernel(
+    postf_ref,
+    posth_ref,
+    recva_ref,
+    recvb_ref,
+    list_ref,
+    chunks_ref,
+    conduction_ref,
+    senda_ref,
+    sendb_ref,
+    metal_ref,
+    source_ref,
+):
+    wide, deep, lanes = postf_ref.shape[1:]
     blocks = chunks_ref.shape[0]
-    wide, deep, lanes = source_ref.shape
-    lists = lists_of(list_ref[...])
-    found = metal_at(metal_rows(chunks_ref, 0), lists)[0]
-    source_ref[...] = give_planes(found, lists[2], 0, wide, deep)
     sums = chunks_ref[0]
     for d in range(1, blocks):
         sums = sums + chunks_ref[d]
@@ -428,28 +442,13 @@
     metal_ref[...] = jnp.zeros(metal_ref.shape, F32)
     put_rows(metal_ref, 0, metal)
     metal_ref[2:4, :] = count
-
-
-def source_kernel(
-    place_ref,
-    postf_ref,
-    posth_ref,
-    recva_ref,
-    recvb_ref,
-    list_ref,
-    chunks_ref,
-    metal_ref,
-    own_ref,
-    senda_ref,
-    sendb_ref,
-    source_ref,
-):
-    wide, deep, lanes = postf_ref.shape[1:]
-    low, high = sides(place_ref[0] % 2 == 1, recva_ref, recvb_ref)
+    own = lists_of(list_ref[...])
+    found = metal_at(metal_rows(chunks_ref, 0), own)[0]
+    source_ref[2 : wide + 2] = give_planes(found, own[2], 0, wide, deep)
+    low, high = sides(lax.axis_index("blk") % 2 == 1, recva_ref, recvb_ref)
     before, after = side_lists(low), side_lists(high)
     found = metal_at(metal_rows(chunks_ref, 0), before, after)
     source_ref[0:2] = give_planes(found[0], before[2], wide - 2, 2, deep)
-    source_ref[2 : wide + 2] = own_ref[...]
     source_ref[wide + 2 :] = give_planes(found[1], after[2], 0, 2, deep)
     get = planes(postf_ref, posth_ref, low, high, wide, source_ref)
 
@@ -461,17 +460,17 @@
                     at = j * EDGES + n
                     ref[at : at + 1, :] = value[row : row + 1, :]
             at = (wide + 2) * EDGES
-            ref[at : at + 2, :] = metal_ref[0:2]
+            put_rows(ref, at, metal)
             ref[at + 2 : at + 2 + LIST_ROWS, :] = list_ref[0:LIST_ROWS]
 
     for ref in (senda_ref, sendb_ref):
         ref[ref.shape[0] - 8 :, :] = jnp.zeros((8, lanes), F32)
 
-    @pl.when(place_ref[1] % 2 == 1)
+    @pl.when(lax.axis_index("span") % 2 == 1)
     def _():
         fill(sendb_ref, senda_ref)
 
-    @pl.when(place_ref[1] % 2 == 0)
+    @pl.when(lax.axis_index("span") % 2 == 0)
     def _():
         fill(senda_ref, sendb_ref)
 
@@ -503,8 +502,8 @@
     return edge
 
 
-def heat_kernel(
-    place_ref,
+def step_kernel(
+    postf_ref,
     posth_ref,
     recva_ref,
     recvb_ref,
@@ -513,21 +512,28 @@
     edgeb_ref,
     list_ref,
     metal_ref,
-    heat_ref,
+    solid_ref,
+    counts_ref,
+    chunks_hbm,
+    outf_ref,
+    outh_ref,
+    senda_ref,
+    sendb_ref,
     out_ref,
+    sem,
 ):
     wide, deep, lanes = posth_ref.shape[1:]
     blocks = out_ref.shape[0]
-    low, high = sides(place_ref[0] % 2 == 1, recva_ref, recvb_ref)
+    low, high = sides(lax.axis_index("blk") % 2 == 1, recva_ref, recvb_ref)
     get = planes(None, posth_ref, low, high, wide, source_ref)
-    odd = place_ref[1] % 2 == 1
+    odd = lax.axis_index("span") % 2 == 1
     edge = edge_rows(odd, edgea_ref, edgeb_ref, -1)
     tempers = []
     for x in range(-1, wide + 1):
         temper = None
         for k in range(HEATS):
             value = stream(get, edge, deep, FLOWS + k, x)
-            heat_ref[k, x + 1] = value
+            outh_ref[k, x + 1] = value
             temper = value if temper is None else temper + value
         if 0 <= x < wide:
             tempers.append(temper)
@@ -544,27 +550,9 @@
         out_ref[d, 2:4, :] = jnp.where(odd, a, b)
         out_ref[d, 4:6, :] = jnp.where(odd, b, a)
         out_ref[d, 6:8, :] = sums[2 * d : 2 * d + 2]
-
-
-def flow_kernel(
-    place_ref,
-    postf_ref,
-    recva_ref,
-    recvb_ref,
-    edgea_ref,
-    edgeb_ref,
-    heat_ref,
-    solid_ref,
-    counts_ref,
-    outf_ref,
-    outh_ref,
-    senda_ref,
-    sendb_ref,
-):
-    wide, deep, lanes = postf_ref.shape[1:]
-    low, high = sides(place_ref[0] % 2 == 1, recva_ref, recvb_ref)
+    copy = pltpu.make_async_copy(out_ref, chunks_hbm, sem)
+    copy.start()
     get = planes(postf_ref, None, low, high, wide, None)
-    edge = edge_rows(place_ref[1] % 2 == 1, edgea_ref, edgeb_ref, -1)
     for x in range(-1, wide + 1):
         flow = [stream(get, edge, deep, i, x) for i in range(FLOWS)]
         if x < 0:
@@ -574,7 +562,7 @@
         else:
             solid, counts = solid_ref[x] != 0, counts_ref[x]
         post, speed = collide_flow(flow, solid)
-        heat = [heat_ref[k, x + 1] for k in range(HEATS)]
+        heat = [outh_ref[k, x + 1] for k in range(HEATS)]
         temper = heat[0]
         for k in range(1, HEATS):
             temper = temper + heat[k]
@@ -590,20 +578,49 @@
                 for n, i in enumerate(comps):
                     at = x + 1 - VELOCITY[i][0]
                     value = outf_ref[i, at] if i < FLOWS else outh_ref[i - FLOWS, at]
-                    where = x * EDGES + n
-                    ref[where : where + 1, :] = value[row : row + 1, :]
-
-    @pl.when(place_ref[1] % 2 == 1)
+                    cy = VELOCITY[i][1]
+                    value = pltpu.roll(value, cy % lanes, 1) if cy else value
+                    ref[n, x] = value[row : row + 1, :]
+
+    @pl.when(lax.axis_index("span") % 2 == 1)
     def _():
         fill(sendb_ref, senda_ref)
 
-    @pl.when(place_ref[1] % 2 == 0)
+    @pl.when(lax.axis_index("span") % 2 == 0)
     def _():
         fill(senda_ref, sendb_ref)
 
-
-def last_metal_kernel(
-    place_ref,
+    copy.wait()
+
+
+def shift(value, i):
+    cx, cy, cz = VELOCITY[i]
+    if cz != 0:
+        value = pltpu.roll(value, cz % value.shape[0], 0)
+    if cy != 0:
+        value = pltpu.roll(value, cy % value.shape[1], 1)
+    return value
+
+
+def stream_kernel(postf_ref, flow_hbm, flow_ref, sems):
+    wide = flow_ref.shape[1]
+    copies = []
+    for n, i in enumerate(range(FLOWS)):
+        for x in range(wide):
+            flow_ref[i, x] = shift(postf_ref[i, x + 1 - VELOCITY[i][0]], i)
+        if i % 4 == 3 or i == FLOWS - 1:
+            part = pl.ds(i - i % 4, i % 4 + 1)
+            copy = pltpu.make_async_copy(
+                flow_ref.at[part], flow_hbm.at[part], sems.at[len(copies)]
+            )
+            copy.start()
+            copies.append(copy)
+    for copy in copies:
+        copy.wait()
+
+
+def heat_kernel(
+    posth_ref,
     recva_ref,
     recvb_ref,
     list_ref,
@@ -612,89 +629,93 @@
     edgeb_ref,
     metal_ref,
     conduction_ref,
-    source_ref,
+    heat_hbm,
+    metal_hbm,
     row_ref,
+    heat_ref,
     out_ref,
+    sems,
 ):
     blocks = chunks_ref.shape[0]
-    wide, deep, lanes = source_ref.shape
-    wide = wide - 2
-    low, high = sides(place_ref[0] % 2 == 1, recva_ref, recvb_ref)
-    own, before, after = lists_of(list_ref[...]), side_lists(low), side_lists(high)
-    found = metal_at(metal_rows(chunks_ref, 0), own)[0]
-    source_ref[1 : wide + 1] = give_planes(found, own[2], 0, wide, deep)
-    found = metal_at(metal_rows(chunks_ref, 0), before, after)
-    source_ref[0:1] = give_planes(found[0], before[2], wide - 1, 1, deep)
-    source_ref[wide + 1 :] = give_planes(found[1], after[2], 0, 1, deep)
-    odd = place_ref[1] % 2 == 1
-    at = (wide + 2) * EDGES + 2
-    a = edgea_ref[at : at + LIST_ROWS, :]
-    b = edgeb_ref[at : at + LIST_ROWS, :]
-    for n, (block, shift, z) in enumerate(
-        ((jnp.where(odd, a, b), 2, deep - 1), (jnp.where(odd, b, a), 4, 0))
-    ):
-        lists = lists_of(block)
-        node = lists[2]
-        column = node >> 7
-        row = jnp.where(lax.rem(column, deep) == z, lax.div(column, deep), -1)
-        found = metal_at(metal_rows(chunks_ref, shift), lists)[0]
-        row_ref[wide * n : wide * (n + 1), :] = give(found, row, node, wide)
+    wide, deep, lanes = heat_ref.shape[1:]
+    odd = lax.axis_index("span") % 2 == 1
     sums = chunks_ref[0]
     for d in range(1, blocks):
         sums = sums + chunks_ref[d]
     out_ref[...] = next_metal(conduction_ref[...], metal_ref[0:2], sums[6:8], metal_ref[2:4])
-
-
-def final_kernel(
-    place_ref,
-    postf_ref,
-    posth_ref,
-    source_ref,
+    copies = [pltpu.make_async_copy(out_ref, metal_hbm, sems.at[0])]
+    copies[0].start()
+
+    low, high = sides(lax.axis_index("blk") % 2 == 1, recva_ref, recvb_ref)
+    own, before, after = lists_of(list_ref[...]), side_lists(low), side_lists(high)
+    inner = metal_at(metal_rows(chunks_ref, 0), own)[0]
+    found = metal_at(metal_rows(chunks_ref, 0), before, after)
+    source = [give_planes(found[0], before[2], wide - 1, 1, deep)]
+    source.append(give_planes(inner, own[2], 0, wide, deep))
+    source.append(give_planes(found[1], after[2], 0, 1, deep))
+    source = jnp.concatenate(source, axis=0)
+    for k in range(HEATS):
+        i = FLOWS + k
+        for x in range(wide):
+            at = x + 1 - VELOCITY[i][0]
+            heat_ref[k, x] = shift(posth_ref[k, at] + WEIGHT_HEAT[k] * source[at], i)
+    copies.append(pltpu.make_async_copy(heat_ref, heat_hbm, sems.at[1]))
+    copies[1].start()
+
+    at = (wide + 2) * EDGES + 2
+    a = edgea_ref[at : at + LIST_ROWS, :]
+    b = edgeb_ref[at : at + LIST_ROWS, :]
+    for n, (block, moved, z) in enumerate(
+        ((jnp.where(odd, a, b), 2, deep - 1), (jnp.where(odd, b, a), 4, 0))
+    ):
+        lists = lists_of(block)
+        column = lists[2] >> 7
+        row = jnp.where(lax.rem(column, deep) == z, lax.div(column, deep), -1)
+        found = metal_at(metal_rows(chunks_ref, moved), lists)[0]
+        row_ref[n * wide : (n + 1) * wide] = give(found, row, lists[2], wide)
+    for copy in copies:
+        copy.wait()
+
+
+def edge_kernel(
     row_ref,
-    metal_ref,
-    edgea_ref,
-    edgeb_ref,
+    lasta_ref,
+    lastb_ref,
+    flow_in,
+    heat_in,
     flow_hbm,
     heat_hbm,
-    metal_hbm,
-    flow_ref,
-    heat_ref,
+    rows_ref,
     sems,
 ):
-    wide, deep, lanes = flow_ref.shape[1:]
-    strip = wide // STRIPS
-
-    def get(i, x):
-        if i < FLOWS:
-            return postf_ref[i, x + 1]
-        return posth_ref[i - FLOWS, x + 1] + WEIGHT_HEAT[i - FLOWS] * source_ref[x + 1]
-
-    sent = edge_rows(place_ref[1] % 2 == 1, edgea_ref, edgeb_ref, 0)
-
-    def edge(i, x):
-        value = sent(i, x)
-        if i < FLOWS:
-            return value
-        at = x if VELOCITY[i][2] == 1 else wide + x
-        return value + WEIGHT_HEAT[i - FLOWS] * row_ref[at : at + 1, :]
-
-    copies = [pltpu.make_async_copy(metal_ref, metal_hbm, sems.at[2 * STRIPS])]
-    copies[0].start()
-    for n in range(STRIPS):
-        for x in range(n * strip, (n + 1) * strip):
-            for i in range(FLOWS):
-                flow_ref[i, x] = stream(get, edge, deep, i, x)
-            for k in range(HEATS):
-                heat_ref[k, x] = stream(get, edge, deep, FLOWS + k, x)
-        part = pl.ds(n * strip, strip)
-        for m, (source, target) in enumerate(((flow_ref, flow_hbm), (heat_ref, heat_hbm))):
-            copy = pltpu.make_async_copy(
-                source.at[:, part], target.at[:, part], sems.at[2 * n + m]
-            )
-            copy.start()
-            copies.append(copy)
-    for copy in copies:
-        copy.wait()
+    wide, deep, lanes = flow_hbm.shape[1:]
+
+    def fill(low_ref, high_ref):
+        copies = []
+        for m, (ref, comps, z) in enumerate(((low_ref, UP, 0), (high_ref, DOWN, deep - 1))):
+            for n, i in enumerate(comps):
+                if i < FLOWS:
+                    source, target = ref.at[n], flow_hbm.at[i]
+                else:
+                    source, target = rows_ref.at[m], heat_hbm.at[i - FLOWS]
+                    for x in range(wide):
+                        given = row_ref[m * wide + x : m * wide + x + 1, :]
+                        rows_ref[m, x] = ref[n, x] + WEIGHT_HEAT[i - FLOWS] * given
+                copy = pltpu.make_async_copy(
+                    source, target.at[:, z : z + 1, :], sems.at[m * EDGES + n]
+                )
+                copy.start()
+                copies.append(copy)
+        for copy in copies:
+            copy.wait()
+
+    @pl.when(lax.axis_index("span") % 2 == 1)
+    def _():
+        fill(lasta_ref, lastb_ref)
+
+    @pl.when(lax.axis_index("span") % 2 == 0)
+    def _():
+        fill(lastb_ref, lasta_ref)
 
 
 def swap(value, axis, offset):
@@ -719,20 +740,21 @@
 ):
     blocks = lax.axis_size("blk")
     wide, deep, lanes = solid_mask.shape
-    place = jnp.stack([lax.axis_index("blk"), lax.axis_index("span")]).astype(jnp.int32)
     smem = pl.BlockSpec(memory_space=pltpu.SMEM)
     hbm = pl.BlockSpec(memory_space=pltpu.HBM)
-
-    def call(kernel, name, outs, scalars, *args, far=0, scratch=(), out_spec=None):
+    near_spec = pl.BlockSpec(memory_space=pltpu.VMEM)
+
+    def call(kernel, name, outs, scalars, *args, far=0, scratch=(), out_spec=None, alias=None):
         near = len(args) - far
         held = [pltpu.with_memory_space_constraint(arg, pltpu.HBM) for arg in args[near:]]
-        out_spec = out_spec or in_vmem(1)[0]
+        out_spec = out_spec or jax.tree.map(lambda _: near_spec, outs)
         return pl.pallas_call(
             kernel,
             in_specs=[smem] * len(scalars) + in_vmem(near) + [hbm] * far,
-            out_specs=jax.tree.map(lambda _: out_spec, outs),
+            out_specs=out_spec,
             out_shape=outs,
             scratch_shapes=scratch,
+            input_output_aliases=alias or {},
             compiler_params=params(),
             name=name,
         )(*scalars, *args[:near], *held)
@@ -747,7 +769,7 @@
         first_kernel,
         "collide_first",
         (shape(blocks, 8, lanes), shape(16, lanes), field, field, flows, heats, side, side),
-        (place, wall_count),
+        (wall_count,),
         populations,
         thermal,
         solid_mask,
@@ -772,36 +794,35 @@
     recvb = swap(sendb, "blk", 1)
     edge_count = -(-((wide + 2) * EDGES + 2 + LIST_ROWS) // 8) * 8
     edges = shape(edge_count, lanes)
-    metal, own = call(
-        metal_kernel,
-        "metal_first",
-        (shape(8, lanes), shape(wide, deep, lanes)),
-        (),
-        lists,
-        chunks,
-        conduction,
-    )
-    senda, sendb, source = call(
+    senda, sendb, metal, source = call(
         source_kernel,
         "source_first",
-        (edges, edges, shape(wide + 4, deep, lanes)),
-        (place,),
+        (edges, edges, shape(8, lanes), shape(wide + 4, deep, lanes)),
+        (),
         postf,
         posth,
         recva,
         recvb,
         lists,
         chunks,
-        metal,
-        own,
+        conduction,
     )
     edgea = swap(senda, "span", 0)
     edgeb = swap(sendb, "span", 1)
-    heat, chunks = call(
-        heat_kernel,
-        "heat_second",
-        (shape(HEATS, wide + 2, deep, lanes), shape(blocks, 8, lanes)),
-        (place,),
+    edges = shape(EDGES, wide, 1, lanes)
+    chunk = shape(blocks, 8, lanes)
+    chunks, postf, posth, senda, sendb = call(
+        step_kernel,
+        "collide_second",
+        (
+            chunk,
+            shape(FLOWS, wide + 2, deep, lanes),
+            shape(HEATS, wide + 2, deep, lanes),
+            edges,
+            edges,
+        ),
+        (),
+        postf,
         posth,
         recva,
         recvb,
@@ -810,39 +831,29 @@
         edgeb,
         lists,
         metal,
-    )
-    chunks = to_all(chunks)
-    edges = shape(wide * EDGES, lanes)
-    postf, posth, senda, sendb = call(
-        flow_kernel,
-        "collide_second",
-        (
-            shape(FLOWS, wide + 2, deep, lanes),
-            shape(HEATS, wide + 2, deep, lanes),
-            edges,
-            edges,
-        ),
-        (place,),
-        postf,
-        recva,
-        recvb,
-        edgea,
-        edgeb,
-        heat,
         solid,
         counts,
-    )
+        scratch=[pltpu.VMEM(chunk.shape, F32), pltpu.SemaphoreType.DMA],
+        out_spec=(hbm,) + (near_spec,) * 4,
+    )
+    chunks = to_all(chunks)
     lasta = swap(senda, "span", 0)
     lastb = swap(sendb, "span", 1)
-    source, rows, metal = call(
-        last_metal_kernel,
-        "source_second",
-        (
-            shape(wide + 2, deep, lanes),
-            shape(2 * wide, lanes),
-            shape(1, metal_temp.shape[1]),
-        ),
-        (place,),
+    part = call(
+        stream_kernel,
+        "stream_flow",
+        flows,
+        (),
+        postf,
+        scratch=[pltpu.VMEM(flows.shape, F32), pltpu.SemaphoreType.DMA((-(-FLOWS // 4),))],
+        out_spec=hbm,
+    )
+    heat, metal, rows = call(
+        heat_kernel,
+        "stream_heat",
+        (heats, shape(*metal_temp.shape), shape(2 * wide, lanes)),
+        (),
+        posth,
         recva,
         recvb,
         lists,
@@ -851,26 +862,32 @@
         edgeb,
         metal,
         conduction,
-    )
-    return call(
-        final_kernel,
-        "stream_last",
-        (flows, heats, shape(*metal_temp.shape)),
-        (place,),
-        postf,
-        posth,
-        source,
+        scratch=[
+            pltpu.VMEM(heats.shape, F32),
+            pltpu.VMEM(metal_temp.shape, F32),
+            pltpu.SemaphoreType.DMA((2,)),
+        ],
+        out_spec=(hbm, hbm, near_spec),
+    )
+    flow, heat = call(
+        edge_kernel,
+        "stream_edges",
+        (flows, heats),
+        (),
         rows,
-        metal,
         lasta,
         lastb,
+        part,
+        heat,
+        far=2,
         scratch=[
-            pltpu.VMEM(flows.shape, F32),
-            pltpu.VMEM(heats.shape, F32),
-            pltpu.SemaphoreType.DMA((2 * STRIPS + 1,)),
+            pltpu.VMEM((2, wide, 1, lanes), F32),
+            pltpu.SemaphoreType.DMA((2 * EDGES,)),
         ],
-        out_spec=hbm,
-    )
+        out_spec=(hbm, hbm),
+        alias={3: 0, 4: 1},
+    )
+    return (flow, heat, metal)
 
 
 def solution(mesh):

time: 37.2 us -> 33.8 us (0.909)
  Pallas kernels: 8.65 us -> 6.31 us
  waiting for transfers between devices: 5.45 us -> 4.48 us
    pallas_call x7 -> x6, Pallas kernels: 8.65 us -> 6.31 us  [call(): pl.pallas_call(kernel, in_specs=[smem] * len(scalars) + in_vmem(near) + [...]
    ppermute x6, waiting for transfers between devices: 4.38 us -> 3.3 us  [swap(): return lax.ppermute(value, axis, pairs)]
  transfers between devices with their start and end apart: 7 -> 7, of which waited for: 3 -> 2; matrix products, arithmetic and copies ran while one was open for 0% -> 0% of each run, Pallas kernels for 6% -> 6%
where the time goes in v4:
time: 33.8 us; the launch traced here: 33.6 us
  starting transfers between devices  14.2 us (42%)
  blocking collectives  7.2 us (21%)
  Pallas kernels  6.31 us (19%)
  waiting for transfers between devices  4.48 us (13%)
  between operations  1.37 us (4%)
    ppermute x6, starting transfers between devices, swap(): return lax.ppermute(value, axis, pairs)  10.8 us
    all_to_all x1, blocking collectives, to_all(): return lax.all_to_all(chunks, 'blk', 0, 0, tiled=True)  7.2 us
    pallas_call x6, Pallas kernels, call(): pl.pallas_call(kernel, in_specs=[smem] * len(scalars) + in_vmem(near) + [...  6.31 us
    all_to_all x1, starting transfers between devices, to_all(): return lax.all_to_all(chunks, 'blk', 0, 0, tiled=True)  3.35 us
    ppermute x6, waiting for transfers between devices, swap(): return lax.ppermute(value, axis, pairs)  3.3 us
    all_to_all x1, waiting for transfers between devices, to_all(): return lax.all_to_all(chunks, 'blk', 0, 0, tiled=True)  1.18 us
  transfers between devices with their start and end apart: 7, of which 2 were waited for; matrix products, arithmetic and copies ran while one was open for 0% of the time, Pallas kernels for 6%

profile of v4, /device:TPU:0, one launch (start us, length us, event | category | flops | bytes accessed | tf_op | source)
XLA Modules:
  0.0 33.6 jit_solution(6341311015303033227)
XLA Ops:
  1.3 0.0 copy-start
  1.3 1.8 %collide_first.1 = (f32[8,8,128]{2,1,0:T(8,128)S(1)}, f32[16,128]{1,0:T(8,128)S(1)}, f32[8,8,128]{2,1,0:T(8,128)S(1)}, f32[8,8,128]{2,1,0:T(8,128)S(1)}, f32[19,...) custom-call(s32[1,1]{1,0:T(1,128)S(6)} %copy.16.count_ref, ...), custom_call_target="tpu_custom_call" | custom-call | tf_op jit(solution)/shard_map/collide_first/pallas_call | solution.py:751
  3.1 0.5 %collective-permute-start = (f32[30,8,128]{2,1,0:T(8,128)S(1)}, f32[30,8,128]{2,1,0:T(8,128)S(1)}, u32[]{:S(2)}, u32[]{:S(2)}) collective-permute-start(f32[30,8,128]{2,1,0:T(8,128)S(1)} %get-tuple-element.27), channel_id=1, source_target_pairs={{0,1},{1,0},{2,3},{3,2},{4,5},{5,4},{6,7},{7,6},{8,9},{9,8},{10,11... | collective-permute-start | bytes 368648 | tf_op jit(solution)/shard_map/ppermute | solution.py:727
  3.6 3.6 %collective-permute-start.1 = (f32[30,8,128]{2,1,0:T(8,128)S(1)}, f32[30,8,128]{2,1,0:T(8,128)S(1)}, u32[]{:S(2)}, u32[]{:S(2)}) collective-permute-start(f32[30,8,128]{2,1,0:T(8,128)S(1)} %get-tuple-element.28), channel_id=1, source_target_pairs={{1,2},{2,1},{3,4},{4,3},{5,6},{6,5},{7,0},{0,7},{9,10},{10,9},{11,... | collective-permute-start | bytes 368648 | tf_op jit(solution)/shard_map/ppermute | solution.py:727
  7.2 7.2 %all_to_all.10.chunks_ref = f32[8,8,128]{2,1,0:T(8,128)S(1)} all-to-all(f32[8,8,128]{2,1,0:T(8,128)S(1)} %get-tuple-element.30), channel_id=1, replica_groups=mesh['span'=4,'blk'=8] {'blk'}, dimensions={0} | all-to-all | bytes 65536 | tf_op jit(solution)/shard_map/all_to_all | solution.py:763
  14.4 0.0 collective-permute-done.recva_ref
  14.4 0.0 collective-permute-done.1.recvb_ref
  14.4 0.0 copy-done
  14.4 0.4 %source_first.1 = (f32[80,128]{1,0:T(8,128)S(1)}, f32[80,128]{1,0:T(8,128)S(1)}, f32[8,128]{1,0:T(8,128)S(1)}, f32[12,8,128]{2,1,0:T(8,128)S(1)}) custom-call(f32[19,8,8,128]{3,2,1,0:T(8,128)S(1)} %get-tuple-element.25.postf_ref, f32[7,8,8,128]{3,2,1,0:T(8,128)S(1)} %get-tuple-element.26.posth_ref, f32[30,8,128]{2,1,0:T(8,128)S(1)} %collective-permute-done.recva_ref, ...), custom_call_target="tpu_custom_call" | custom-call | tf_op jit(solution)/shard_map/source_first/pallas_call | solution.py:751
  14.9 1.6 %collective-permute-start.2 = (f32[80,128]{1,0:T(8,128)S(1)}, f32[80,128]{1,0:T(8,128)S(1)}, u32[]{:S(2)}, u32[]{:S(2)}) collective-permute-start(f32[80,128]{1,0:T(8,128)S(1)} %get-tuple-element.32), channel_id=1, source_target_pairs={{0,8},{8,0},{16,24},{24,16},{1,9},{9,1},{17,25},{25,17},{2,10},{10... | collective-permute-start | bytes 122888 | tf_op jit(solution)/shard_map/ppermute | solution.py:727
  16.5 2.5 %collective-permute-start.3 = (f32[80,128]{1,0:T(8,128)S(1)}, f32[80,128]{1,0:T(8,128)S(1)}, u32[]{:S(2)}, u32[]{:S(2)}) collective-permute-start(f32[80,128]{1,0:T(8,128)S(1)} %get-tuple-element.33), channel_id=1, source_target_pairs={{8,16},{16,8},{24,0},{0,24},{9,17},{17,9},{25,1},{1,25},{10,18},{1... | collective-permute-start | bytes 122888 | tf_op jit(solution)/shard_map/ppermute | solution.py:727
  19.0 0.0 collective-permute-done.2.edgea_ref
  19.0 3.3 %collective-permute-done.3.edgeb_ref = f32[80,128]{1,0:T(8,128)S(1)} collective-permute-done((f32[80,128]{1,0:T(8,128)S(1)}, f32[80,128]{1,0:T(8,128)S(1)}, u32[]{:S(2)}, u32[]{:S(2)}) %collective-permute-start.3) | collective-permute-done | bytes 40992 | tf_op jit(solution)/shard_map/ppermute | solution.py:727
  22.3 1.2 %collide_second.1 = (f32[8,8,128]{2,1,0:T(8,128)}, f32[19,10,8,128]{3,2,1,0:T(8,128)S(1)}, f32[7,10,8,128]{3,2,1,0:T(8,128)S(1)}, f32[6,8,1,128]{3,2,1,0:T(1,128)S(1)}, f32[6,8,1,128]{3,2,1,0:T(1,128)S(1)}) custom-call(f32[19,8,8,128]{3,2,1,0:T(8,128)S(1)} %get-tuple-element.25.postf_ref, f32[7,8,8,128]{3,2,1,0:T(8,128)S(1)} %get-tuple-element.26.posth_ref, ...), custom_call_target="tpu_custom_call" | custom-call | tf_op jit(solution)/shard_map/collide_second/pallas_call | solution.py:751
  23.5 3.4 %all-to-all-start.1 = ((f32[8,8,128]{2,1,0:T(8,128)}), f32[8,8,128]{2,1,0:T(8,128)S(1)}, u32[]{:S(2)}, u32[]{:S(2)}) async-start(f32[8,8,128]{2,1,0:T(8,128)} %get-tuple-element.38), calls=%async_computation.1 | async-start | bytes 65536 | tf_op jit(solution)/shard_map/all_to_all | solution.py:763
  26.8 0.1 collective-permute-start.4
  26.9 2.6 %collective-permute-start.5 = (f32[6,8,1,128]{3,2,1,0:T(1,128)S(1)}, f32[6,8,1,128]{3,2,1,0:T(1,128)S(1)}, u32[]{:S(2)}, u32[]{:S(2)}) collective-permute-start(f32[6,8,1,128]{3,2,1,0:T(1,128)S(1)} %get-tuple-element.41), channel_id=1, source_target_pairs={{8,16},{16,8},{24,0},{0,24},{9,17},{17,9},{25,1},{1,25},{10,18},{1... | collective-permute-start | bytes 73736 | tf_op jit(solution)/shard_map/ppermute | solution.py:727
  29.5 0.9 %stream_flow.1.flow_in = f32[19,8,8,128]{3,2,1,0:T(8,128)} custom-call(f32[19,10,8,128]{3,2,1,0:T(8,128)S(1)} %get-tuple-element.42.postf_ref), custom_call_target="tpu_custom_call" | custom-call | tf_op jit(solution)/shard_map/stream_flow/pallas_call | solution.py:751
  30.4 1.2 %all-to-all-done.1.chunks_ref = f32[8,8,128]{2,1,0:T(8,128)S(1)} async-done(((f32[8,8,128]{2,1,0:T(8,128)}), f32[8,8,128]{2,1,0:T(8,128)S(1)}, u32[]{:S(2)}, u32[]{:S(2)}) %all-to-all-start.1) | async-done | bytes 32800 | tf_op jit(solution)/shard_map/all_to_all | solution.py:763
  31.6 1.1 %stream_heat.1 = (f32[7,8,8,128]{3,2,1,0:T(8,128)}, f32[1,256]{1,0:T(1,128)}, f32[16,128]{1,0:T(8,128)S(1)}) custom-call(f32[7,10,8,128]{3,2,1,0:T(8,128)S(1)} %get-tuple-element.37.posth_ref, f32[30,8,128]{2,1,0:T(8,128)S(1)} %collective-permute-done.recva_ref, f32[30,8,128]{2,1,0:T(8,128)S(1)} %collective-permute-done.1.recvb_ref, ...), custom_call_target="tpu_custom_call" | custom-call | tf_op jit(solution)/shard_map/stream_heat/pallas_call | solution.py:751
  32.8 0.0 collective-permute-done.4.lasta_ref
  32.8 0.0 collective-permute-done.5.lastb_ref
  32.8 0.8 %stream_edges.1 = (f32[19,8,8,128]{3,2,1,0:T(8,128)}, f32[7,8,8,128]{3,2,1,0:T(8,128)}) custom-call(f32[16,128]{1,0:T(8,128)S(1)} %get-tuple-element.39.row_ref, f32[6,8,1,128]{3,2,1,0:T(1,128)S(1)} %collective-permute-done.4.lasta_ref, f32[6,8,1,128]{3,2,1,0:T(1,128)S(1)} %collective-permute-done.5.lastb_ref, ...), custom_call_target="tpu_custom_call", output_to_operand_aliasing={{0}: (3, {}), {1}: (4, {})} | custom-call | tf_op jit(solution)/shard_map/stream_edges/pallas_call | solution.py:751
Async XLA Ops:
  1.3 13.1 %copy-start = (f32[256,256]{1,0:T(8,128)S(1)}, f32[256,256]{1,0:T(8,128)}, u32[]{:S(2)}) copy-start(f32[256,256]{1,0:T(8,128)} %conduction_ref.3) | copy-start | bytes 786436
  3.1 11.3 %collective-permute-start = (f32[30,8,128]{2,1,0:T(8,128)S(1)}, f32[30,8,128]{2,1,0:T(8,128)S(1)}, u32[]{:S(2)}, u32[]{:S(2)}) collective-permute-start(f32[30,8,128]{2,1,0:T(8,128)S(1)} %get-tuple-element.27), channel_id=1, source_target_pairs={{0,1},{1,0},{2,3},{3,2},{4,5},{5,4},{6,7},{7,6},{8,9},{9,8},{10,11... | collective-permute-start | bytes 368648 | tf_op jit(solution)/shard_map/ppermute | solution.py:727
  3.6 10.8 %collective-permute-start.1 = (f32[30,8,128]{2,1,0:T(8,128)S(1)}, f32[30,8,128]{2,1,0:T(8,128)S(1)}, u32[]{:S(2)}, u32[]{:S(2)}) collective-permute-start(f32[30,8,128]{2,1,0:T(8,128)S(1)} %get-tuple-element.28), channel_id=1, source_target_pairs={{1,2},{2,1},{3,4},{4,3},{5,6},{6,5},{7,0},{0,7},{9,10},{10,9},{11,... | collective-permute-start | bytes 368648 | tf_op jit(solution)/shard_map/ppermute | solution.py:727
  14.9 4.1 %collective-permute-start.2 = (f32[80,128]{1,0:T(8,128)S(1)}, f32[80,128]{1,0:T(8,128)S(1)}, u32[]{:S(2)}, u32[]{:S(2)}) collective-permute-start(f32[80,128]{1,0:T(8,128)S(1)} %get-tuple-element.32), channel_id=1, source_target_pairs={{0,8},{8,0},{16,24},{24,16},{1,9},{9,1},{17,25},{25,17},{2,10},{10... | collective-permute-start | bytes 122888 | tf_op jit(solution)/shard_map/ppermute | solution.py:727
  16.5 5.8 %collective-permute-start.3 = (f32[80,128]{1,0:T(8,128)S(1)}, f32[80,128]{1,0:T(8,128)S(1)}, u32[]{:S(2)}, u32[]{:S(2)}) collective-permute-start(f32[80,128]{1,0:T(8,128)S(1)} %get-tuple-element.33), channel_id=1, source_target_pairs={{8,16},{16,8},{24,0},{0,24},{9,17},{17,9},{25,1},{1,25},{10,18},{1... | collective-permute-start | bytes 122888 | tf_op jit(solution)/shard_map/ppermute | solution.py:727
  23.5 8.1 %all-to-all-start.1 = ((f32[8,8,128]{2,1,0:T(8,128)}), f32[8,8,128]{2,1,0:T(8,128)S(1)}, u32[]{:S(2)}, u32[]{:S(2)}) async-start(f32[8,8,128]{2,1,0:T(8,128)} %get-tuple-element.38), calls=%async_computation.1 | async-start | bytes 65536 | tf_op jit(solution)/shard_map/all_to_all | solution.py:763
  26.8 5.9 %collective-permute-start.4 = (f32[6,8,1,128]{3,2,1,0:T(1,128)S(1)}, f32[6,8,1,128]{3,2,1,0:T(1,128)S(1)}, u32[]{:S(2)}, u32[]{:S(2)}) collective-permute-start(f32[6,8,1,128]{3,2,1,0:T(1,128)S(1)} %get-tuple-element.40), channel_id=1, source_target_pairs={{0,8},{8,0},{16,24},{24,16},{1,9},{9,1},{17,25},{25,17},{2,10},{10... | collective-permute-start | bytes 73736 | tf_op jit(solution)/shard_map/ppermute | solution.py:727
  26.9 5.9 %collective-permute-start.5 = (f32[6,8,1,128]{3,2,1,0:T(1,128)S(1)}, f32[6,8,1,128]{3,2,1,0:T(1,128)S(1)}, u32[]{:S(2)}, u32[]{:S(2)}) collective-permute-start(f32[6,8,1,128]{3,2,1,0:T(1,128)S(1)} %get-tuple-element.41), channel_id=1, source_target_pairs={{8,16},{16,8},{24,0},{0,24},{9,17},{17,9},{25,1},{1,25},{10,18},{1... | collective-permute-start | bytes 73736 | tf_op jit(solution)/shard_map/ppermute | solution.py:727

commit v5 on v4

--- a/solution.py
+++ b/solution.py
@@ -238,9 +238,6 @@
     return [post[k] + WEIGHT_HEAT[k] * lost for k in range(HEATS)]
 
 
-STRIPS = 4
-
-
 def first_kernel(
     count_ref,
     flow_hbm,
@@ -268,7 +265,6 @@
     sems,
 ):
     wide = flow_ref.shape[1]
-    strip = wide // STRIPS
     odd = lax.axis_index("blk") % 2 == 1
     small = [
         pltpu.make_async_copy(source, target, sems.at[n])
@@ -283,15 +279,8 @@
             )
         )
     ]
-    strips = [
-        pltpu.make_async_copy(
-            flow_hbm.at[:, pl.ds(n * strip, strip)],
-            flow_ref.at[:, pl.ds(n * strip, strip)],
-            sems.at[len(small) + n],
-        )
-        for n in range(STRIPS)
-    ]
-    for copy in small + strips:
+    large = pltpu.make_async_copy(flow_hbm, flow_ref, sems.at[len(small)])
+    for copy in small + [large]:
         copy.start()
     for copy in small:
         copy.wait()
@@ -307,9 +296,8 @@
         counts_ref,
     )
     solid_ref[...] = mask_ref[...].astype(F32)
+    large.wait()
     for x in range(wide):
-        if x % strip == 0:
-            strips[x // strip].wait()
         flow = [flow_ref[i, x] for i in range(FLOWS)]
         heat = [heat_ref[k, x] for k in range(HEATS)]
         solid = mask_ref[x] != 0
@@ -427,8 +415,8 @@
     list_ref,
     chunks_ref,
     conduction_ref,
-    senda_ref,
-    sendb_ref,
+    up_ref,
+    down_ref,
     metal_ref,
     source_ref,
 ):
@@ -452,27 +440,17 @@
     source_ref[wide + 2 :] = give_planes(found[1], after[2], 0, 2, deep)
     get = planes(postf_ref, posth_ref, low, high, wide, source_ref)
 
-    def fill(up_ref, down_ref):
-        for ref, comps, row in ((up_ref, UP, deep - 1), (down_ref, DOWN, 0)):
-            for j in range(wide + 2):
-                for n, i in enumerate(comps):
-                    value = get(i, j - 1 - VELOCITY[i][0])
-                    at = j * EDGES + n
-                    ref[at : at + 1, :] = value[row : row + 1, :]
-            at = (wide + 2) * EDGES
-            put_rows(ref, at, metal)
-            ref[at + 2 : at + 2 + LIST_ROWS, :] = list_ref[0:LIST_ROWS]
-
-    for ref in (senda_ref, sendb_ref):
+    for ref in (up_ref, down_ref):
         ref[ref.shape[0] - 8 :, :] = jnp.zeros((8, lanes), F32)
-
-    @pl.when(lax.axis_index("span") % 2 == 1)
-    def _():
-        fill(sendb_ref, senda_ref)
-
-    @pl.when(lax.axis_index("span") % 2 == 0)
-    def _():
-        fill(senda_ref, sendb_ref)
+    for ref, comps, row in ((up_ref, UP, deep - 1), (down_ref, DOWN, 0)):
+        for j in range(wide + 2):
+            for n, i in enumerate(comps):
+                value = get(i, j - 1 - VELOCITY[i][0])
+                at = j * EDGES + n
+                ref[at : at + 1, :] = value[row : row + 1, :]
+        at = (wide + 2) * EDGES
+        put_rows(ref, at, metal)
+        ref[at + 2 : at + 2 + LIST_ROWS, :] = list_ref[0:LIST_ROWS]
 
 
 def stream(get, edge, deep, i, x):
@@ -489,15 +467,11 @@
     return value
 
 
-def edge_rows(odd, a_ref, b_ref, first):
+def edge_rows(low_ref, high_ref, first):
     def edge(i, x):
-        comps = UP if VELOCITY[i][2] == 1 else DOWN
+        ref, comps = (low_ref, UP) if VELOCITY[i][2] == 1 else (high_ref, DOWN)
         at = (x - first) * EDGES + comps.index(i)
-        a = a_ref[at : at + 1, :]
-        b = b_ref[at : at + 1, :]
-        if VELOCITY[i][2] == 1:
-            return jnp.where(odd, a, b)
-        return jnp.where(odd, b, a)
+        return ref[at : at + 1, :]
 
     return edge
 
@@ -508,8 +482,8 @@
     recva_ref,
     recvb_ref,
     source_ref,
-    edgea_ref,
-    edgeb_ref,
+    low_edge_ref,
+    high_edge_ref,
     list_ref,
     metal_ref,
     solid_ref,
@@ -517,8 +491,8 @@
     chunks_hbm,
     outf_ref,
     outh_ref,
-    senda_ref,
-    sendb_ref,
+    up_ref,
+    down_ref,
     out_ref,
     sem,
 ):
@@ -526,8 +500,7 @@
     blocks = out_ref.shape[0]
     low, high = sides(lax.axis_index("blk") % 2 == 1, recva_ref, recvb_ref)
     get = planes(None, posth_ref, low, high, wide, source_ref)
-    odd = lax.axis_index("span") % 2 == 1
-    edge = edge_rows(odd, edgea_ref, edgeb_ref, -1)
+    edge = edge_rows(low_edge_ref, high_edge_ref, -1)
     tempers = []
     for x in range(-1, wide + 1):
         temper = None
@@ -543,12 +516,11 @@
     row_mask = rows_of(owner * 2 + (cell >> 7), 2 * blocks)
     sums = add_up(wall, row_mask, hot(rows_of(cell & 127, lanes)))
     at = (wide + 2) * EDGES
-    a = edgea_ref[at : at + 2, :]
-    b = edgeb_ref[at : at + 2, :]
+    below, above = low_edge_ref[at : at + 2, :], high_edge_ref[at : at + 2, :]
     for d in range(blocks):
         out_ref[d, 0:2, :] = metal_ref[0:2]
-        out_ref[d, 2:4, :] = jnp.where(odd, a, b)
-        out_ref[d, 4:6, :] = jnp.where(odd, b, a)
+        out_ref[d, 2:4, :] = below
+        out_ref[d, 4:6, :] = above
         out_ref[d, 6:8, :] = sums[2 * d : 2 * d + 2]
     copy = pltpu.make_async_copy(out_ref, chunks_hbm, sem)
     copy.start()
@@ -572,23 +544,14 @@
         for k in range(HEATS):
             outh_ref[k, x + 1] = posth[k]
 
-    def fill(up_ref, down_ref):
-        for ref, comps, row in ((up_ref, UP, deep - 1), (down_ref, DOWN, 0)):
-            for x in range(wide):
-                for n, i in enumerate(comps):
-                    at = x + 1 - VELOCITY[i][0]
-                    value = outf_ref[i, at] if i < FLOWS else outh_ref[i - FLOWS, at]
-                    cy = VELOCITY[i][1]
-                    value = pltpu.roll(value, cy % lanes, 1) if cy else value
-                    ref[n, x] = value[row : row + 1, :]
-
-    @pl.when(lax.axis_index("span") % 2 == 1)
-    def _():
-        fill(sendb_ref, senda_ref)
-
-    @pl.when(lax.axis_index("span") % 2 == 0)
-    def _():
-        fill(senda_ref, sendb_ref)
+    for ref, comps, row in ((up_ref, UP, deep - 1), (down_ref, DOWN, 0)):
+        for x in range(wide):
+            for n, i in enumerate(comps):
+                at = x + 1 - VELOCITY[i][0]
+                value = outf_ref[i, at] if i < FLOWS else outh_ref[i - FLOWS, at]
+                cy = VELOCITY[i][1]
+                value = pltpu.roll(value, cy % lanes, 1) if cy else value
+                ref[n, x] = value[row : row + 1, :]
 
     copy.wait()
 
@@ -625,27 +588,20 @@
     recvb_ref,
     list_ref,
     chunks_ref,
-    edgea_ref,
-    edgeb_ref,
+    low_edge_ref,
+    high_edge_ref,
     metal_ref,
     conduction_ref,
-    heat_hbm,
-    metal_hbm,
-    row_ref,
     heat_ref,
     out_ref,
-    sems,
+    row_ref,
 ):
     blocks = chunks_ref.shape[0]
     wide, deep, lanes = heat_ref.shape[1:]
-    odd = lax.axis_index("span") % 2 == 1
     sums = chunks_ref[0]
     for d in range(1, blocks):
         sums = sums + chunks_ref[d]
     out_ref[...] = next_metal(conduction_ref[...], metal_ref[0:2], sums[6:8], metal_ref[2:4])
-    copies = [pltpu.make_async_copy(out_ref, metal_hbm, sems.at[0])]
-    copies[0].start()
-
     low, high = sides(lax.axis_index("blk") % 2 == 1, recva_ref, recvb_ref)
     own, before, after = lists_of(list_ref[...]), side_lists(low), side_lists(high)
     inner = metal_at(metal_rows(chunks_ref, 0), own)[0]
@@ -659,63 +615,61 @@
         for x in range(wide):
             at = x + 1 - VELOCITY[i][0]
             heat_ref[k, x] = shift(posth_ref[k, at] + WEIGHT_HEAT[k] * source[at], i)
-    copies.append(pltpu.make_async_copy(heat_ref, heat_hbm, sems.at[1]))
-    copies[1].start()
 
     at = (wide + 2) * EDGES + 2
-    a = edgea_ref[at : at + LIST_ROWS, :]
-    b = edgeb_ref[at : at + LIST_ROWS, :]
-    for n, (block, moved, z) in enumerate(
-        ((jnp.where(odd, a, b), 2, deep - 1), (jnp.where(odd, b, a), 4, 0))
-    ):
-        lists = lists_of(block)
+    for n, (ref, moved, z) in enumerate(((low_edge_ref, 2, deep - 1), (high_edge_ref, 4, 0))):
+        lists = lists_of(ref[at : at + LIST_ROWS, :])
         column = lists[2] >> 7
         row = jnp.where(lax.rem(column, deep) == z, lax.div(column, deep), -1)
         found = metal_at(metal_rows(chunks_ref, moved), lists)[0]
         row_ref[n * wide : (n + 1) * wide] = give(found, row, lists[2], wide)
-    for copy in copies:
-        copy.wait()
 
 
 def edge_kernel(
+    heat_ref,
+    metal_ref,
     row_ref,
-    lasta_ref,
-    lastb_ref,
+    low_ref,
+    high_ref,
     flow_in,
-    heat_in,
     flow_hbm,
     heat_hbm,
-    rows_ref,
+    metal_hbm,
+    tilted_ref,
     sems,
 ):
     wide, deep, lanes = flow_hbm.shape[1:]
-
-    def fill(low_ref, high_ref):
-        copies = []
-        for m, (ref, comps, z) in enumerate(((low_ref, UP, 0), (high_ref, DOWN, deep - 1))):
-            for n, i in enumerate(comps):
-                if i < FLOWS:
-                    source, target = ref.at[n], flow_hbm.at[i]
-                else:
-                    source, target = rows_ref.at[m], heat_hbm.at[i - FLOWS]
-                    for x in range(wide):
-                        given = row_ref[m * wide + x : m * wide + x + 1, :]
-                        rows_ref[m, x] = ref[n, x] + WEIGHT_HEAT[i - FLOWS] * given
-                copy = pltpu.make_async_copy(
-                    source, target.at[:, z : z + 1, :], sems.at[m * EDGES + n]
+    level = HEATS - 2
+    sublane = lax.broadcasted_iota(jnp.int32, (deep, lanes), 0)
+
+    copies = [
+        pltpu.make_async_copy(
+            heat_ref.at[pl.ds(0, level)], heat_hbm.at[pl.ds(0, level)], sems.at[0]
+        ),
+        pltpu.make_async_copy(metal_ref, metal_hbm, sems.at[1]),
+    ]
+    for m, (ref, comps, z) in enumerate(((low_ref, UP, 0), (high_ref, DOWN, deep - 1))):
+        for n, i in enumerate(comps[:-1]):
+            copies.append(
+                pltpu.make_async_copy(
+                    ref.at[n],
+                    flow_hbm.at[i, :, z : z + 1, :],
+                    sems.at[3 + m * EDGES + n],
                 )
-                copy.start()
-                copies.append(copy)
-        for copy in copies:
-            copy.wait()
-
-    @pl.when(lax.axis_index("span") % 2 == 1)
-    def _():
-        fill(lasta_ref, lastb_ref)
-
-    @pl.when(lax.axis_index("span") % 2 == 0)
-    def _():
-        fill(lastb_ref, lasta_ref)
+            )
+    for copy in copies:
+        copy.start()
+    for m, (ref, comps, z) in enumerate(((low_ref, UP, 0), (high_ref, DOWN, deep - 1))):
+        for x in range(wide):
+            given = row_ref[m * wide + x : m * wide + x + 1, :]
+            row = ref[EDGES - 1, x] + WEIGHT_HEAT[level + m] * given
+            tilted_ref[m, x] = jnp.where(sublane == z, row, heat_ref[level + m, x])
+    copies.append(
+        pltpu.make_async_copy(tilted_ref, heat_hbm.at[pl.ds(level, 2)], sems.at[2])
+    )
+    copies[-1].start()
+    for copy in copies:
+        copy.wait()
 
 
 def swap(value, axis, offset):
@@ -725,6 +679,12 @@
         one, other = first % count, (first + 1) % count
         pairs += [(one, other), (other, one)]
     return lax.ppermute(value, axis, pairs)
+
+
+def shift_both(up, down, axis):
+    count = lax.axis_size(axis)
+    ahead = [(i, (i + 1) % count) for i in range(count)]
+    return lax.ppermute(up, axis, ahead), lax.ppermute(down, axis, [(j, i) for i, j in ahead])
 
 
 def local(
@@ -786,7 +746,7 @@
             pltpu.VMEM(wall_node.shape, jnp.int32),
             pltpu.VMEM(wall_node.shape, jnp.int32),
             pltpu.VMEM(wall_node.shape, jnp.int32),
-            pltpu.SemaphoreType.DMA((6 + STRIPS,)),
+            pltpu.SemaphoreType.DMA((7,)),
         ],
     )
     chunks = to_all(chunks)
@@ -794,7 +754,7 @@
     recvb = swap(sendb, "blk", 1)
     edge_count = -(-((wide + 2) * EDGES + 2 + LIST_ROWS) // 8) * 8
     edges = shape(edge_count, lanes)
-    senda, sendb, metal, source = call(
+    up, down, metal, source = call(
         source_kernel,
         "source_first",
         (edges, edges, shape(8, lanes), shape(wide + 4, deep, lanes)),
@@ -807,11 +767,10 @@
         chunks,
         conduction,
     )
-    edgea = swap(senda, "span", 0)
-    edgeb = swap(sendb, "span", 1)
+    low_edge, high_edge = shift_both(up, down, "span")
     edges = shape(EDGES, wide, 1, lanes)
     chunk = shape(blocks, 8, lanes)
-    chunks, postf, posth, senda, sendb = call(
+    chunks, postf, posth, up, down = call(
         step_kernel,
         "collide_second",
         (
@@ -827,8 +786,8 @@
         recva,
         recvb,
         source,
-        edgea,
-        edgeb,
+        low_edge,
+        high_edge,
         lists,
         metal,
         solid,
@@ -837,8 +796,7 @@
         out_spec=(hbm,) + (near_spec,) * 4,
     )
     chunks = to_all(chunks)
-    lasta = swap(senda, "span", 0)
-    lastb = swap(sendb, "span", 1)
+    low_last, high_last = shift_both(up, down, "span")
     part = call(
         stream_kernel,
         "stream_flow",
@@ -858,36 +816,30 @@
         recvb,
         lists,
         chunks,
-        edgea,
-        edgeb,
+        low_edge,
+        high_edge,
         metal,
         conduction,
+    )
+    return call(
+        edge_kernel,
+        "write_last",
+        (flows, heats, shape(*metal_temp.shape)),
+        (),
+        heat,
+        metal,
+        rows,
+        low_last,
+        high_last,
+        part,
+        far=1,
         scratch=[
-            pltpu.VMEM(heats.shape, F32),
-            pltpu.VMEM(metal_temp.shape, F32),
-            pltpu.SemaphoreType.DMA((2,)),
+            pltpu.VMEM((2, wide, deep, lanes), F32),
+            pltpu.SemaphoreType.DMA((3 + 2 * EDGES,)),
         ],
-        out_spec=(hbm, hbm, near_spec),
-    )
-    flow, heat = call(
-        edge_kernel,
-        "stream_edges",
-        (flows, heats),
-        (),
-        rows,
-        lasta,
-        lastb,
-        part,
-        heat,
-        far=2,
-        scratch=[
-            pltpu.VMEM((2, wide, 1, lanes), F32),
-            pltpu.SemaphoreType.DMA((2 * EDGES,)),
-        ],
-        out_spec=(hbm, hbm),
-        alias={3: 0, 4: 1},
-    )
-    return (flow, heat, metal)
+        out_spec=(hbm,) * 3,
+        alias={5: 0},
+    )
 
 
 def solution(mesh):

time: 33.8 us -> 32.2 us (0.953)
  waiting for transfers between devices: 4.48 us -> 2.59 us
  starting transfers between devices: 14.2 us -> 15.1 us
  Pallas kernels: 6.31 us -> 5.71 us
    ppermute x0 -> x4, starting transfers between devices: none -> 7.71 us  [the longest x2 4.93 us: shift_both(): lax.ppermute(down, axis, [(j, i) for i, j in ahead])]
    ppermute x6 -> x2, starting transfers between devices: 10.8 us -> 4.07 us  [swap(): return lax.ppermute(value, axis, pairs)]
    ppermute x6 -> x2, waiting for transfers between devices: 3.3 us -> 0.01 us  [swap(): return lax.ppermute(value, axis, pairs)]
    ppermute x0 -> x4, waiting for transfers between devices: none -> 2.58 us  [the longest x2 2.51 us: shift_both(): lax.ppermute(up, axis, ahead)]
    all_to_all x1, waiting for transfers between devices: 1.18 us -> 0.01 us  [to_all(): return lax.all_to_all(chunks, 'blk', 0, 0, tiled=True)]
    pallas_call x6, Pallas kernels: 6.31 us -> 5.71 us  [call(): pl.pallas_call(kernel, in_specs=[smem] * len(scalars) + in_vmem(near) + [...]
  transfers between devices with their start and end apart: 7 -> 7, of which waited for: 2 -> 3; matrix products, arithmetic and copies ran while one was open for 0% -> 0% of each run, Pallas kernels for 6% -> 4%
where the time goes in v5:
time: 32.2 us; the launch traced here: 32 us
  starting transfers between devices  15.1 us (47%)
  blocking collectives  7.2 us (22%)
  Pallas kernels  5.71 us (18%)
  waiting for transfers between devices  2.59 us (8%)
  between operations  1.34 us (4%)
    all_to_all x1, blocking collectives, to_all(): return lax.all_to_all(chunks, 'blk', 0, 0, tiled=True)  7.2 us
    pallas_call x6, Pallas kernels, call(): pl.pallas_call(kernel, in_specs=[smem] * len(scalars) + in_vmem(near) + [...  5.71 us
    ppermute x2, starting transfers between devices, shift_both(): lax.ppermute(down, axis, [(j, i) for i, j in ahead])  4.93 us
    ppermute x2, starting transfers between devices, swap(): return lax.ppermute(value, axis, pairs)  4.07 us
    all_to_all x1, starting transfers between devices, to_all(): return lax.all_to_all(chunks, 'blk', 0, 0, tiled=True)  3.35 us
    ppermute x2, starting transfers between devices, shift_both(): lax.ppermute(up, axis, ahead)  2.77 us
    ppermute x2, waiting for transfers between devices, shift_both(): lax.ppermute(up, axis, ahead)  2.51 us
  transfers between devices with their start and end apart: 7, of which 3 were waited for; matrix products, arithmetic and copies ran while one was open for 0% of the time, Pallas kernels for 4%

profile of v5, /device:TPU:0, one launch (start us, length us, event | category | flops | bytes accessed | tf_op | source)
XLA Modules:
  0.0 32.0 jit_solution(12842266438437363805)
XLA Ops:
  1.3 0.0 copy-start
  1.3 1.8 %collide_first.1 = (f32[8,8,128]{2,1,0:T(8,128)S(1)}, f32[16,128]{1,0:T(8,128)S(1)}, f32[8,8,128]{2,1,0:T(8,128)S(1)}, f32[8,8,128]{2,1,0:T(8,128)S(1)}, f32[19,...) custom-call(s32[1,1]{1,0:T(1,128)S(6)} %copy.14.count_ref, ...), custom_call_target="tpu_custom_call" | custom-call | tf_op jit(solution)/shard_map/collide_first/pallas_call | solution.py:711
  3.1 0.5 %collective-permute-start = (f32[30,8,128]{2,1,0:T(8,128)S(1)}, f32[30,8,128]{2,1,0:T(8,128)S(1)}, u32[]{:S(2)}, u32[]{:S(2)}) collective-permute-start(f32[30,8,128]{2,1,0:T(8,128)S(1)} %get-tuple-element.25), channel_id=1, source_target_pairs={{0,1},{1,0},{2,3},{3,2},{4,5},{5,4},{6,7},{7,6},{8,9},{9,8},{10,11... | collective-permute-start | bytes 368648 | tf_op jit(solution)/shard_map/ppermute | solution.py:681
  3.6 3.6 %collective-permute-start.1 = (f32[30,8,128]{2,1,0:T(8,128)S(1)}, f32[30,8,128]{2,1,0:T(8,128)S(1)}, u32[]{:S(2)}, u32[]{:S(2)}) collective-permute-start(f32[30,8,128]{2,1,0:T(8,128)S(1)} %get-tuple-element.26), channel_id=1, source_target_pairs={{1,2},{2,1},{3,4},{4,3},{5,6},{6,5},{7,0},{0,7},{9,10},{10,9},{11,... | collective-permute-start | bytes 368648 | tf_op jit(solution)/shard_map/ppermute | solution.py:681
  7.2 7.2 %all_to_all.10.chunks_ref = f32[8,8,128]{2,1,0:T(8,128)S(1)} all-to-all(f32[8,8,128]{2,1,0:T(8,128)S(1)} %get-tuple-element.28), channel_id=1, replica_groups=mesh['span'=4,'blk'=8] {'blk'}, dimensions={0} | all-to-all | bytes 65536 | tf_op jit(solution)/shard_map/all_to_all | solution.py:723
  14.4 0.0 collective-permute-done.recva_ref
  14.4 0.0 collective-permute-done.1.recvb_ref
  14.4 0.0 copy-done
  14.4 0.4 %source_first.1 = (f32[80,128]{1,0:T(8,128)S(1)}, f32[80,128]{1,0:T(8,128)S(1)}, f32[8,128]{1,0:T(8,128)S(1)}, f32[12,8,128]{2,1,0:T(8,128)S(1)}) custom-call(f32[19,8,8,128]{3,2,1,0:T(8,128)S(1)} %get-tuple-element.23.postf_ref, f32[7,8,8,128]{3,2,1,0:T(8,128)S(1)} %get-tuple-element.24.posth_ref, f32[30,8,128]{2,1,0:T(8,128)S(1)} %collective-permute-done.recva_ref, ...), custom_call_target="tpu_custom_call" | custom-call | tf_op jit(solution)/shard_map/source_first/pallas_call | solution.py:711
  14.8 1.6 %collective-permute-start.2 = (f32[80,128]{1,0:T(8,128)S(1)}, f32[80,128]{1,0:T(8,128)S(1)}, u32[]{:S(2)}, u32[]{:S(2)}) collective-permute-start(f32[80,128]{1,0:T(8,128)S(1)} %get-tuple-element.30), channel_id=1, source_target_pairs={{0,8},{8,16},{16,24},{24,0},{1,9},{9,17},{17,25},{25,1},{2,10},{10... | collective-permute-start | bytes 122888 | tf_op jit(solution)/shard_map/ppermute | solution.py:687
  16.4 2.2 %collective-permute-start.3 = (f32[80,128]{1,0:T(8,128)S(1)}, f32[80,128]{1,0:T(8,128)S(1)}, u32[]{:S(2)}, u32[]{:S(2)}) collective-permute-start(f32[80,128]{1,0:T(8,128)S(1)} %get-tuple-element.31), channel_id=1, source_target_pairs={{8,0},{16,8},{24,16},{0,24},{9,1},{17,9},{25,17},{1,25},{10,2},{18... | collective-permute-start | bytes 122888 | tf_op jit(solution)/shard_map/ppermute | solution.py:687
  18.6 2.1 %collective-permute-done.2.low_edge_ref = f32[80,128]{1,0:T(8,128)S(1)} collective-permute-done((f32[80,128]{1,0:T(8,128)S(1)}, f32[80,128]{1,0:T(8,128)S(1)}, u32[]{:S(2)}, u32[]{:S(2)}) %collective-permute-start.2) | collective-permute-done | bytes 40992 | tf_op jit(solution)/shard_map/ppermute | solution.py:687
  20.8 0.1 collective-permute-done.3.high_edge_ref
  20.8 1.2 %collide_second.1 = (f32[8,8,128]{2,1,0:T(8,128)}, f32[19,10,8,128]{3,2,1,0:T(8,128)S(1)}, f32[7,10,8,128]{3,2,1,0:T(8,128)S(1)}, f32[6,8,1,128]{3,2,1,0:T(1,128)S(1)}, f32[6,8,1,128]{3,2,1,0:T(1,128)S(1)}) custom-call(f32[19,8,8,128]{3,2,1,0:T(8,128)S(1)} %get-tuple-element.23.postf_ref, f32[7,8,8,128]{3,2,1,0:T(8,128)S(1)} %get-tuple-element.24.posth_ref, ...), custom_call_target="tpu_custom_call" | custom-call | tf_op jit(solution)/shard_map/collide_second/pallas_call | solution.py:711
  22.1 3.4 %all-to-all-start.1 = ((f32[8,8,128]{2,1,0:T(8,128)}), f32[8,8,128]{2,1,0:T(8,128)S(1)}, u32[]{:S(2)}, u32[]{:S(2)}) async-start(f32[8,8,128]{2,1,0:T(8,128)} %get-tuple-element.36), calls=%async_computation.1 | async-start | bytes 65536 | tf_op jit(solution)/shard_map/all_to_all | solution.py:723
  25.4 1.2 %collective-permute-start.4 = (f32[6,8,1,128]{3,2,1,0:T(1,128)S(1)}, f32[6,8,1,128]{3,2,1,0:T(1,128)S(1)}, u32[]{:S(2)}, u32[]{:S(2)}) collective-permute-start(f32[6,8,1,128]{3,2,1,0:T(1,128)S(1)} %get-tuple-element.40), channel_id=1, source_target_pairs={{0,8},{8,16},{16,24},{24,0},{1,9},{9,17},{17,25},{25,1},{2,10},{10... | collective-permute-start | bytes 73736 | tf_op jit(solution)/shard_map/ppermute | solution.py:687
  26.6 2.7 %collective-permute-start.5 = (f32[6,8,1,128]{3,2,1,0:T(1,128)S(1)}, f32[6,8,1,128]{3,2,1,0:T(1,128)S(1)}, u32[]{:S(2)}, u32[]{:S(2)}) collective-permute-start(f32[6,8,1,128]{3,2,1,0:T(1,128)S(1)} %get-tuple-element.41), channel_id=1, source_target_pairs={{8,0},{16,8},{24,16},{0,24},{9,1},{17,9},{25,17},{1,25},{10,2},{18... | collective-permute-start | bytes 73736 | tf_op jit(solution)/shard_map/ppermute | solution.py:687
  29.3 0.9 %stream_flow.1.flow_in = f32[19,8,8,128]{3,2,1,0:T(8,128)} custom-call(f32[19,10,8,128]{3,2,1,0:T(8,128)S(1)} %get-tuple-element.42.postf_ref), custom_call_target="tpu_custom_call" | custom-call | tf_op jit(solution)/shard_map/stream_flow/pallas_call | solution.py:711
  30.2 0.0 all-to-all-done.1.chunks_ref
  30.3 0.5 %stream_heat.1 = (f32[7,8,8,128]{3,2,1,0:T(8,128)S(1)}, f32[1,256]{1,0:T(1,128)S(1)}, f32[16,128]{1,0:T(8,128)S(1)}) custom-call(f32[7,10,8,128]{3,2,1,0:T(8,128)S(1)} %get-tuple-element.35.posth_ref, f32[30,8,128]{2,1,0:T(8,128)S(1)} %collective-permute-done.recva_ref, f32[30,8,128]{2,1,0:T(8,128)S(1)} %collective-permute-done.1.recvb_ref, ...), custom_call_target="tpu_custom_call" | custom-call | tf_op jit(solution)/shard_map/stream_heat/pallas_call | solution.py:711
  30.7 0.4 %collective-permute-done.4.low_ref = f32[6,8,1,128]{3,2,1,0:T(1,128)S(1)} collective-permute-done((f32[6,8,1,128]{3,2,1,0:T(1,128)S(1)}, f32[6,8,1,128]{3,2,1,0:T(1,128)S(1)}, u32[]{:S(2)}, u32[]{:S(2)}) %collective-permute-start.4) | collective-permute-done | bytes 24608 | tf_op jit(solution)/shard_map/ppermute | solution.py:687
  31.1 0.0 collective-permute-done.5.high_ref
  31.1 0.9 %write_last.1 = (f32[19,8,8,128]{3,2,1,0:T(8,128)}, f32[7,8,8,128]{3,2,1,0:T(8,128)}, f32[1,256]{1,0:T(1,128)}) custom-call(f32[7,8,8,128]{3,2,1,0:T(8,128)S(1)} %get-tuple-element.37.heat_ref, f32[1,256]{1,0:T(1,128)S(1)} %get-tuple-element.38.metal_ref, f32[16,128]{1,0:T(8,128)S(1)} %get-tuple-element.39.row_ref, ...), custom_call_target="tpu_custom_call", output_to_operand_aliasing={{0}: (5, {})} | custom-call | tf_op jit(solution)/shard_map/write_last/pallas_call | solution.py:711
Async XLA Ops:
  1.3 13.1 %copy-start = (f32[256,256]{1,0:T(8,128)S(1)}, f32[256,256]{1,0:T(8,128)}, u32[]{:S(2)}) copy-start(f32[256,256]{1,0:T(8,128)} %conduction_ref.3) | copy-start | bytes 786436
  3.1 11.3 %collective-permute-start = (f32[30,8,128]{2,1,0:T(8,128)S(1)}, f32[30,8,128]{2,1,0:T(8,128)S(1)}, u32[]{:S(2)}, u32[]{:S(2)}) collective-permute-start(f32[30,8,128]{2,1,0:T(8,128)S(1)} %get-tuple-element.25), channel_id=1, source_target_pairs={{0,1},{1,0},{2,3},{3,2},{4,5},{5,4},{6,7},{7,6},{8,9},{9,8},{10,11... | collective-permute-start | bytes 368648 | tf_op jit(solution)/shard_map/ppermute | solution.py:681
  3.6 10.8 %collective-permute-start.1 = (f32[30,8,128]{2,1,0:T(8,128)S(1)}, f32[30,8,128]{2,1,0:T(8,128)S(1)}, u32[]{:S(2)}, u32[]{:S(2)}) collective-permute-start(f32[30,8,128]{2,1,0:T(8,128)S(1)} %get-tuple-element.26), channel_id=1, source_target_pairs={{1,2},{2,1},{3,4},{4,3},{5,6},{6,5},{7,0},{0,7},{9,10},{10,9},{11,... | collective-permute-start | bytes 368648 | tf_op jit(solution)/shard_map/ppermute | solution.py:681
  14.8 6.0 %collective-permute-start.2 = (f32[80,128]{1,0:T(8,128)S(1)}, f32[80,128]{1,0:T(8,128)S(1)}, u32[]{:S(2)}, u32[]{:S(2)}) collective-permute-start(f32[80,128]{1,0:T(8,128)S(1)} %get-tuple-element.30), channel_id=1, source_target_pairs={{0,8},{8,16},{16,24},{24,0},{1,9},{9,17},{17,25},{25,1},{2,10},{10... | collective-permute-start | bytes 122888 | tf_op jit(solution)/shard_map/ppermute | solution.py:687
  16.4 4.4 %collective-permute-start.3 = (f32[80,128]{1,0:T(8,128)S(1)}, f32[80,128]{1,0:T(8,128)S(1)}, u32[]{:S(2)}, u32[]{:S(2)}) collective-permute-start(f32[80,128]{1,0:T(8,128)S(1)} %get-tuple-element.31), channel_id=1, source_target_pairs={{8,0},{16,8},{24,16},{0,24},{9,1},{17,9},{25,17},{1,25},{10,2},{18... | collective-permute-start | bytes 122888 | tf_op jit(solution)/shard_map/ppermute | solution.py:687
  22.1 8.2 %all-to-all-start.1 = ((f32[8,8,128]{2,1,0:T(8,128)}), f32[8,8,128]{2,1,0:T(8,128)S(1)}, u32[]{:S(2)}, u32[]{:S(2)}) async-start(f32[8,8,128]{2,1,0:T(8,128)} %get-tuple-element.36), calls=%async_computation.1 | async-start | bytes 65536 | tf_op jit(solution)/shard_map/all_to_all | solution.py:723
  25.4 5.7 %collective-permute-start.4 = (f32[6,8,1,128]{3,2,1,0:T(1,128)S(1)}, f32[6,8,1,128]{3,2,1,0:T(1,128)S(1)}, u32[]{:S(2)}, u32[]{:S(2)}) collective-permute-start(f32[6,8,1,128]{3,2,1,0:T(1,128)S(1)} %get-tuple-element.40), channel_id=1, source_target_pairs={{0,8},{8,16},{16,24},{24,0},{1,9},{9,17},{17,25},{25,1},{2,10},{10... | collective-permute-start | bytes 73736 | tf_op jit(solution)/shard_map/ppermute | solution.py:687
  26.6 4.5 %collective-permute-start.5 = (f32[6,8,1,128]{3,2,1,0:T(1,128)S(1)}, f32[6,8,1,128]{3,2,1,0:T(1,128)S(1)}, u32[]{:S(2)}, u32[]{:S(2)}) collective-permute-start(f32[6,8,1,128]{3,2,1,0:T(1,128)S(1)} %get-tuple-element.41), channel_id=1, source_target_pairs={{8,0},{16,8},{24,16},{0,24},{9,1},{17,9},{25,17},{1,25},{10,2},{18... | collective-permute-start | bytes 73736 | tf_op jit(solution)/shard_map/ppermute | solution.py:687

commit v6 on v5

--- a/solution.py
+++ b/solution.py
@@ -407,11 +407,21 @@
     return conduct(conduction, [value[0:1], value[1:2]])
 
 
+def along_y(value, i):
+    cy = VELOCITY[i][1]
+    return pltpu.roll(value, cy % value.shape[1], 1) if cy else value
+
+
+def shift(value, i):
+    cz = VELOCITY[i][2]
+    return along_y(pltpu.roll(value, cz % value.shape[0], 0) if cz else value, i)
+
+
 def source_kernel(
     postf_ref,
     posth_ref,
+    recvb_ref,
     recva_ref,
-    recvb_ref,
     list_ref,
     chunks_ref,
     conduction_ref,
@@ -445,7 +455,7 @@
     for ref, comps, row in ((up_ref, UP, deep - 1), (down_ref, DOWN, 0)):
         for j in range(wide + 2):
             for n, i in enumerate(comps):
-                value = get(i, j - 1 - VELOCITY[i][0])
+                value = along_y(get(i, j - 1 - VELOCITY[i][0]), i)
                 at = j * EDGES + n
                 ref[at : at + 1, :] = value[row : row + 1, :]
         at = (wide + 2) * EDGES
@@ -453,35 +463,48 @@
         ref[at + 2 : at + 2 + LIST_ROWS, :] = list_ref[0:LIST_ROWS]
 
 
-def stream(get, edge, deep, i, x):
-    cx, cy, cz = VELOCITY[i]
-    value = get(i, x - cx)
-    if cz != 0:
-        rows = lax.broadcasted_iota(jnp.int32, value.shape, 0)
-        if cz == 1:
-            value = jnp.where(rows == 0, edge(i, x), pltpu.roll(value, 1, 0))
-        else:
-            value = jnp.where(rows == deep - 1, edge(i, x), pltpu.roll(value, deep - 1, 0))
-    if cy != 0:
-        value = pltpu.roll(value, cy % value.shape[1], 1)
-    return value
-
-
-def edge_rows(low_ref, high_ref, first):
-    def edge(i, x):
-        ref, comps = (low_ref, UP) if VELOCITY[i][2] == 1 else (high_ref, DOWN)
-        at = (x - first) * EDGES + comps.index(i)
-        return ref[at : at + 1, :]
-
-    return edge
-
-
-def step_kernel(
+def early_kernel(
     postf_ref,
     posth_ref,
+    recvb_ref,
     recva_ref,
+    source_ref,
+    list_ref,
+    flow_ref,
+    heat_ref,
+    wall_ref,
+):
+    wide, deep, lanes = postf_ref.shape[1:]
+    low, high = sides(lax.axis_index("blk") % 2 == 1, recva_ref, recvb_ref)
+    get = planes(postf_ref, posth_ref, low, high, wide, source_ref)
+    sublane = lax.broadcasted_iota(jnp.int32, (deep, lanes), 0)
+    tempers = []
+    for x in range(-1, wide + 1):
+        temper = None
+        for k in range(HEATS):
+            i = FLOWS + k
+            cx, cy, cz = VELOCITY[i]
+            value = shift(get(i, x - cx), i)
+            if cz != 0:
+                value = jnp.where(sublane == (0 if cz == 1 else deep - 1), 0.0, value)
+            heat_ref[k, x + 1] = value
+            temper = value if temper is None else temper + value
+        if 0 <= x < wide:
+            tempers.append(temper)
+    node = lists_of(list_ref[...])[2]
+    wall_ref[4:8] = jnp.zeros((4, lanes), F32)
+    wall_ref[0:4] = wall_temper(tempers, node)
+    for x in range(-1, wide + 1):
+        for i in range(FLOWS):
+            flow_ref[i, x + 1] = shift(get(i, x - VELOCITY[i][0]), i)
+
+
+def step_kernel(
+    flow_ref,
+    heat_ref,
+    wall_ref,
     recvb_ref,
-    source_ref,
+    recva_ref,
     low_edge_ref,
     high_edge_ref,
     list_ref,
@@ -496,22 +519,19 @@
     out_ref,
     sem,
 ):
-    wide, deep, lanes = posth_ref.shape[1:]
+    wide, deep, lanes = solid_ref.shape
     blocks = out_ref.shape[0]
     low, high = sides(lax.axis_index("blk") % 2 == 1, recva_ref, recvb_ref)
-    get = planes(None, posth_ref, low, high, wide, source_ref)
-    edge = edge_rows(low_edge_ref, high_edge_ref, -1)
-    tempers = []
-    for x in range(-1, wide + 1):
-        temper = None
-        for k in range(HEATS):
-            value = stream(get, edge, deep, FLOWS + k, x)
-            outh_ref[k, x + 1] = value
-            temper = value if temper is None else temper + value
-        if 0 <= x < wide:
-            tempers.append(temper)
     owner, cell, node = lists_of(list_ref[...])
-    wall = one_row(wall_temper(tempers, node))
+    column = node >> 7
+    place, z = lax.div(column, deep), lax.rem(column, deep)
+    rows = [
+        ref[(x + 2) * EDGES - 1 : (x + 2) * EDGES, :]
+        for ref in (low_edge_ref, high_edge_ref)
+        for x in range(wide)
+    ]
+    row_index = jnp.where(z == 0, place, jnp.where(z == deep - 1, wide + place, -1))
+    wall = one_row(wall_ref[0:4] + pick_twice(rows, [row_index], [node & 127])[0])
     owner, cell = one_row(owner), one_row(cell)
     row_mask = rows_of(owner * 2 + (cell >> 7), 2 * blocks)
     sums = add_up(wall, row_mask, hot(rows_of(cell & 127, lanes)))
@@ -524,9 +544,20 @@
         out_ref[d, 6:8, :] = sums[2 * d : 2 * d + 2]
     copy = pltpu.make_async_copy(out_ref, chunks_hbm, sem)
     copy.start()
-    get = planes(postf_ref, None, low, high, wide, None)
+    sublane = lax.broadcasted_iota(jnp.int32, (deep, lanes), 0)
+
+    def whole(value, i, x):
+        cz = VELOCITY[i][2]
+        if cz == 0:
+            return value
+        ref, comps, row = (
+            (low_edge_ref, UP, 0) if cz == 1 else (high_edge_ref, DOWN, deep - 1)
+        )
+        at = (x + 1) * EDGES + comps.index(i)
+        return jnp.where(sublane == row, ref[at : at + 1, :], value)
+
     for x in range(-1, wide + 1):
-        flow = [stream(get, edge, deep, i, x) for i in range(FLOWS)]
+        flow = [whole(flow_ref[i, x + 1], i, x) for i in range(FLOWS)]
         if x < 0:
             solid, counts = low(SOLID) != 0, low(COUNTS)
         elif x >= wide:
@@ -534,7 +565,7 @@
         else:
             solid, counts = solid_ref[x] != 0, counts_ref[x]
         post, speed = collide_flow(flow, solid)
-        heat = [outh_ref[k, x + 1] for k in range(HEATS)]
+        heat = [whole(heat_ref[k, x + 1], FLOWS + k, x) for k in range(HEATS)]
         temper = heat[0]
         for k in range(1, HEATS):
             temper = temper + heat[k]
@@ -549,20 +580,9 @@
             for n, i in enumerate(comps):
                 at = x + 1 - VELOCITY[i][0]
                 value = outf_ref[i, at] if i < FLOWS else outh_ref[i - FLOWS, at]
-                cy = VELOCITY[i][1]
-                value = pltpu.roll(value, cy % lanes, 1) if cy else value
-                ref[n, x] = value[row : row + 1, :]
+                ref[n, x] = along_y(value, i)[row : row + 1, :]
 
     copy.wait()
-
-
-def shift(value, i):
-    cx, cy, cz = VELOCITY[i]
-    if cz != 0:
-        value = pltpu.roll(value, cz % value.shape[0], 0)
-    if cy != 0:
-        value = pltpu.roll(value, cy % value.shape[1], 1)
-    return value
 
 
 def stream_kernel(postf_ref, flow_hbm, flow_ref, sems):
@@ -584,8 +604,8 @@
 
 def heat_kernel(
     posth_ref,
+    recvb_ref,
     recva_ref,
-    recvb_ref,
     list_ref,
     chunks_ref,
     low_edge_ref,
@@ -761,13 +781,29 @@
         (),
         postf,
         posth,
+        recvb,
         recva,
-        recvb,
         lists,
         chunks,
         conduction,
     )
     low_edge, high_edge = shift_both(up, down, "span")
+    flow, heat, wall = call(
+        early_kernel,
+        "stream_early",
+        (
+            shape(FLOWS, wide + 2, deep, lanes),
+            shape(HEATS, wide + 2, deep, lanes),
+            shape(8, lanes),
+        ),
+        (),
+        postf,
+        posth,
+        recvb,
+        recva,
+        source,
+        lists,
+    )
     edges = shape(EDGES, wide, 1, lanes)
     chunk = shape(blocks, 8, lanes)
     chunks, postf, posth, up, down = call(
@@ -781,11 +817,11 @@
             edges,
         ),
         (),
-        postf,
-        posth,
+        flow,
+        heat,
+        wall,
+        recvb,
         recva,
-        recvb,
-        source,
         low_edge,
         high_edge,
         lists,
@@ -812,8 +848,8 @@
         (heats, shape(*metal_temp.shape), shape(2 * wide, lanes)),
         (),
         posth,
+        recvb,
         recva,
-        recvb,
         lists,
         chunks,
         low_edge,

time: 32.2 us -> 31.3 us (0.972)
  starting transfers between devices: 15.1 us -> 14.5 us
  waiting for transfers between devices: 2.59 us -> 2.26 us
    ppermute x2, starting transfers between devices: 4.07 us -> 3.4 us  [swap(): return lax.ppermute(value, axis, pairs)]
    ppermute x2, waiting for transfers between devices: 2.51 us -> 2.18 us  [shift_both(): lax.ppermute(up, axis, ahead)]
    pallas_call x6 -> x7, Pallas kernels: 5.71 us -> 5.81 us  [call(): pl.pallas_call(kernel, in_specs=[smem] * len(scalars) + in_vmem(near) + [...]
  transfers between devices with their start and end apart: 7 -> 7, of which waited for: 3 -> 3; matrix products, arithmetic and copies ran while one was open for 0% -> 0% of each run, Pallas kernels for 4% -> 6%
where the time goes in v6:
time: 31.3 us; the launch traced here: 31.1 us
  starting transfers between devices  14.5 us (46%)
  blocking collectives  7.2 us (23%)
  Pallas kernels  5.81 us (19%)
  waiting for transfers between devices  2.26 us (7%)
  between operations  1.34 us (4%)
    all_to_all x1, blocking collectives, to_all(): return lax.all_to_all(chunks, 'blk', 0, 0, tiled=True)  7.2 us
    pallas_call x7, Pallas kernels, call(): pl.pallas_call(kernel, in_specs=[smem] * len(scalars) + in_vmem(near) + [...  5.81 us
    ppermute x2, starting transfers between devices, shift_both(): lax.ppermute(down, axis, [(j, i) for i, j in ahead])  4.93 us
    ppermute x2, starting transfers between devices, swap(): return lax.ppermute(value, axis, pairs)  3.4 us
    all_to_all x1, starting transfers between devices, to_all(): return lax.all_to_all(chunks, 'blk', 0, 0, tiled=True)  3.35 us
    ppermute x2, starting transfers between devices, shift_both(): lax.ppermute(up, axis, ahead)  2.77 us
    ppermute x2, waiting for transfers between devices, shift_both(): lax.ppermute(up, axis, ahead)  2.18 us
  transfers between devices with their start and end apart: 7, of which 3 were waited for; matrix products, arithmetic and copies ran while one was open for 0% of the time, Pallas kernels for 6%

profile of v6, /device:TPU:0, one launch (start us, length us, event | category | flops | bytes accessed | tf_op | source)
XLA Modules:
  0.0 31.1 jit_solution(10859130535935157828)
XLA Ops:
  1.3 0.0 copy-start
  1.3 1.8 %collide_first.1 = (f32[8,8,128]{2,1,0:T(8,128)S(1)}, f32[16,128]{1,0:T(8,128)S(1)}, f32[8,8,128]{2,1,0:T(8,128)S(1)}, f32[8,8,128]{2,1,0:T(8,128)S(1)}, f32[19,...) custom-call(s32[1,1]{1,0:T(1,128)S(6)} %copy.14.count_ref, ...), custom_call_target="tpu_custom_call" | custom-call | tf_op jit(solution)/shard_map/collide_first/pallas_call | solution.py:731
  3.1 3.4 %collective-permute-start = (f32[30,8,128]{2,1,0:T(8,128)S(1)}, f32[30,8,128]{2,1,0:T(8,128)S(1)}, u32[]{:S(2)}, u32[]{:S(2)}) collective-permute-start(f32[30,8,128]{2,1,0:T(8,128)S(1)} %get-tuple-element.28), channel_id=1, source_target_pairs={{1,2},{2,1},{3,4},{4,3},{5,6},{6,5},{7,0},{0,7},{9,10},{10,9},{11,... | collective-permute-start | bytes 368648 | tf_op jit(solution)/shard_map/ppermute | solution.py:701
  6.5 0.0 collective-permute-start.1
  6.5 7.2 %all_to_all.10.chunks_ref = f32[8,8,128]{2,1,0:T(8,128)S(1)} all-to-all(f32[8,8,128]{2,1,0:T(8,128)S(1)} %get-tuple-element.31), channel_id=1, replica_groups=mesh['span'=4,'blk'=8] {'blk'}, dimensions={0} | all-to-all | bytes 65536 | tf_op jit(solution)/shard_map/all_to_all | solution.py:743
  13.7 0.0 collective-permute-done.recvb_ref
  13.7 0.0 collective-permute-done.1.recva_ref
  13.7 0.0 copy-done
  13.7 0.4 %source_first.1 = (f32[80,128]{1,0:T(8,128)S(1)}, f32[80,128]{1,0:T(8,128)S(1)}, f32[8,128]{1,0:T(8,128)S(1)}, f32[12,8,128]{2,1,0:T(8,128)S(1)}) custom-call(f32[19,8,8,128]{3,2,1,0:T(8,128)S(1)} %get-tuple-element.26.postf_ref, f32[7,8,8,128]{3,2,1,0:T(8,128)S(1)} %get-tuple-element.27.posth_ref, f32[30,8,128]{2,1,0:T(8,128)S(1)} %collective-permute-done.recvb_ref, ...), custom_call_target="tpu_custom_call" | custom-call | tf_op jit(solution)/shard_map/source_first/pallas_call | solution.py:731
  14.1 1.6 %collective-permute-start.2 = (f32[80,128]{1,0:T(8,128)S(1)}, f32[80,128]{1,0:T(8,128)S(1)}, u32[]{:S(2)}, u32[]{:S(2)}) collective-permute-start(f32[80,128]{1,0:T(8,128)S(1)} %get-tuple-element.36), channel_id=1, source_target_pairs={{0,8},{8,16},{16,24},{24,0},{1,9},{9,17},{17,25},{25,1},{2,10},{10... | collective-permute-start | bytes 122888 | tf_op jit(solution)/shard_map/ppermute | solution.py:707
  15.7 2.2 %collective-permute-start.3 = (f32[80,128]{1,0:T(8,128)S(1)}, f32[80,128]{1,0:T(8,128)S(1)}, u32[]{:S(2)}, u32[]{:S(2)}) collective-permute-start(f32[80,128]{1,0:T(8,128)S(1)} %get-tuple-element.37), channel_id=1, source_target_pairs={{8,0},{16,8},{24,16},{0,24},{9,1},{17,9},{25,17},{1,25},{10,2},{18... | collective-permute-start | bytes 122888 | tf_op jit(solution)/shard_map/ppermute | solution.py:707
  17.9 0.3 %stream_early.1 = (f32[19,10,8,128]{3,2,1,0:T(8,128)S(1)}, f32[7,10,8,128]{3,2,1,0:T(8,128)S(1)}, f32[8,128]{1,0:T(8,128)S(1)}) custom-call(f32[19,8,8,128]{3,2,1,0:T(8,128)S(1)} %get-tuple-element.26.postf_ref, f32[7,8,8,128]{3,2,1,0:T(8,128)S(1)} %get-tuple-element.27.posth_ref, f32[30,8,128]{2,1,0:T(8,128)S(1)} %collective-permute-done.recvb_ref, ...), custom_call_target="tpu_custom_call" | custom-call | tf_op jit(solution)/shard_map/stream_early/pallas_call | solution.py:731
  18.2 1.8 %collective-permute-done.2.low_edge_ref = f32[80,128]{1,0:T(8,128)S(1)} collective-permute-done((f32[80,128]{1,0:T(8,128)S(1)}, f32[80,128]{1,0:T(8,128)S(1)}, u32[]{:S(2)}, u32[]{:S(2)}) %collective-permute-start.2) | collective-permute-done | bytes 40992 | tf_op jit(solution)/shard_map/ppermute | solution.py:707
  20.1 0.1 collective-permute-done.3.high_edge_ref
  20.1 1.0 %collide_second.1 = (f32[8,8,128]{2,1,0:T(8,128)}, f32[19,10,8,128]{3,2,1,0:T(8,128)S(1)}, f32[7,10,8,128]{3,2,1,0:T(8,128)S(1)}, f32[6,8,1,128]{3,2,1,0:T(1,128)S(1)}, f32[6,8,1,128]{3,2,1,0:T(1,128)S(1)}) custom-call(f32[19,10,8,128]{3,2,1,0:T(8,128)S(1)} %get-tuple-element.33.flow_ref, f32[7,10,8,128]{3,2,1,0:T(8,128)S(1)} %get-tuple-element.34.heat_ref, ...), custom_call_target="tpu_custom_call" | custom-call | tf_op jit(solution)/shard_map/collide_second/pallas_call | solution.py:731
  21.2 3.4 %all-to-all-start.1 = ((f32[8,8,128]{2,1,0:T(8,128)}), f32[8,8,128]{2,1,0:T(8,128)S(1)}, u32[]{:S(2)}, u32[]{:S(2)}) async-start(f32[8,8,128]{2,1,0:T(8,128)} %get-tuple-element.42), calls=%async_computation.1 | async-start | bytes 65536 | tf_op jit(solution)/shard_map/all_to_all | solution.py:743
  24.5 1.2 %collective-permute-start.4 = (f32[6,8,1,128]{3,2,1,0:T(1,128)S(1)}, f32[6,8,1,128]{3,2,1,0:T(1,128)S(1)}, u32[]{:S(2)}, u32[]{:S(2)}) collective-permute-start(f32[6,8,1,128]{3,2,1,0:T(1,128)S(1)} %get-tuple-element.46), channel_id=1, source_target_pairs={{0,8},{8,16},{16,24},{24,0},{1,9},{9,17},{17,25},{25,1},{2,10},{10... | collective-permute-start | bytes 73736 | tf_op jit(solution)/shard_map/ppermute | solution.py:707
  25.7 2.7 %collective-permute-start.5 = (f32[6,8,1,128]{3,2,1,0:T(1,128)S(1)}, f32[6,8,1,128]{3,2,1,0:T(1,128)S(1)}, u32[]{:S(2)}, u32[]{:S(2)}) collective-permute-start(f32[6,8,1,128]{3,2,1,0:T(1,128)S(1)} %get-tuple-element.47), channel_id=1, source_target_pairs={{8,0},{16,8},{24,16},{0,24},{9,1},{17,9},{25,17},{1,25},{10,2},{18... | collective-permute-start | bytes 73736 | tf_op jit(solution)/shard_map/ppermute | solution.py:707
  28.4 0.9 %stream_flow.1.flow_in = f32[19,8,8,128]{3,2,1,0:T(8,128)} custom-call(f32[19,10,8,128]{3,2,1,0:T(8,128)S(1)} %get-tuple-element.48.postf_ref), custom_call_target="tpu_custom_call" | custom-call | tf_op jit(solution)/shard_map/stream_flow/pallas_call | solution.py:731
  29.3 0.0 all-to-all-done.1.chunks_ref
  29.4 0.5 %stream_heat.1 = (f32[7,8,8,128]{3,2,1,0:T(8,128)S(1)}, f32[1,256]{1,0:T(1,128)S(1)}, f32[16,128]{1,0:T(8,128)S(1)}) custom-call(f32[7,10,8,128]{3,2,1,0:T(8,128)S(1)} %get-tuple-element.41.posth_ref, f32[30,8,128]{2,1,0:T(8,128)S(1)} %collective-permute-done.recvb_ref, f32[30,8,128]{2,1,0:T(8,128)S(1)} %collective-permute-done.1.recva_ref, ...), custom_call_target="tpu_custom_call" | custom-call | tf_op jit(solution)/shard_map/stream_heat/pallas_call | solution.py:731
  29.8 0.4 %collective-permute-done.4.low_ref = f32[6,8,1,128]{3,2,1,0:T(1,128)S(1)} collective-permute-done((f32[6,8,1,128]{3,2,1,0:T(1,128)S(1)}, f32[6,8,1,128]{3,2,1,0:T(1,128)S(1)}, u32[]{:S(2)}, u32[]{:S(2)}) %collective-permute-start.4) | collective-permute-done | bytes 24608 | tf_op jit(solution)/shard_map/ppermute | solution.py:707
  30.2 0.0 collective-permute-done.5.high_ref
  30.2 0.9 %write_last.1 = (f32[19,8,8,128]{3,2,1,0:T(8,128)}, f32[7,8,8,128]{3,2,1,0:T(8,128)}, f32[1,256]{1,0:T(1,128)}) custom-call(f32[7,8,8,128]{3,2,1,0:T(8,128)S(1)} %get-tuple-element.43.heat_ref, f32[1,256]{1,0:T(1,128)S(1)} %get-tuple-element.44.metal_ref, f32[16,128]{1,0:T(8,128)S(1)} %get-tuple-element.45.row_ref, ...), custom_call_target="tpu_custom_call", output_to_operand_aliasing={{0}: (5, {})} | custom-call | tf_op jit(solution)/shard_map/write_last/pallas_call | solution.py:731
Async XLA Ops:
  1.3 12.4 %copy-start = (f32[256,256]{1,0:T(8,128)S(1)}, f32[256,256]{1,0:T(8,128)}, u32[]{:S(2)}) copy-start(f32[256,256]{1,0:T(8,128)} %conduction_ref.3) | copy-start | bytes 786436
  3.1 10.6 %collective-permute-start = (f32[30,8,128]{2,1,0:T(8,128)S(1)}, f32[30,8,128]{2,1,0:T(8,128)S(1)}, u32[]{:S(2)}, u32[]{:S(2)}) collective-permute-start(f32[30,8,128]{2,1,0:T(8,128)S(1)} %get-tuple-element.28), channel_id=1, source_target_pairs={{1,2},{2,1},{3,4},{4,3},{5,6},{6,5},{7,0},{0,7},{9,10},{10,9},{11,... | collective-permute-start | bytes 368648 | tf_op jit(solution)/shard_map/ppermute | solution.py:701
  6.5 7.2 %collective-permute-start.1 = (f32[30,8,128]{2,1,0:T(8,128)S(1)}, f32[30,8,128]{2,1,0:T(8,128)S(1)}, u32[]{:S(2)}, u32[]{:S(2)}) collective-permute-start(f32[30,8,128]{2,1,0:T(8,128)S(1)} %get-tuple-element.29), channel_id=1, source_target_pairs={{0,1},{1,0},{2,3},{3,2},{4,5},{5,4},{6,7},{7,6},{8,9},{9,8},{10,11... | collective-permute-start | bytes 368648 | tf_op jit(solution)/shard_map/ppermute | solution.py:701
  14.1 6.0 %collective-permute-start.2 = (f32[80,128]{1,0:T(8,128)S(1)}, f32[80,128]{1,0:T(8,128)S(1)}, u32[]{:S(2)}, u32[]{:S(2)}) collective-permute-start(f32[80,128]{1,0:T(8,128)S(1)} %get-tuple-element.36), channel_id=1, source_target_pairs={{0,8},{8,16},{16,24},{24,0},{1,9},{9,17},{17,25},{25,1},{2,10},{10... | collective-permute-start | bytes 122888 | tf_op jit(solution)/shard_map/ppermute | solution.py:707
  15.7 4.4 %collective-permute-start.3 = (f32[80,128]{1,0:T(8,128)S(1)}, f32[80,128]{1,0:T(8,128)S(1)}, u32[]{:S(2)}, u32[]{:S(2)}) collective-permute-start(f32[80,128]{1,0:T(8,128)S(1)} %get-tuple-element.37), channel_id=1, source_target_pairs={{8,0},{16,8},{24,16},{0,24},{9,1},{17,9},{25,17},{1,25},{10,2},{18... | collective-permute-start | bytes 122888 | tf_op jit(solution)/shard_map/ppermute | solution.py:707
  21.2 8.2 %all-to-all-start.1 = ((f32[8,8,128]{2,1,0:T(8,128)}), f32[8,8,128]{2,1,0:T(8,128)S(1)}, u32[]{:S(2)}, u32[]{:S(2)}) async-start(f32[8,8,128]{2,1,0:T(8,128)} %get-tuple-element.42), calls=%async_computation.1 | async-start | bytes 65536 | tf_op jit(solution)/shard_map/all_to_all | solution.py:743
  24.5 5.7 %collective-permute-start.4 = (f32[6,8,1,128]{3,2,1,0:T(1,128)S(1)}, f32[6,8,1,128]{3,2,1,0:T(1,128)S(1)}, u32[]{:S(2)}, u32[]{:S(2)}) collective-permute-start(f32[6,8,1,128]{3,2,1,0:T(1,128)S(1)} %get-tuple-element.46), channel_id=1, source_target_pairs={{0,8},{8,16},{16,24},{24,0},{1,9},{9,17},{17,25},{25,1},{2,10},{10... | collective-permute-start | bytes 73736 | tf_op jit(solution)/shard_map/ppermute | solution.py:707
  25.7 4.5 %collective-permute-start.5 = (f32[6,8,1,128]{3,2,1,0:T(1,128)S(1)}, f32[6,8,1,128]{3,2,1,0:T(1,128)S(1)}, u32[]{:S(2)}, u32[]{:S(2)}) collective-permute-start(f32[6,8,1,128]{3,2,1,0:T(1,128)S(1)} %get-tuple-element.47), channel_id=1, source_target_pairs={{8,0},{16,8},{24,16},{0,24},{9,1},{17,9},{25,17},{1,25},{10,2},{18... | collective-permute-start | bytes 73736 | tf_op jit(solution)/shard_map/ppermute | solution.py:707

commit v7 on v6

--- a/solution.py
+++ b/solution.py
@@ -69,12 +69,6 @@
 
 def split(value):
     high = value.astype(BF16)
-    low = (value - high.astype(F32)).astype(BF16)
-    return high, low
-
-
-def split_three(value):
-    high = value.astype(BF16)
     rest = value - high.astype(F32)
     middle = rest.astype(BF16)
     low = (rest - middle.astype(F32)).astype(BF16)
@@ -114,7 +108,7 @@
         [jnp.where(row_mask, part.astype(F32), 0.0) for part in split(values)], axis=0
     ).astype(BF16)
     sums = dot(stacked, lane_hot, ((1,), (1,)))
-    return sums[:count] + sums[count:]
+    return sums[:count] + sums[count : 2 * count] + sums[2 * count :]
 
 
 def one_row(block):
@@ -124,6 +118,10 @@
 def put_rows(ref, start, row):
     for r in range(row.shape[1] // LANES):
         ref[start + r : start + r + 1, :] = row[:, r * LANES : (r + 1) * LANES]
+
+
+def rows_from(ref, start, count):
+    return jnp.concatenate([ref[start + r] for r in range(count)], axis=0)
 
 
 def lists_of(block):
@@ -391,13 +389,13 @@
 
 def conduct(conduction, halves):
     vector = jnp.concatenate(halves, axis=1)
-    parts = split_three(vector)
+    parts = split(vector)
     rows = lax.broadcasted_iota(jnp.int32, (16, vector.shape[1]), 0)
     stacked = jnp.zeros((16, vector.shape[1]), F32)
     for r, part in enumerate(parts):
         stacked = jnp.where(rows == r, part.astype(F32), stacked)
     stacked = stacked.astype(BF16)
-    out = sum([dot(stacked, part, ((1,), (1,))) for part in split_three(conduction)])
+    out = sum([dot(stacked, part, ((1,), (1,))) for part in split(conduction)])
     return out[0:1] + out[1:2] + out[2:3]
 
 
@@ -450,17 +448,17 @@
     source_ref[wide + 2 :] = give_planes(found[1], after[2], 0, 2, deep)
     get = planes(postf_ref, posth_ref, low, high, wide, source_ref)
 
-    for ref in (up_ref, down_ref):
-        ref[ref.shape[0] - 8 :, :] = jnp.zeros((8, lanes), F32)
     for ref, comps, row in ((up_ref, UP, deep - 1), (down_ref, DOWN, 0)):
         for j in range(wide + 2):
             for n, i in enumerate(comps):
                 value = along_y(get(i, j - 1 - VELOCITY[i][0]), i)
                 at = j * EDGES + n
-                ref[at : at + 1, :] = value[row : row + 1, :]
+                ref[at] = value[row : row + 1, :]
         at = (wide + 2) * EDGES
-        put_rows(ref, at, metal)
-        ref[at + 2 : at + 2 + LIST_ROWS, :] = list_ref[0:LIST_ROWS]
+        for r in range(2):
+            ref[at + r] = metal[:, r * lanes : (r + 1) * lanes]
+        for r in range(LIST_ROWS):
+            ref[at + 2 + r] = list_ref[r : r + 1, :]
 
 
 def early_kernel(
@@ -526,7 +524,7 @@
     column = node >> 7
     place, z = lax.div(column, deep), lax.rem(column, deep)
     rows = [
-        ref[(x + 2) * EDGES - 1 : (x + 2) * EDGES, :]
+        ref[(x + 2) * EDGES - 1]
         for ref in (low_edge_ref, high_edge_ref)
         for x in range(wide)
     ]
@@ -536,7 +534,7 @@
     row_mask = rows_of(owner * 2 + (cell >> 7), 2 * blocks)
     sums = add_up(wall, row_mask, hot(rows_of(cell & 127, lanes)))
     at = (wide + 2) * EDGES
-    below, above = low_edge_ref[at : at + 2, :], high_edge_ref[at : at + 2, :]
+    below, above = rows_from(low_edge_ref, at, 2), rows_from(high_edge_ref, at, 2)
     for d in range(blocks):
         out_ref[d, 0:2, :] = metal_ref[0:2]
         out_ref[d, 2:4, :] = below
@@ -554,7 +552,7 @@
             (low_edge_ref, UP, 0) if cz == 1 else (high_edge_ref, DOWN, deep - 1)
         )
         at = (x + 1) * EDGES + comps.index(i)
-        return jnp.where(sublane == row, ref[at : at + 1, :], value)
+        return jnp.where(sublane == row, ref[at], value)
 
     for x in range(-1, wide + 1):
         flow = [whole(flow_ref[i, x + 1], i, x) for i in range(FLOWS)]
@@ -638,11 +636,16 @@
 
     at = (wide + 2) * EDGES + 2
     for n, (ref, moved, z) in enumerate(((low_edge_ref, 2, deep - 1), (high_edge_ref, 4, 0))):
-        lists = lists_of(ref[at : at + LIST_ROWS, :])
+        lists = lists_of(rows_from(ref, at, LIST_ROWS))
         column = lists[2] >> 7
         row = jnp.where(lax.rem(column, deep) == z, lax.div(column, deep), -1)
         found = metal_at(metal_rows(chunks_ref, moved), lists)[0]
         row_ref[n * wide : (n + 1) * wide] = give(found, row, lists[2], wide)
+
+
+def runs(comps):
+    starts = [n for n, i in enumerate(comps) if n == 0 or comps[n - 1] != i - 1]
+    return [(n, comps[n], end - n) for n, end in zip(starts, starts[1:] + [len(comps)])]
 
 
 def edge_kernel(
@@ -669,11 +672,11 @@
         pltpu.make_async_copy(metal_ref, metal_hbm, sems.at[1]),
     ]
     for m, (ref, comps, z) in enumerate(((low_ref, UP, 0), (high_ref, DOWN, deep - 1))):
-        for n, i in enumerate(comps[:-1]):
+        for n, i, count in runs(comps[:-1]):
             copies.append(
                 pltpu.make_async_copy(
-                    ref.at[n],
-                    flow_hbm.at[i, :, z : z + 1, :],
+                    ref.at[pl.ds(n, count)],
+                    flow_hbm.at[pl.ds(i, count), :, z : z + 1, :],
                     sems.at[3 + m * EDGES + n],
                 )
             )
@@ -772,8 +775,7 @@
     chunks = to_all(chunks)
     recva = swap(senda, "blk", 0)
     recvb = swap(sendb, "blk", 1)
-    edge_count = -(-((wide + 2) * EDGES + 2 + LIST_ROWS) // 8) * 8
-    edges = shape(edge_count, lanes)
+    edges = shape((wide + 2) * EDGES + 2 + LIST_ROWS, 1, lanes)
     up, down, metal, source = call(
         source_kernel,
         "source_first",

time: 31.3 us -> 31.3 us (level)
  no operation moved by 1% of the time
where the time goes in v7:
time: 31.3 us; the launch traced here: 31.1 us
  starting transfers between devices  14.5 us (46%)
  blocking collectives  7.2 us (23%)
  Pallas kernels  5.87 us (19%)
  waiting for transfers between devices  2.19 us (7%)
  between operations  1.34 us (4%)
    all_to_all x1, blocking collectives, to_all(): return lax.all_to_all(chunks, 'blk', 0, 0, tiled=True)  7.2 us
    pallas_call x7, Pallas kernels, call(): pl.pallas_call(kernel, in_specs=[smem] * len(scalars) + in_vmem(near) + [...  5.87 us
    ppermute x2, starting transfers between devices, shift_both(): lax.ppermute(down, axis, [(j, i) for i, j in ahead])  4.9 us
    ppermute x2, starting transfers between devices, swap(): return lax.ppermute(value, axis, pairs)  3.4 us
    all_to_all x1, starting transfers between devices, to_all(): return lax.all_to_all(chunks, 'blk', 0, 0, tiled=True)  3.35 us
    ppermute x2, starting transfers between devices, shift_both(): lax.ppermute(up, axis, ahead)  2.8 us
    ppermute x2, waiting for transfers between devices, shift_both(): lax.ppermute(up, axis, ahead)  2.12 us
  transfers between devices with their start and end apart: 7, of which 3 were waited for; matrix products, arithmetic and copies ran while one was open for 0% of the time, Pallas kernels for 6%

profile of v7, /device:TPU:0, one launch (start us, length us, event | category | flops | bytes accessed | tf_op | source)
XLA Modules:
  0.0 31.1 jit_solution(16332864263020255851)
XLA Ops:
  1.3 0.0 copy-start
  1.3 1.8 %collide_first.1 = (f32[8,8,128]{2,1,0:T(8,128)S(1)}, f32[16,128]{1,0:T(8,128)S(1)}, f32[8,8,128]{2,1,0:T(8,128)S(1)}, f32[8,8,128]{2,1,0:T(8,128)S(1)}, f32[19,...) custom-call(s32[1,1]{1,0:T(1,128)S(6)} %copy.14.count_ref, ...), custom_call_target="tpu_custom_call" | custom-call | tf_op jit(solution)/shard_map/collide_first/pallas_call | solution.py:734
  3.1 3.4 %collective-permute-start = (f32[30,8,128]{2,1,0:T(8,128)S(1)}, f32[30,8,128]{2,1,0:T(8,128)S(1)}, u32[]{:S(2)}, u32[]{:S(2)}) collective-permute-start(f32[30,8,128]{2,1,0:T(8,128)S(1)} %get-tuple-element.28), channel_id=1, source_target_pairs={{1,2},{2,1},{3,4},{4,3},{5,6},{6,5},{7,0},{0,7},{9,10},{10,9},{11,... | collective-permute-start | bytes 368648 | tf_op jit(solution)/shard_map/ppermute | solution.py:704
  6.5 0.0 collective-permute-start.1
  6.5 7.2 %all_to_all.10.chunks_ref = f32[8,8,128]{2,1,0:T(8,128)S(1)} all-to-all(f32[8,8,128]{2,1,0:T(8,128)S(1)} %get-tuple-element.31), channel_id=1, replica_groups=mesh['span'=4,'blk'=8] {'blk'}, dimensions={0} | all-to-all | bytes 65536 | tf_op jit(solution)/shard_map/all_to_all | solution.py:746
  13.7 0.0 collective-permute-done.recvb_ref
  13.7 0.0 collective-permute-done.1.recva_ref
  13.7 0.0 copy-done
  13.7 0.4 %source_first.1 = (f32[74,1,128]{2,1,0:T(1,128)S(1)}, f32[74,1,128]{2,1,0:T(1,128)S(1)}, f32[8,128]{1,0:T(8,128)S(1)}, f32[12,8,128]{2,1,0:T(8,128)S(1)}) custom-call(f32[19,8,8,128]{3,2,1,0:T(8,128)S(1)} %get-tuple-element.26.postf_ref, f32[7,8,8,128]{3,2,1,0:T(8,128)S(1)} %get-tuple-element.27.posth_ref, f32[30,8,128]{2,1,0:T(8,128)S(1)} %collective-permute-done.recvb_ref, ...), custom_call_target="tpu_custom_call" | custom-call | tf_op jit(solution)/shard_map/source_first/pallas_call | solution.py:734
  14.1 1.6 %collective-permute-start.2 = (f32[74,1,128]{2,1,0:T(1,128)S(1)}, f32[74,1,128]{2,1,0:T(1,128)S(1)}, u32[]{:S(2)}, u32[]{:S(2)}) collective-permute-start(f32[74,1,128]{2,1,0:T(1,128)S(1)} %get-tuple-element.36), channel_id=1, source_target_pairs={{0,8},{8,16},{16,24},{24,0},{1,9},{9,17},{17,25},{25,1},{2,10},{10... | collective-permute-start | bytes 113672 | tf_op jit(solution)/shard_map/ppermute | solution.py:710
  15.7 2.2 %collective-permute-start.3 = (f32[74,1,128]{2,1,0:T(1,128)S(1)}, f32[74,1,128]{2,1,0:T(1,128)S(1)}, u32[]{:S(2)}, u32[]{:S(2)}) collective-permute-start(f32[74,1,128]{2,1,0:T(1,128)S(1)} %get-tuple-element.37), channel_id=1, source_target_pairs={{8,0},{16,8},{24,16},{0,24},{9,1},{17,9},{25,17},{1,25},{10,2},{18... | collective-permute-start | bytes 113672 | tf_op jit(solution)/shard_map/ppermute | solution.py:710
  18.0 0.3 %stream_early.1 = (f32[19,10,8,128]{3,2,1,0:T(8,128)S(1)}, f32[7,10,8,128]{3,2,1,0:T(8,128)S(1)}, f32[8,128]{1,0:T(8,128)S(1)}) custom-call(f32[19,8,8,128]{3,2,1,0:T(8,128)S(1)} %get-tuple-element.26.postf_ref, f32[7,8,8,128]{3,2,1,0:T(8,128)S(1)} %get-tuple-element.27.posth_ref, f32[30,8,128]{2,1,0:T(8,128)S(1)} %collective-permute-done.recvb_ref, ...), custom_call_target="tpu_custom_call" | custom-call | tf_op jit(solution)/shard_map/stream_early/pallas_call | solution.py:734
  18.3 1.7 %collective-permute-done.2.low_edge_ref = f32[74,1,128]{2,1,0:T(1,128)S(1)} collective-permute-done((f32[74,1,128]{2,1,0:T(1,128)S(1)}, f32[74,1,128]{2,1,0:T(1,128)S(1)}, u32[]{:S(2)}, u32[]{:S(2)}) %collective-permute-start.2) | collective-permute-done | bytes 37920 | tf_op jit(solution)/shard_map/ppermute | solution.py:710
  20.0 0.1 collective-permute-done.3.high_edge_ref
  20.1 1.0 %collide_second.1 = (f32[8,8,128]{2,1,0:T(8,128)}, f32[19,10,8,128]{3,2,1,0:T(8,128)S(1)}, f32[7,10,8,128]{3,2,1,0:T(8,128)S(1)}, f32[6,8,1,128]{3,2,1,0:T(1,128)S(1)}, f32[6,8,1,128]{3,2,1,0:T(1,128)S(1)}) custom-call(f32[19,10,8,128]{3,2,1,0:T(8,128)S(1)} %get-tuple-element.33.flow_ref, f32[7,10,8,128]{3,2,1,0:T(8,128)S(1)} %get-tuple-element.34.heat_ref, ...), custom_call_target="tpu_custom_call" | custom-call | tf_op jit(solution)/shard_map/collide_second/pallas_call | solution.py:734
  21.1 3.4 %all-to-all-start.1 = ((f32[8,8,128]{2,1,0:T(8,128)}), f32[8,8,128]{2,1,0:T(8,128)S(1)}, u32[]{:S(2)}, u32[]{:S(2)}) async-start(f32[8,8,128]{2,1,0:T(8,128)} %get-tuple-element.42), calls=%async_computation.1 | async-start | bytes 65536 | tf_op jit(solution)/shard_map/all_to_all | solution.py:746
  24.5 1.2 %collective-permute-start.4 = (f32[6,8,1,128]{3,2,1,0:T(1,128)S(1)}, f32[6,8,1,128]{3,2,1,0:T(1,128)S(1)}, u32[]{:S(2)}, u32[]{:S(2)}) collective-permute-start(f32[6,8,1,128]{3,2,1,0:T(1,128)S(1)} %get-tuple-element.46), channel_id=1, source_target_pairs={{0,8},{8,16},{16,24},{24,0},{1,9},{9,17},{17,25},{25,1},{2,10},{10... | collective-permute-start | bytes 73736 | tf_op jit(solution)/shard_map/ppermute | solution.py:710
  25.7 2.7 %collective-permute-start.5 = (f32[6,8,1,128]{3,2,1,0:T(1,128)S(1)}, f32[6,8,1,128]{3,2,1,0:T(1,128)S(1)}, u32[]{:S(2)}, u32[]{:S(2)}) collective-permute-start(f32[6,8,1,128]{3,2,1,0:T(1,128)S(1)} %get-tuple-element.47), channel_id=1, source_target_pairs={{8,0},{16,8},{24,16},{0,24},{9,1},{17,9},{25,17},{1,25},{10,2},{18... | collective-permute-start | bytes 73736 | tf_op jit(solution)/shard_map/ppermute | solution.py:710
  28.4 0.9 %stream_flow.1.flow_in = f32[19,8,8,128]{3,2,1,0:T(8,128)} custom-call(f32[19,10,8,128]{3,2,1,0:T(8,128)S(1)} %get-tuple-element.48.postf_ref), custom_call_target="tpu_custom_call" | custom-call | tf_op jit(solution)/shard_map/stream_flow/pallas_call | solution.py:734
  29.3 0.0 all-to-all-done.1.chunks_ref
  29.3 0.5 %stream_heat.1 = (f32[7,8,8,128]{3,2,1,0:T(8,128)S(1)}, f32[1,256]{1,0:T(1,128)S(1)}, f32[16,128]{1,0:T(8,128)S(1)}) custom-call(f32[7,10,8,128]{3,2,1,0:T(8,128)S(1)} %get-tuple-element.41.posth_ref, f32[30,8,128]{2,1,0:T(8,128)S(1)} %collective-permute-done.recvb_ref, f32[30,8,128]{2,1,0:T(8,128)S(1)} %collective-permute-done.1.recva_ref, ...), custom_call_target="tpu_custom_call" | custom-call | tf_op jit(solution)/shard_map/stream_heat/pallas_call | solution.py:734
  29.8 0.4 %collective-permute-done.4.low_ref = f32[6,8,1,128]{3,2,1,0:T(1,128)S(1)} collective-permute-done((f32[6,8,1,128]{3,2,1,0:T(1,128)S(1)}, f32[6,8,1,128]{3,2,1,0:T(1,128)S(1)}, u32[]{:S(2)}, u32[]{:S(2)}) %collective-permute-start.4) | collective-permute-done | bytes 24608 | tf_op jit(solution)/shard_map/ppermute | solution.py:710
  30.2 0.0 collective-permute-done.5.high_ref
  30.2 0.8 %write_last.1 = (f32[19,8,8,128]{3,2,1,0:T(8,128)}, f32[7,8,8,128]{3,2,1,0:T(8,128)}, f32[1,256]{1,0:T(1,128)}) custom-call(f32[7,8,8,128]{3,2,1,0:T(8,128)S(1)} %get-tuple-element.43.heat_ref, f32[1,256]{1,0:T(1,128)S(1)} %get-tuple-element.44.metal_ref, f32[16,128]{1,0:T(8,128)S(1)} %get-tuple-element.45.row_ref, ...), custom_call_target="tpu_custom_call", output_to_operand_aliasing={{0}: (5, {})} | custom-call | tf_op jit(solution)/shard_map/write_last/pallas_call | solution.py:734
Async XLA Ops:
  1.3 12.4 %copy-start = (f32[256,256]{1,0:T(8,128)S(1)}, f32[256,256]{1,0:T(8,128)}, u32[]{:S(2)}) copy-start(f32[256,256]{1,0:T(8,128)} %conduction_ref.3) | copy-start | bytes 786436
  3.1 10.6 %collective-permute-start = (f32[30,8,128]{2,1,0:T(8,128)S(1)}, f32[30,8,128]{2,1,0:T(8,128)S(1)}, u32[]{:S(2)}, u32[]{:S(2)}) collective-permute-start(f32[30,8,128]{2,1,0:T(8,128)S(1)} %get-tuple-element.28), channel_id=1, source_target_pairs={{1,2},{2,1},{3,4},{4,3},{5,6},{6,5},{7,0},{0,7},{9,10},{10,9},{11,... | collective-permute-start | bytes 368648 | tf_op jit(solution)/shard_map/ppermute | solution.py:704
  6.5 7.2 %collective-permute-start.1 = (f32[30,8,128]{2,1,0:T(8,128)S(1)}, f32[30,8,128]{2,1,0:T(8,128)S(1)}, u32[]{:S(2)}, u32[]{:S(2)}) collective-permute-start(f32[30,8,128]{2,1,0:T(8,128)S(1)} %get-tuple-element.29), channel_id=1, source_target_pairs={{0,1},{1,0},{2,3},{3,2},{4,5},{5,4},{6,7},{7,6},{8,9},{9,8},{10,11... | collective-permute-start | bytes 368648 | tf_op jit(solution)/shard_map/ppermute | solution.py:704
  14.1 5.9 %collective-permute-start.2 = (f32[74,1,128]{2,1,0:T(1,128)S(1)}, f32[74,1,128]{2,1,0:T(1,128)S(1)}, u32[]{:S(2)}, u32[]{:S(2)}) collective-permute-start(f32[74,1,128]{2,1,0:T(1,128)S(1)} %get-tuple-element.36), channel_id=1, source_target_pairs={{0,8},{8,16},{16,24},{24,0},{1,9},{9,17},{17,25},{25,1},{2,10},{10... | collective-permute-start | bytes 113672 | tf_op jit(solution)/shard_map/ppermute | solution.py:710
  15.7 4.4 %collective-permute-start.3 = (f32[74,1,128]{2,1,0:T(1,128)S(1)}, f32[74,1,128]{2,1,0:T(1,128)S(1)}, u32[]{:S(2)}, u32[]{:S(2)}) collective-permute-start(f32[74,1,128]{2,1,0:T(1,128)S(1)} %get-tuple-element.37), channel_id=1, source_target_pairs={{8,0},{16,8},{24,16},{0,24},{9,1},{17,9},{25,17},{1,25},{10,2},{18... | collective-permute-start | bytes 113672 | tf_op jit(solution)/shard_map/ppermute | solution.py:710
  21.1 8.2 %all-to-all-start.1 = ((f32[8,8,128]{2,1,0:T(8,128)}), f32[8,8,128]{2,1,0:T(8,128)S(1)}, u32[]{:S(2)}, u32[]{:S(2)}) async-start(f32[8,8,128]{2,1,0:T(8,128)} %get-tuple-element.42), calls=%async_computation.1 | async-start | bytes 65536 | tf_op jit(solution)/shard_map/all_to_all | solution.py:746
  24.5 5.7 %collective-permute-start.4 = (f32[6,8,1,128]{3,2,1,0:T(1,128)S(1)}, f32[6,8,1,128]{3,2,1,0:T(1,128)S(1)}, u32[]{:S(2)}, u32[]{:S(2)}) collective-permute-start(f32[6,8,1,128]{3,2,1,0:T(1,128)S(1)} %get-tuple-element.46), channel_id=1, source_target_pairs={{0,8},{8,16},{16,24},{24,0},{1,9},{9,17},{17,25},{25,1},{2,10},{10... | collective-permute-start | bytes 73736 | tf_op jit(solution)/shard_map/ppermute | solution.py:710
  25.7 4.5 %collective-permute-start.5 = (f32[6,8,1,128]{3,2,1,0:T(1,128)S(1)}, f32[6,8,1,128]{3,2,1,0:T(1,128)S(1)}, u32[]{:S(2)}, u32[]{:S(2)}) collective-permute-start(f32[6,8,1,128]{3,2,1,0:T(1,128)S(1)} %get-tuple-element.47), channel_id=1, source_target_pairs={{8,0},{16,8},{24,16},{0,24},{9,1},{17,9},{25,17},{1,25},{10,2},{18... | collective-permute-start | bytes 73736 | tf_op jit(solution)/shard_map/ppermute | solution.py:710

commit v8 on v7

--- a/solution.py
+++ b/solution.py
@@ -134,16 +134,10 @@
 
 
 def pack(
-    count_ref, heat_ref, metal_ref, node_ref, owner_ref, cell_ref, out_ref, list_ref, counts_ref
+    arrive, count_ref, heat_ref, metal_ref, node_ref, owner_ref, cell_ref, out_ref, list_ref, counts_ref
 ):
     blocks = out_ref.shape[0]
     wide, deep, lanes = heat_ref.shape[1:]
-    tempers = []
-    for x in range(wide):
-        temper = heat_ref[0, x]
-        for k in range(1, HEATS):
-            temper = temper + heat_ref[k, x]
-        tempers.append(temper)
     node = node_ref[...]
     cell = cell_ref[...]
     entries = node.shape[1]
@@ -155,21 +149,28 @@
     put_rows(list_ref, 8, node.astype(F32))
     put_rows(list_ref, LIST_ROWS, metal_ref[...])
     lane_mask = rows_of(node & 127, lanes)
+    cell_hot = hot(rows_of(cell & 127, lanes))
+    row_mask = rows_of(owner * 2 + (cell >> 7), 2 * blocks)
+    counts = dot(hot(row_mask), cell_hot, ((1,), (1,)))
+    at_nodes = dot(
+        hot(rows_of(jnp.where(live, node >> 7, -1), wide * deep)), hot(lane_mask), ((1,), (1,))
+    )
+    counts_ref[...] = at_nodes.reshape(wide, deep, lanes)
+    arrive()
+    tempers = []
+    for x in range(wide):
+        temper = heat_ref[0, x]
+        for k in range(1, HEATS):
+            temper = temper + heat_ref[k, x]
+        tempers.append(temper)
     nodes = list_ref[8:12].astype(jnp.int32)
     wall = one_row(wall_temper(tempers, nodes))
-    cell_hot = hot(rows_of(cell & 127, lanes))
-    row_mask = rows_of(owner * 2 + (cell >> 7), 2 * blocks)
     sums = add_up(wall, row_mask, cell_hot)
-    counts = dot(hot(row_mask), cell_hot, ((1,), (1,)))
     for d in range(blocks):
         put_rows(out_ref.at[d], 0, metal_ref[...])
         out_ref[d, 2:4, :] = sums[2 * d : 2 * d + 2]
         out_ref[d, 4:6, :] = counts[2 * d : 2 * d + 2]
         out_ref[d, 6:8, :] = jnp.zeros((2, lanes), F32)
-    at_nodes = dot(
-        hot(rows_of(jnp.where(live, node >> 7, -1), wide * deep)), hot(lane_mask), ((1,), (1,))
-    )
-    counts_ref[...] = at_nodes.reshape(wide, deep, lanes)
 
 
 def tree(values):
@@ -277,12 +278,21 @@
             )
         )
     ]
-    large = pltpu.make_async_copy(flow_hbm, flow_ref, sems.at[len(small)])
-    for copy in small + [large]:
+    strip = wide // 2
+    strips = [
+        pltpu.make_async_copy(
+            flow_hbm.at[:, pl.ds(n * strip, strip)],
+            flow_ref.at[:, pl.ds(n * strip, strip)],
+            sems.at[len(small) + n],
+        )
+        for n in range(2)
+    ]
+    for copy in small[1:5] + [small[0], small[5]] + strips:
         copy.start()
-    for copy in small:
+    for copy in small[1:5]:
         copy.wait()
     pack(
+        small[0].wait,
         count_ref,
         heat_ref,
         metal_ref,
@@ -293,9 +303,11 @@
         list_ref,
         counts_ref,
     )
+    small[5].wait()
     solid_ref[...] = mask_ref[...].astype(F32)
-    large.wait()
     for x in range(wide):
+        if x % strip == 0:
+            strips[x // strip].wait()
         flow = [flow_ref[i, x] for i in range(FLOWS)]
         heat = [heat_ref[k, x] for k in range(HEATS)]
         solid = mask_ref[x] != 0
@@ -769,7 +781,7 @@
             pltpu.VMEM(wall_node.shape, jnp.int32),
             pltpu.VMEM(wall_node.shape, jnp.int32),
             pltpu.VMEM(wall_node.shape, jnp.int32),
-            pltpu.SemaphoreType.DMA((7,)),
+            pltpu.SemaphoreType.DMA((8,)),
         ],
     )
     chunks = to_all(chunks)

time: 31.3 us -> 31.3 us (level)
  no operation moved by 1% of the time
where the time goes in v8:
time: 31.3 us; the launch traced here: 31 us
  starting transfers between devices  14.5 us (46%)
  blocking collectives  7.2 us (23%)
  Pallas kernels  5.85 us (19%)
  waiting for transfers between devices  2.19 us (7%)
  between operations  1.34 us (4%)
    all_to_all x1, blocking collectives, to_all(): return lax.all_to_all(chunks, 'blk', 0, 0, tiled=True)  7.2 us
    pallas_call x7, Pallas kernels, call(): pl.pallas_call(kernel, in_specs=[smem] * len(scalars) + in_vmem(near) + [...  5.85 us
    ppermute x2, starting transfers between devices, shift_both(): lax.ppermute(down, axis, [(j, i) for i, j in ahead])  4.9 us
    ppermute x2, starting transfers between devices, swap(): return lax.ppermute(value, axis, pairs)  3.4 us
    all_to_all x1, starting transfers between devices, to_all(): return lax.all_to_all(chunks, 'blk', 0, 0, tiled=True)  3.35 us
    ppermute x2, starting transfers between devices, shift_both(): lax.ppermute(up, axis, ahead)  2.8 us
    ppermute x2, waiting for transfers between devices, shift_both(): lax.ppermute(up, axis, ahead)  2.11 us
  transfers between devices with their start and end apart: 7, of which 3 were waited for; matrix products, arithmetic and copies ran while one was open for 0% of the time, Pallas kernels for 6%

profile of v8, /device:TPU:0, one launch (start us, length us, event | category | flops | bytes accessed | tf_op | source)
XLA Modules:
  0.0 31.0 jit_solution(8138052970313243959)
XLA Ops:
  1.3 0.0 copy-start
  1.3 1.8 %collide_first.1 = (f32[8,8,128]{2,1,0:T(8,128)S(1)}, f32[16,128]{1,0:T(8,128)S(1)}, f32[8,8,128]{2,1,0:T(8,128)S(1)}, f32[8,8,128]{2,1,0:T(8,128)S(1)}, f32[19,...) custom-call(s32[1,1]{1,0:T(1,128)S(6)} %copy.14.count_ref, ...), custom_call_target="tpu_custom_call" | custom-call | tf_op jit(solution)/shard_map/collide_first/pallas_call | solution.py:746
  3.1 3.4 %collective-permute-start = (f32[30,8,128]{2,1,0:T(8,128)S(1)}, f32[30,8,128]{2,1,0:T(8,128)S(1)}, u32[]{:S(2)}, u32[]{:S(2)}) collective-permute-start(f32[30,8,128]{2,1,0:T(8,128)S(1)} %get-tuple-element.28), channel_id=1, source_target_pairs={{1,2},{2,1},{3,4},{4,3},{5,6},{6,5},{7,0},{0,7},{9,10},{10,9},{11,... | collective-permute-start | bytes 368648 | tf_op jit(solution)/shard_map/ppermute | solution.py:716
  6.5 0.0 collective-permute-start.1
  6.5 7.2 %all_to_all.10.chunks_ref = f32[8,8,128]{2,1,0:T(8,128)S(1)} all-to-all(f32[8,8,128]{2,1,0:T(8,128)S(1)} %get-tuple-element.31), channel_id=1, replica_groups=mesh['span'=4,'blk'=8] {'blk'}, dimensions={0} | all-to-all | bytes 65536 | tf_op jit(solution)/shard_map/all_to_all | solution.py:758
  13.7 0.0 collective-permute-done.recvb_ref
  13.7 0.0 collective-permute-done.1.recva_ref
  13.7 0.0 copy-done
  13.7 0.4 %source_first.1 = (f32[74,1,128]{2,1,0:T(1,128)S(1)}, f32[74,1,128]{2,1,0:T(1,128)S(1)}, f32[8,128]{1,0:T(8,128)S(1)}, f32[12,8,128]{2,1,0:T(8,128)S(1)}) custom-call(f32[19,8,8,128]{3,2,1,0:T(8,128)S(1)} %get-tuple-element.26.postf_ref, f32[7,8,8,128]{3,2,1,0:T(8,128)S(1)} %get-tuple-element.27.posth_ref, f32[30,8,128]{2,1,0:T(8,128)S(1)} %collective-permute-done.recvb_ref, ...), custom_call_target="tpu_custom_call" | custom-call | tf_op jit(solution)/shard_map/source_first/pallas_call | solution.py:746
  14.1 1.6 %collective-permute-start.2 = (f32[74,1,128]{2,1,0:T(1,128)S(1)}, f32[74,1,128]{2,1,0:T(1,128)S(1)}, u32[]{:S(2)}, u32[]{:S(2)}) collective-permute-start(f32[74,1,128]{2,1,0:T(1,128)S(1)} %get-tuple-element.36), channel_id=1, source_target_pairs={{0,8},{8,16},{16,24},{24,0},{1,9},{9,17},{17,25},{25,1},{2,10},{10... | collective-permute-start | bytes 113672 | tf_op jit(solution)/shard_map/ppermute | solution.py:722
  15.7 2.2 %collective-permute-start.3 = (f32[74,1,128]{2,1,0:T(1,128)S(1)}, f32[74,1,128]{2,1,0:T(1,128)S(1)}, u32[]{:S(2)}, u32[]{:S(2)}) collective-permute-start(f32[74,1,128]{2,1,0:T(1,128)S(1)} %get-tuple-element.37), channel_id=1, source_target_pairs={{8,0},{16,8},{24,16},{0,24},{9,1},{17,9},{25,17},{1,25},{10,2},{18... | collective-permute-start | bytes 113672 | tf_op jit(solution)/shard_map/ppermute | solution.py:722
  17.9 0.3 %stream_early.1 = (f32[19,10,8,128]{3,2,1,0:T(8,128)S(1)}, f32[7,10,8,128]{3,2,1,0:T(8,128)S(1)}, f32[8,128]{1,0:T(8,128)S(1)}) custom-call(f32[19,8,8,128]{3,2,1,0:T(8,128)S(1)} %get-tuple-element.26.postf_ref, f32[7,8,8,128]{3,2,1,0:T(8,128)S(1)} %get-tuple-element.27.posth_ref, f32[30,8,128]{2,1,0:T(8,128)S(1)} %collective-permute-done.recvb_ref, ...), custom_call_target="tpu_custom_call" | custom-call | tf_op jit(solution)/shard_map/stream_early/pallas_call | solution.py:746
  18.3 1.7 %collective-permute-done.2.low_edge_ref = f32[74,1,128]{2,1,0:T(1,128)S(1)} collective-permute-done((f32[74,1,128]{2,1,0:T(1,128)S(1)}, f32[74,1,128]{2,1,0:T(1,128)S(1)}, u32[]{:S(2)}, u32[]{:S(2)}) %collective-permute-start.2) | collective-permute-done | bytes 37920 | tf_op jit(solution)/shard_map/ppermute | solution.py:722
  20.0 0.1 collective-permute-done.3.high_edge_ref
  20.1 1.0 %collide_second.1 = (f32[8,8,128]{2,1,0:T(8,128)}, f32[19,10,8,128]{3,2,1,0:T(8,128)S(1)}, f32[7,10,8,128]{3,2,1,0:T(8,128)S(1)}, f32[6,8,1,128]{3,2,1,0:T(1,128)S(1)}, f32[6,8,1,128]{3,2,1,0:T(1,128)S(1)}) custom-call(f32[19,10,8,128]{3,2,1,0:T(8,128)S(1)} %get-tuple-element.33.flow_ref, f32[7,10,8,128]{3,2,1,0:T(8,128)S(1)} %get-tuple-element.34.heat_ref, ...), custom_call_target="tpu_custom_call" | custom-call | tf_op jit(solution)/shard_map/collide_second/pallas_call | solution.py:746
  21.1 3.4 %all-to-all-start.1 = ((f32[8,8,128]{2,1,0:T(8,128)}), f32[8,8,128]{2,1,0:T(8,128)S(1)}, u32[]{:S(2)}, u32[]{:S(2)}) async-start(f32[8,8,128]{2,1,0:T(8,128)} %get-tuple-element.42), calls=%async_computation.1 | async-start | bytes 65536 | tf_op jit(solution)/shard_map/all_to_all | solution.py:758
  24.5 1.2 %collective-permute-start.4 = (f32[6,8,1,128]{3,2,1,0:T(1,128)S(1)}, f32[6,8,1,128]{3,2,1,0:T(1,128)S(1)}, u32[]{:S(2)}, u32[]{:S(2)}) collective-permute-start(f32[6,8,1,128]{3,2,1,0:T(1,128)S(1)} %get-tuple-element.46), channel_id=1, source_target_pairs={{0,8},{8,16},{16,24},{24,0},{1,9},{9,17},{17,25},{25,1},{2,10},{10... | collective-permute-start | bytes 73736 | tf_op jit(solution)/shard_map/ppermute | solution.py:722
  25.7 2.7 %collective-permute-start.5 = (f32[6,8,1,128]{3,2,1,0:T(1,128)S(1)}, f32[6,8,1,128]{3,2,1,0:T(1,128)S(1)}, u32[]{:S(2)}, u32[]{:S(2)}) collective-permute-start(f32[6,8,1,128]{3,2,1,0:T(1,128)S(1)} %get-tuple-element.47), channel_id=1, source_target_pairs={{8,0},{16,8},{24,16},{0,24},{9,1},{17,9},{25,17},{1,25},{10,2},{18... | collective-permute-start | bytes 73736 | tf_op jit(solution)/shard_map/ppermute | solution.py:722
  28.4 0.9 %stream_flow.1.flow_in = f32[19,8,8,128]{3,2,1,0:T(8,128)} custom-call(f32[19,10,8,128]{3,2,1,0:T(8,128)S(1)} %get-tuple-element.48.postf_ref), custom_call_target="tpu_custom_call" | custom-call | tf_op jit(solution)/shard_map/stream_flow/pallas_call | solution.py:746
  29.3 0.0 all-to-all-done.1.chunks_ref
  29.3 0.5 %stream_heat.1 = (f32[7,8,8,128]{3,2,1,0:T(8,128)S(1)}, f32[1,256]{1,0:T(1,128)S(1)}, f32[16,128]{1,0:T(8,128)S(1)}) custom-call(f32[7,10,8,128]{3,2,1,0:T(8,128)S(1)} %get-tuple-element.41.posth_ref, f32[30,8,128]{2,1,0:T(8,128)S(1)} %collective-permute-done.recvb_ref, f32[30,8,128]{2,1,0:T(8,128)S(1)} %collective-permute-done.1.recva_ref, ...), custom_call_target="tpu_custom_call" | custom-call | tf_op jit(solution)/shard_map/stream_heat/pallas_call | solution.py:746
  29.8 0.4 %collective-permute-done.4.low_ref = f32[6,8,1,128]{3,2,1,0:T(1,128)S(1)} collective-permute-done((f32[6,8,1,128]{3,2,1,0:T(1,128)S(1)}, f32[6,8,1,128]{3,2,1,0:T(1,128)S(1)}, u32[]{:S(2)}, u32[]{:S(2)}) %collective-permute-start.4) | collective-permute-done | bytes 24608 | tf_op jit(solution)/shard_map/ppermute | solution.py:722
  30.2 0.0 collective-permute-done.5.high_ref
  30.2 0.8 %write_last.1 = (f32[19,8,8,128]{3,2,1,0:T(8,128)}, f32[7,8,8,128]{3,2,1,0:T(8,128)}, f32[1,256]{1,0:T(1,128)}) custom-call(f32[7,8,8,128]{3,2,1,0:T(8,128)S(1)} %get-tuple-element.43.heat_ref, f32[1,256]{1,0:T(1,128)S(1)} %get-tuple-element.44.metal_ref, f32[16,128]{1,0:T(8,128)S(1)} %get-tuple-element.45.row_ref, ...), custom_call_target="tpu_custom_call", output_to_operand_aliasing={{0}: (5, {})} | custom-call | tf_op jit(solution)/shard_map/write_last/pallas_call | solution.py:746
Async XLA Ops:
  1.3 12.4 %copy-start = (f32[256,256]{1,0:T(8,128)S(1)}, f32[256,256]{1,0:T(8,128)}, u32[]{:S(2)}) copy-start(f32[256,256]{1,0:T(8,128)} %conduction_ref.3) | copy-start | bytes 786436
  3.1 10.6 %collective-permute-start = (f32[30,8,128]{2,1,0:T(8,128)S(1)}, f32[30,8,128]{2,1,0:T(8,128)S(1)}, u32[]{:S(2)}, u32[]{:S(2)}) collective-permute-start(f32[30,8,128]{2,1,0:T(8,128)S(1)} %get-tuple-element.28), channel_id=1, source_target_pairs={{1,2},{2,1},{3,4},{4,3},{5,6},{6,5},{7,0},{0,7},{9,10},{10,9},{11,... | collective-permute-start | bytes 368648 | tf_op jit(solution)/shard_map/ppermute | solution.py:716
  6.5 7.2 %collective-permute-start.1 = (f32[30,8,128]{2,1,0:T(8,128)S(1)}, f32[30,8,128]{2,1,0:T(8,128)S(1)}, u32[]{:S(2)}, u32[]{:S(2)}) collective-permute-start(f32[30,8,128]{2,1,0:T(8,128)S(1)} %get-tuple-element.29), channel_id=1, source_target_pairs={{0,1},{1,0},{2,3},{3,2},{4,5},{5,4},{6,7},{7,6},{8,9},{9,8},{10,11... | collective-permute-start | bytes 368648 | tf_op jit(solution)/shard_map/ppermute | solution.py:716
  14.1 5.9 %collective-permute-start.2 = (f32[74,1,128]{2,1,0:T(1,128)S(1)}, f32[74,1,128]{2,1,0:T(1,128)S(1)}, u32[]{:S(2)}, u32[]{:S(2)}) collective-permute-start(f32[74,1,128]{2,1,0:T(1,128)S(1)} %get-tuple-element.36), channel_id=1, source_target_pairs={{0,8},{8,16},{16,24},{24,0},{1,9},{9,17},{17,25},{25,1},{2,10},{10... | collective-permute-start | bytes 113672 | tf_op jit(solution)/shard_map/ppermute | solution.py:722
  15.7 4.4 %collective-permute-start.3 = (f32[74,1,128]{2,1,0:T(1,128)S(1)}, f32[74,1,128]{2,1,0:T(1,128)S(1)}, u32[]{:S(2)}, u32[]{:S(2)}) collective-permute-start(f32[74,1,128]{2,1,0:T(1,128)S(1)} %get-tuple-element.37), channel_id=1, source_target_pairs={{8,0},{16,8},{24,16},{0,24},{9,1},{17,9},{25,17},{1,25},{10,2},{18... | collective-permute-start | bytes 113672 | tf_op jit(solution)/shard_map/ppermute | solution.py:722
  21.1 8.2 %all-to-all-start.1 = ((f32[8,8,128]{2,1,0:T(8,128)}), f32[8,8,128]{2,1,0:T(8,128)S(1)}, u32[]{:S(2)}, u32[]{:S(2)}) async-start(f32[8,8,128]{2,1,0:T(8,128)} %get-tuple-element.42), calls=%async_computation.1 | async-start | bytes 65536 | tf_op jit(solution)/shard_map/all_to_all | solution.py:758
  24.5 5.7 %collective-permute-start.4 = (f32[6,8,1,128]{3,2,1,0:T(1,128)S(1)}, f32[6,8,1,128]{3,2,1,0:T(1,128)S(1)}, u32[]{:S(2)}, u32[]{:S(2)}) collective-permute-start(f32[6,8,1,128]{3,2,1,0:T(1,128)S(1)} %get-tuple-element.46), channel_id=1, source_target_pairs={{0,8},{8,16},{16,24},{24,0},{1,9},{9,17},{17,25},{25,1},{2,10},{10... | collective-permute-start | bytes 73736 | tf_op jit(solution)/shard_map/ppermute | solution.py:722
  25.7 4.5 %collective-permute-start.5 = (f32[6,8,1,128]{3,2,1,0:T(1,128)S(1)}, f32[6,8,1,128]{3,2,1,0:T(1,128)S(1)}, u32[]{:S(2)}, u32[]{:S(2)}) collective-permute-start(f32[6,8,1,128]{3,2,1,0:T(1,128)S(1)} %get-tuple-element.47), channel_id=1, source_target_pairs={{8,0},{16,8},{24,16},{0,24},{9,1},{17,9},{25,17},{1,25},{10,2},{18... | collective-permute-start | bytes 73736 | tf_op jit(solution)/shard_map/ppermute | solution.py:722

commit v9 on v7

--- a/solution.py
+++ b/solution.py
@@ -430,6 +430,14 @@
 ):
     wide, deep, lanes = postf_ref.shape[1:]
     blocks = chunks_ref.shape[0]
+    own = lists_of(list_ref[...])
+    found = metal_at(metal_rows(chunks_ref, 0), own)[0]
+    source_ref[2 : wide + 2] = give_planes(found, own[2], 0, wide, deep)
+    low, high = sides(lax.axis_index("blk") % 2 == 1, recva_ref, recvb_ref)
+    before, after = side_lists(low), side_lists(high)
+    found = metal_at(metal_rows(chunks_ref, 0), before, after)
+    source_ref[0:2] = give_planes(found[0], before[2], wide - 2, 2, deep)
+    source_ref[wide + 2 :] = give_planes(found[1], after[2], 0, 2, deep)
     sums = chunks_ref[0]
     for d in range(1, blocks):
         sums = sums + chunks_ref[d]
@@ -438,14 +446,6 @@
     metal_ref[...] = jnp.zeros(metal_ref.shape, F32)
     put_rows(metal_ref, 0, metal)
     metal_ref[2:4, :] = count
-    own = lists_of(list_ref[...])
-    found = metal_at(metal_rows(chunks_ref, 0), own)[0]
-    source_ref[2 : wide + 2] = give_planes(found, own[2], 0, wide, deep)
-    low, high = sides(lax.axis_index("blk") % 2 == 1, recva_ref, recvb_ref)
-    before, after = side_lists(low), side_lists(high)
-    found = metal_at(metal_rows(chunks_ref, 0), before, after)
-    source_ref[0:2] = give_planes(found[0], before[2], wide - 2, 2, deep)
-    source_ref[wide + 2 :] = give_planes(found[1], after[2], 0, 2, deep)
     get = planes(postf_ref, posth_ref, low, high, wide, source_ref)
 
     for ref, comps, row in ((up_ref, UP, deep - 1), (down_ref, DOWN, 0)):

time: 31.3 us -> 31.3 us (level)
  no operation moved by 1% of the time
where the time goes in v9:
time: 31.3 us; the launch traced here: 31.1 us
  starting transfers between devices  14.5 us (46%)
  blocking collectives  7.2 us (23%)
  Pallas kernels  5.86 us (19%)
  waiting for transfers between devices  2.19 us (7%)
  between operations  1.34 us (4%)
    all_to_all x1, blocking collectives, to_all(): return lax.all_to_all(chunks, 'blk', 0, 0, tiled=True)  7.2 us
    pallas_call x7, Pallas kernels, call(): pl.pallas_call(kernel, in_specs=[smem] * len(scalars) + in_vmem(near) + [...  5.86 us
    ppermute x2, starting transfers between devices, shift_both(): lax.ppermute(down, axis, [(j, i) for i, j in ahead])  4.9 us
    ppermute x2, starting transfers between devices, swap(): return lax.ppermute(value, axis, pairs)  3.4 us
    all_to_all x1, starting transfers between devices, to_all(): return lax.all_to_all(chunks, 'blk', 0, 0, tiled=True)  3.35 us
    ppermute x2, starting transfers between devices, shift_both(): lax.ppermute(up, axis, ahead)  2.82 us
    ppermute x2, waiting for transfers between devices, shift_both(): lax.ppermute(up, axis, ahead)  2.12 us
  transfers between devices with their start and end apart: 7, of which 3 were waited for; matrix products, arithmetic and copies ran while one was open for 0% of the time, Pallas kernels for 6%

profile of v9, /device:TPU:0, one launch (start us, length us, event | category | flops | bytes accessed | tf_op | source)
XLA Modules:
  0.0 31.1 jit_solution(5027450228656336768)
XLA Ops:
  1.3 0.0 copy-start
  1.3 1.8 %collide_first.1 = (f32[8,8,128]{2,1,0:T(8,128)S(1)}, f32[16,128]{1,0:T(8,128)S(1)}, f32[8,8,128]{2,1,0:T(8,128)S(1)}, f32[8,8,128]{2,1,0:T(8,128)S(1)}, f32[19,...) custom-call(s32[1,1]{1,0:T(1,128)S(6)} %copy.14.count_ref, ...), custom_call_target="tpu_custom_call" | custom-call | tf_op jit(solution)/shard_map/collide_first/pallas_call | solution.py:734
  3.1 3.4 %collective-permute-start = (f32[30,8,128]{2,1,0:T(8,128)S(1)}, f32[30,8,128]{2,1,0:T(8,128)S(1)}, u32[]{:S(2)}, u32[]{:S(2)}) collective-permute-start(f32[30,8,128]{2,1,0:T(8,128)S(1)} %get-tuple-element.28), channel_id=1, source_target_pairs={{1,2},{2,1},{3,4},{4,3},{5,6},{6,5},{7,0},{0,7},{9,10},{10,9},{11,... | collective-permute-start | bytes 368648 | tf_op jit(solution)/shard_map/ppermute | solution.py:704
  6.5 0.0 collective-permute-start.1
  6.5 7.2 %all_to_all.10.chunks_ref = f32[8,8,128]{2,1,0:T(8,128)S(1)} all-to-all(f32[8,8,128]{2,1,0:T(8,128)S(1)} %get-tuple-element.31), channel_id=1, replica_groups=mesh['span'=4,'blk'=8] {'blk'}, dimensions={0} | all-to-all | bytes 65536 | tf_op jit(solution)/shard_map/all_to_all | solution.py:746
  13.7 0.0 collective-permute-done.recvb_ref
  13.7 0.0 collective-permute-done.1.recva_ref
  13.7 0.0 copy-done
  13.7 0.4 %source_first.1 = (f32[74,1,128]{2,1,0:T(1,128)S(1)}, f32[74,1,128]{2,1,0:T(1,128)S(1)}, f32[8,128]{1,0:T(8,128)S(1)}, f32[12,8,128]{2,1,0:T(8,128)S(1)}) custom-call(f32[19,8,8,128]{3,2,1,0:T(8,128)S(1)} %get-tuple-element.26.postf_ref, f32[7,8,8,128]{3,2,1,0:T(8,128)S(1)} %get-tuple-element.27.posth_ref, f32[30,8,128]{2,1,0:T(8,128)S(1)} %collective-permute-done.recvb_ref, ...), custom_call_target="tpu_custom_call" | custom-call | tf_op jit(solution)/shard_map/source_first/pallas_call | solution.py:734
  14.1 1.6 %collective-permute-start.2 = (f32[74,1,128]{2,1,0:T(1,128)S(1)}, f32[74,1,128]{2,1,0:T(1,128)S(1)}, u32[]{:S(2)}, u32[]{:S(2)}) collective-permute-start(f32[74,1,128]{2,1,0:T(1,128)S(1)} %get-tuple-element.36), channel_id=1, source_target_pairs={{0,8},{8,16},{16,24},{24,0},{1,9},{9,17},{17,25},{25,1},{2,10},{10... | collective-permute-start | bytes 113672 | tf_op jit(solution)/shard_map/ppermute | solution.py:710
  15.7 2.2 %collective-permute-start.3 = (f32[74,1,128]{2,1,0:T(1,128)S(1)}, f32[74,1,128]{2,1,0:T(1,128)S(1)}, u32[]{:S(2)}, u32[]{:S(2)}) collective-permute-start(f32[74,1,128]{2,1,0:T(1,128)S(1)} %get-tuple-element.37), channel_id=1, source_target_pairs={{8,0},{16,8},{24,16},{0,24},{9,1},{17,9},{25,17},{1,25},{10,2},{18... | collective-permute-start | bytes 113672 | tf_op jit(solution)/shard_map/ppermute | solution.py:710
  18.0 0.3 %stream_early.1 = (f32[19,10,8,128]{3,2,1,0:T(8,128)S(1)}, f32[7,10,8,128]{3,2,1,0:T(8,128)S(1)}, f32[8,128]{1,0:T(8,128)S(1)}) custom-call(f32[19,8,8,128]{3,2,1,0:T(8,128)S(1)} %get-tuple-element.26.postf_ref, f32[7,8,8,128]{3,2,1,0:T(8,128)S(1)} %get-tuple-element.27.posth_ref, f32[30,8,128]{2,1,0:T(8,128)S(1)} %collective-permute-done.recvb_ref, ...), custom_call_target="tpu_custom_call" | custom-call | tf_op jit(solution)/shard_map/stream_early/pallas_call | solution.py:734
  18.3 1.7 %collective-permute-done.2.low_edge_ref = f32[74,1,128]{2,1,0:T(1,128)S(1)} collective-permute-done((f32[74,1,128]{2,1,0:T(1,128)S(1)}, f32[74,1,128]{2,1,0:T(1,128)S(1)}, u32[]{:S(2)}, u32[]{:S(2)}) %collective-permute-start.2) | collective-permute-done | bytes 37920 | tf_op jit(solution)/shard_map/ppermute | solution.py:710
  20.0 0.1 collective-permute-done.3.high_edge_ref
  20.1 1.0 %collide_second.1 = (f32[8,8,128]{2,1,0:T(8,128)}, f32[19,10,8,128]{3,2,1,0:T(8,128)S(1)}, f32[7,10,8,128]{3,2,1,0:T(8,128)S(1)}, f32[6,8,1,128]{3,2,1,0:T(1,128)S(1)}, f32[6,8,1,128]{3,2,1,0:T(1,128)S(1)}) custom-call(f32[19,10,8,128]{3,2,1,0:T(8,128)S(1)} %get-tuple-element.33.flow_ref, f32[7,10,8,128]{3,2,1,0:T(8,128)S(1)} %get-tuple-element.34.heat_ref, ...), custom_call_target="tpu_custom_call" | custom-call | tf_op jit(solution)/shard_map/collide_second/pallas_call | solution.py:734
  21.2 3.4 %all-to-all-start.1 = ((f32[8,8,128]{2,1,0:T(8,128)}), f32[8,8,128]{2,1,0:T(8,128)S(1)}, u32[]{:S(2)}, u32[]{:S(2)}) async-start(f32[8,8,128]{2,1,0:T(8,128)} %get-tuple-element.42), calls=%async_computation.1 | async-start | bytes 65536 | tf_op jit(solution)/shard_map/all_to_all | solution.py:746
  24.5 1.2 %collective-permute-start.4 = (f32[6,8,1,128]{3,2,1,0:T(1,128)S(1)}, f32[6,8,1,128]{3,2,1,0:T(1,128)S(1)}, u32[]{:S(2)}, u32[]{:S(2)}) collective-permute-start(f32[6,8,1,128]{3,2,1,0:T(1,128)S(1)} %get-tuple-element.46), channel_id=1, source_target_pairs={{0,8},{8,16},{16,24},{24,0},{1,9},{9,17},{17,25},{25,1},{2,10},{10... | collective-permute-start | bytes 73736 | tf_op jit(solution)/shard_map/ppermute | solution.py:710
  25.7 2.7 %collective-permute-start.5 = (f32[6,8,1,128]{3,2,1,0:T(1,128)S(1)}, f32[6,8,1,128]{3,2,1,0:T(1,128)S(1)}, u32[]{:S(2)}, u32[]{:S(2)}) collective-permute-start(f32[6,8,1,128]{3,2,1,0:T(1,128)S(1)} %get-tuple-element.47), channel_id=1, source_target_pairs={{8,0},{16,8},{24,16},{0,24},{9,1},{17,9},{25,17},{1,25},{10,2},{18... | collective-permute-start | bytes 73736 | tf_op jit(solution)/shard_map/ppermute | solution.py:710
  28.4 0.9 %stream_flow.1.flow_in = f32[19,8,8,128]{3,2,1,0:T(8,128)} custom-call(f32[19,10,8,128]{3,2,1,0:T(8,128)S(1)} %get-tuple-element.48.postf_ref), custom_call_target="tpu_custom_call" | custom-call | tf_op jit(solution)/shard_map/stream_flow/pallas_call | solution.py:734
  29.3 0.0 all-to-all-done.1.chunks_ref
  29.3 0.5 %stream_heat.1 = (f32[7,8,8,128]{3,2,1,0:T(8,128)S(1)}, f32[1,256]{1,0:T(1,128)S(1)}, f32[16,128]{1,0:T(8,128)S(1)}) custom-call(f32[7,10,8,128]{3,2,1,0:T(8,128)S(1)} %get-tuple-element.41.posth_ref, f32[30,8,128]{2,1,0:T(8,128)S(1)} %collective-permute-done.recvb_ref, f32[30,8,128]{2,1,0:T(8,128)S(1)} %collective-permute-done.1.recva_ref, ...), custom_call_target="tpu_custom_call" | custom-call | tf_op jit(solution)/shard_map/stream_heat/pallas_call | solution.py:734
  29.8 0.4 %collective-permute-done.4.low_ref = f32[6,8,1,128]{3,2,1,0:T(1,128)S(1)} collective-permute-done((f32[6,8,1,128]{3,2,1,0:T(1,128)S(1)}, f32[6,8,1,128]{3,2,1,0:T(1,128)S(1)}, u32[]{:S(2)}, u32[]{:S(2)}) %collective-permute-start.4) | collective-permute-done | bytes 24608 | tf_op jit(solution)/shard_map/ppermute | solution.py:710
  30.2 0.0 collective-permute-done.5.high_ref
  30.2 0.8 %write_last.1 = (f32[19,8,8,128]{3,2,1,0:T(8,128)}, f32[7,8,8,128]{3,2,1,0:T(8,128)}, f32[1,256]{1,0:T(1,128)}) custom-call(f32[7,8,8,128]{3,2,1,0:T(8,128)S(1)} %get-tuple-element.43.heat_ref, f32[1,256]{1,0:T(1,128)S(1)} %get-tuple-element.44.metal_ref, f32[16,128]{1,0:T(8,128)S(1)} %get-tuple-element.45.row_ref, ...), custom_call_target="tpu_custom_call", output_to_operand_aliasing={{0}: (5, {})} | custom-call | tf_op jit(solution)/shard_map/write_last/pallas_call | solution.py:734
Async XLA Ops:
  1.3 12.4 %copy-start = (f32[256,256]{1,0:T(8,128)S(1)}, f32[256,256]{1,0:T(8,128)}, u32[]{:S(2)}) copy-start(f32[256,256]{1,0:T(8,128)} %conduction_ref.3) | copy-start | bytes 786436
  3.1 10.6 %collective-permute-start = (f32[30,8,128]{2,1,0:T(8,128)S(1)}, f32[30,8,128]{2,1,0:T(8,128)S(1)}, u32[]{:S(2)}, u32[]{:S(2)}) collective-permute-start(f32[30,8,128]{2,1,0:T(8,128)S(1)} %get-tuple-element.28), channel_id=1, source_target_pairs={{1,2},{2,1},{3,4},{4,3},{5,6},{6,5},{7,0},{0,7},{9,10},{10,9},{11,... | collective-permute-start | bytes 368648 | tf_op jit(solution)/shard_map/ppermute | solution.py:704
  6.5 7.2 %collective-permute-start.1 = (f32[30,8,128]{2,1,0:T(8,128)S(1)}, f32[30,8,128]{2,1,0:T(8,128)S(1)}, u32[]{:S(2)}, u32[]{:S(2)}) collective-permute-start(f32[30,8,128]{2,1,0:T(8,128)S(1)} %get-tuple-element.29), channel_id=1, source_target_pairs={{0,1},{1,0},{2,3},{3,2},{4,5},{5,4},{6,7},{7,6},{8,9},{9,8},{10,11... | collective-permute-start | bytes 368648 | tf_op jit(solution)/shard_map/ppermute | solution.py:704
  14.1 5.9 %collective-permute-start.2 = (f32[74,1,128]{2,1,0:T(1,128)S(1)}, f32[74,1,128]{2,1,0:T(1,128)S(1)}, u32[]{:S(2)}, u32[]{:S(2)}) collective-permute-start(f32[74,1,128]{2,1,0:T(1,128)S(1)} %get-tuple-element.36), channel_id=1, source_target_pairs={{0,8},{8,16},{16,24},{24,0},{1,9},{9,17},{17,25},{25,1},{2,10},{10... | collective-permute-start | bytes 113672 | tf_op jit(solution)/shard_map/ppermute | solution.py:710
  15.7 4.4 %collective-permute-start.3 = (f32[74,1,128]{2,1,0:T(1,128)S(1)}, f32[74,1,128]{2,1,0:T(1,128)S(1)}, u32[]{:S(2)}, u32[]{:S(2)}) collective-permute-start(f32[74,1,128]{2,1,0:T(1,128)S(1)} %get-tuple-element.37), channel_id=1, source_target_pairs={{8,0},{16,8},{24,16},{0,24},{9,1},{17,9},{25,17},{1,25},{10,2},{18... | collective-permute-start | bytes 113672 | tf_op jit(solution)/shard_map/ppermute | solution.py:710
  21.2 8.2 %all-to-all-start.1 = ((f32[8,8,128]{2,1,0:T(8,128)}), f32[8,8,128]{2,1,0:T(8,128)S(1)}, u32[]{:S(2)}, u32[]{:S(2)}) async-start(f32[8,8,128]{2,1,0:T(8,128)} %get-tuple-element.42), calls=%async_computation.1 | async-start | bytes 65536 | tf_op jit(solution)/shard_map/all_to_all | solution.py:746
  24.5 5.7 %collective-permute-start.4 = (f32[6,8,1,128]{3,2,1,0:T(1,128)S(1)}, f32[6,8,1,128]{3,2,1,0:T(1,128)S(1)}, u32[]{:S(2)}, u32[]{:S(2)}) collective-permute-start(f32[6,8,1,128]{3,2,1,0:T(1,128)S(1)} %get-tuple-element.46), channel_id=1, source_target_pairs={{0,8},{8,16},{16,24},{24,0},{1,9},{9,17},{17,25},{25,1},{2,10},{10... | collective-permute-start | bytes 73736 | tf_op jit(solution)/shard_map/ppermute | solution.py:710
  25.7 4.5 %collective-permute-start.5 = (f32[6,8,1,128]{3,2,1,0:T(1,128)S(1)}, f32[6,8,1,128]{3,2,1,0:T(1,128)S(1)}, u32[]{:S(2)}, u32[]{:S(2)}) collective-permute-start(f32[6,8,1,128]{3,2,1,0:T(1,128)S(1)} %get-tuple-element.47), channel_id=1, source_target_pairs={{8,0},{16,8},{24,16},{0,24},{9,1},{17,9},{25,17},{1,25},{10,2},{18... | collective-permute-start | bytes 73736 | tf_op jit(solution)/shard_map/ppermute | solution.py:710
